TPU v7x, 32 devices: a whole 2x2x4 slice. The times are simulated.
32 devices in a mesh: dp: 16 (over z, x, core), tp: 2 (over y).
Axes of the slice: x: 2, y: 2, z: 4, core: 2. Of those that a mesh axis runs over, the one named last changes fastest.
Arguments:
- layer_input: bfloat16 [16, 1024, 512], P('dp', 'tp'), may hold values from -6 to 6
- memory: bfloat16 [16, 1024, 512], P('dp', 'tp'), may hold values from -6 to 6
- seg_lengths: int32 [16, 16], P('dp'), may hold values from 1 to 256, 1024 in all within a row
- expert_ids: int32 [16, 1], P('dp'), may hold values from 0 to 15
- ln_gains: float32 [3, 512], replicated, may hold values from 0.5 to 1.5
- w_qkv: bfloat16 [3, 512, 512], P(None, None, 'tp'), may hold values from -0.25 to 0.25
- w_out_self: bfloat16 [512, 512], P('tp'), may hold values from -0.75 to 0.75
- w_query_cross: bfloat16 [512, 512], P(None, 'tp'), may hold values from -0.25 to 0.25
- w_kv_cross: bfloat16 [2, 512, 512], P(None, None, 'tp'), may hold values from -0.25 to 0.25
- w_out_cross: bfloat16 [512, 512], P('tp'), may hold values from -6 to 6
- w_up: bfloat16 [16, 512, 2048], P(None, None, 'tp'), may hold values from -0.25 to 0.25
- w_down: bfloat16 [16, 2048, 512], P(None, 'tp'), may hold values from -0.125 to 0.125
- cotangent: bfloat16 [16, 1024, 512], P('dp', 'tp'), may hold values from -6 to 6
Outputs:
- layer_output: bfloat16 [16, 1024, 512], P('dp', 'tp')
- grad_input: float32 [16, 1024, 512], P('dp', 'tp')
- grad_memory: float32 [16, 1024, 512], P('dp', 'tp')
- grad_ln_gains: float32 [3, 512], P(None, 'dp')
- grad_w_qkv: float32 [3, 512, 512], P(None, 'dp', 'tp')
- grad_w_out_self: float32 [512, 512], P('tp', 'dp')
- grad_w_query_cross: float32 [512, 512], P('dp', 'tp')
- grad_w_kv_cross: float32 [2, 512, 512], P(None, 'dp', 'tp')
- grad_w_out_cross: float32 [512, 512], P('tp', 'dp')
- grad_w_up: float32 [16, 512, 2048], P(None, 'dp', 'tp')
- grad_w_down: float32 [16, 2048, 512], P(None, 'tp', 'dp')
Inputs may be any that keep to these rules, and one draw needn't show every extreme that they name: `seg_lengths`: each row's lengths sum to 1024; the longest segment of every row has 256 tokens. `expert_ids`: every expert serves some row.
All inputs are finite; a program needn't handle non-finite values.
Results may differ from a plain program's by a relative error of at most 0.024.
Values may be sent and summed in bfloat16 or wider, within the bound.
A program may use at most 256 MiB of HBM per device.

v0:
```python
from functools import partial

import jax
import jax.numpy as jnp
from jax import lax
from jax.sharding import PartitionSpec as P

HEAD_DIM = 64


epsilon = 1e-05


def layer_norm(values, gain):
    centered = values - jnp.mean(values, axis=-1, keepdims=True)
    spread = jnp.mean(centered * centered, axis=-1, keepdims=True)
    return centered * lax.rsqrt(spread + epsilon) * gain


def norm_backward(state, gain, grad_normed, grad_state):
    unused, pullback = jax.vjp(layer_norm, state, gain)
    grad_values, grad_gain = pullback(grad_normed)
    return (grad_state + grad_values, grad_gain)


def segment_mask(lengths, length, count):
    seg_ends = jnp.cumsum(lengths, dtype=jnp.int32)
    places = jnp.arange(length, dtype=jnp.int32)
    labels = jnp.sum((places[:, None] >= seg_ends[None, :]).astype(jnp.int32), axis=1)
    row_places = jnp.arange(count, dtype=jnp.int32)
    return (labels[:, None] == labels[None, :]) & (row_places[:, None] >= places[None, :])


def to_heads(block):
    return block.reshape(block.shape[:-1] + (block.shape[-1] // HEAD_DIM, HEAD_DIM))


def softmax_rows(queries, key_rows, allowed):
    scores = jnp.einsum(
        "qhd,khd->hqk", queries, key_rows, preferred_element_type=jnp.float32
    ) * HEAD_DIM ** (-0.5)
    if allowed is not None:
        scores = jnp.where(allowed[None], scores, -1e30)
    row_max = jnp.max(scores, axis=-1, keepdims=True)
    weights = jnp.exp(scores - row_max)
    return weights / jnp.sum(weights, axis=-1, keepdims=True)


def attend_both(queries, key_rows, value_rows, allowed, grad_heads):
    row_probs = softmax_rows(queries, key_rows, allowed)
    probs_low = row_probs.astype(jnp.bfloat16)
    heads_out = jnp.einsum(
        "hqk,khd->qhd", probs_low, value_rows, preferred_element_type=jnp.float32
    ).astype(jnp.bfloat16)
    grad_probs = jnp.einsum(
        "qhd,khd->hqk", grad_heads, value_rows, preferred_element_type=jnp.float32
    )
    inner_sum = jnp.sum(row_probs * grad_probs, axis=-1, keepdims=True)
    grad_scores = (row_probs * (grad_probs - inner_sum)).astype(jnp.bfloat16)
    grad_queries = jnp.einsum(
        "hqk,khd->qhd", grad_scores, key_rows, preferred_element_type=jnp.float32
    ) * HEAD_DIM ** (-0.5)
    grad_keys = jnp.einsum(
        "hqk,qhd->khd", grad_scores, queries, preferred_element_type=jnp.float32
    ) * HEAD_DIM ** (-0.5)
    grad_values = jnp.einsum(
        "hqk,qhd->khd", probs_low, grad_heads, preferred_element_type=jnp.float32
    )
    return (heads_out, grad_queries, grad_keys, grad_values)


def spread_tokens(normed):
    return lax.all_gather(normed, "tp", axis=1, tiled=True)


def sum_tokens(partial_out):
    return lax.psum_scatter(partial_out, "tp", scatter_dimension=1, tiled=True)


def gather_grads(grad_state):
    return lax.all_gather(grad_state.astype(jnp.bfloat16), "tp", axis=1, tiled=True)


def sum_grads(grad_normed):
    return lax.psum_scatter(grad_normed, "tp", scatter_dimension=1, tiled=True)


def self_partial(normed_all, seg_lengths, w_qkv, w_out_self):
    projected = jnp.einsum(
        "rld,cde->rcle", normed_all, w_qkv, preferred_element_type=jnp.float32
    ).astype(jnp.bfloat16)

    def one_row(items):
        row_proj, lengths = items
        split_heads = to_heads(row_proj)
        length = row_proj.shape[1]
        row_probs = softmax_rows(
            split_heads[0], split_heads[1], segment_mask(lengths, length, length)
        )
        heads_out = jnp.einsum(
            "hqk,khd->qhd",
            row_probs.astype(jnp.bfloat16),
            split_heads[2],
            preferred_element_type=jnp.float32,
        )
        return heads_out.reshape(row_proj.shape[1:]).astype(jnp.bfloat16)

    heads_all = lax.map(one_row, (projected, seg_lengths))
    return jnp.einsum("rle,ed->rld", heads_all, w_out_self, preferred_element_type=jnp.float32)


def self_backward(normed_all, seg_lengths, w_qkv, w_out_self, grad_branch):
    projected = jnp.einsum(
        "rld,cde->rcle", normed_all, w_qkv, preferred_element_type=jnp.float32
    ).astype(jnp.bfloat16)
    grad_heads = jnp.einsum(
        "rld,ed->rle", grad_branch, w_out_self, preferred_element_type=jnp.float32
    ).astype(jnp.bfloat16)

    def one_row(items):
        row_proj, lengths, row_grad = items
        split_heads = to_heads(row_proj)
        length = row_proj.shape[1]
        results = attend_both(
            split_heads[0],
            split_heads[1],
            split_heads[2],
            segment_mask(lengths, length, length),
            to_heads(row_grad),
        )
        return (
            results[0].reshape(length, -1),
            jnp.stack([piece.reshape(length, -1).astype(jnp.bfloat16) for piece in results[1:]]),
        )

    heads_all, grad_proj = lax.map(one_row, (projected, seg_lengths, grad_heads))
    grad_w_out = jnp.einsum(
        "rle,rld->ed", heads_all, grad_branch, preferred_element_type=jnp.float32
    )
    grad_w_qkv = jnp.einsum(
        "rld,rcle->cde", normed_all, grad_proj, preferred_element_type=jnp.float32
    )
    grad_normed = jnp.einsum("rcle,cde->rld", grad_proj, w_qkv, preferred_element_type=jnp.float32)
    return (grad_normed, grad_w_qkv, grad_w_out)


def cross_partial(normed_all, memory_all, w_query_cross, w_kv_cross, w_out_cross):
    queries = jnp.einsum(
        "rld,de->rle", normed_all, w_query_cross, preferred_element_type=jnp.float32
    ).astype(jnp.bfloat16)
    key_value = jnp.einsum(
        "rmd,cde->rcme", memory_all, w_kv_cross, preferred_element_type=jnp.float32
    ).astype(jnp.bfloat16)

    def one_row(items):
        row_query, row_kv = items
        split_kv = to_heads(row_kv)
        row_probs = softmax_rows(to_heads(row_query), split_kv[0], None)
        heads_out = jnp.einsum(
            "hqk,khd->qhd",
            row_probs.astype(jnp.bfloat16),
            split_kv[1],
            preferred_element_type=jnp.float32,
        )
        return heads_out.reshape(row_query.shape).astype(jnp.bfloat16)

    heads_all = lax.map(one_row, (queries, key_value))
    return jnp.einsum("rle,ed->rld", heads_all, w_out_cross, preferred_element_type=jnp.float32)


def cross_core(normed_all, memory_all, w_query_cross, w_kv_cross, w_out_cross, grad_branch):
    queries = jnp.einsum(
        "rld,de->rle", normed_all, w_query_cross, preferred_element_type=jnp.float32
    ).astype(jnp.bfloat16)
    key_value = jnp.einsum(
        "rmd,cde->rcme", memory_all, w_kv_cross, preferred_element_type=jnp.float32
    ).astype(jnp.bfloat16)
    grad_heads = jnp.einsum(
        "rld,ed->rle", grad_branch, w_out_cross, preferred_element_type=jnp.float32
    ).astype(jnp.bfloat16)

    def one_row(items):
        row_query, row_kv, row_grad = items
        split_kv = to_heads(row_kv)
        query_count = row_query.shape[0]
        memory_count = row_kv.shape[1]
        results = attend_both(
            to_heads(row_query), split_kv[0], split_kv[1], None, to_heads(row_grad)
        )
        grad_kv = jnp.stack(
            [results[2].reshape(memory_count, -1), results[3].reshape(memory_count, -1)]
        )
        return (results[0].reshape(query_count, -1), results[1].reshape(query_count, -1), grad_kv)

    heads_all, grad_queries, grad_kv = lax.map(one_row, (queries, key_value, grad_heads))
    grad_w_out = jnp.einsum(
        "rle,rld->ed", heads_all, grad_branch, preferred_element_type=jnp.float32
    )
    return (grad_queries, grad_kv, grad_w_out)


def cross_backward(normed_all, memory_all, w_query_cross, w_kv_cross, w_out_cross, grad_branch):
    grad_queries, grad_kv, grad_w_out = cross_core(
        normed_all, memory_all, w_query_cross, w_kv_cross, w_out_cross, grad_branch
    )
    grad_queries = grad_queries.astype(jnp.bfloat16)
    grad_kv = grad_kv.astype(jnp.bfloat16)
    grad_w_query = jnp.einsum(
        "rld,rle->de", normed_all, grad_queries, preferred_element_type=jnp.float32
    )
    grad_w_kv = jnp.einsum("rmd,rcme->cde", memory_all, grad_kv, preferred_element_type=jnp.float32)
    grad_normed = jnp.einsum(
        "rle,de->rld", grad_queries, w_query_cross, preferred_element_type=jnp.float32
    )
    grad_memory = jnp.einsum(
        "rcme,cde->rmd", grad_kv, w_kv_cross, preferred_element_type=jnp.float32
    )
    return (grad_normed, grad_memory, grad_w_query, grad_w_kv, grad_w_out)


def expert_rows(weights, expert):
    return lax.dynamic_index_in_dim(weights, expert, 0, keepdims=False)


def ffn_partial(normed_all, expert_ids, w_up, w_down):

    def one_row(items):
        normed_row, expert = items
        pre_act = jnp.dot(normed_row, expert_rows(w_up, expert), preferred_element_type=jnp.float32)
        hidden = jax.nn.gelu(pre_act, approximate=False).astype(jnp.bfloat16)
        return jnp.dot(hidden, expert_rows(w_down, expert), preferred_element_type=jnp.float32)

    return lax.map(one_row, (normed_all, expert_ids[:, 0]))


def ffn_backward(normed_all, expert_ids, w_up, w_down, grad_branch):

    def one_row(items):
        normed_row, expert, grad_row = items
        up_rows = expert_rows(w_up, expert)
        down_rows = expert_rows(w_down, expert)
        pre_act = jnp.dot(normed_row, up_rows, preferred_element_type=jnp.float32)
        activated, gelu_back = jax.vjp(partial(jax.nn.gelu, approximate=False), pre_act)
        hidden = activated.astype(jnp.bfloat16)
        grad_hidden = lax.dot_general(
            grad_row, down_rows, (((1,), (1,)), ((), ())), preferred_element_type=jnp.float32
        )
        grad_pre = gelu_back(grad_hidden)[0].astype(jnp.bfloat16)
        grad_down = lax.dot_general(
            hidden, grad_row, (((0,), (0,)), ((), ())), preferred_element_type=jnp.float32
        )
        grad_up = lax.dot_general(
            normed_row, grad_pre, (((0,), (0,)), ((), ())), preferred_element_type=jnp.float32
        )
        grad_normed = lax.dot_general(
            grad_pre, up_rows, (((1,), (1,)), ((), ())), preferred_element_type=jnp.float32
        )
        return (grad_normed, grad_up, grad_down)

    grad_normed, row_up, row_down = lax.map(one_row, (normed_all, expert_ids[:, 0], grad_branch))
    choose = (
        expert_ids[:, 0][:, None] == jnp.arange(w_up.shape[0], dtype=jnp.int32)[None, :]
    ).astype(jnp.float32)
    grad_w_up = jnp.einsum("re,rdf->edf", choose, row_up, precision=lax.Precision.HIGHEST)
    grad_w_down = jnp.einsum("re,rfd->efd", choose, row_down, precision=lax.Precision.HIGHEST)
    return (grad_normed, grad_w_up, grad_w_down)


def run_forward(layer_input, memory, seg_lengths, expert_ids, ln_gains, attn_weights, w_up, w_down):
    w_qkv, w_out_self, w_query_cross, w_kv_cross, w_out_cross = attn_weights
    state_zero = layer_input.astype(jnp.float32)
    normed_local = layer_norm(state_zero, ln_gains[0]).astype(jnp.bfloat16)
    memory_all = lax.all_gather(memory, "tp", axis=1, tiled=True)
    normed_self = spread_tokens(normed_local)
    state_one = state_zero + sum_tokens(self_partial(normed_self, seg_lengths, w_qkv, w_out_self))
    normed_cross = spread_tokens(layer_norm(state_one, ln_gains[1]).astype(jnp.bfloat16))
    state_two = state_one + sum_tokens(
        cross_partial(normed_cross, memory_all, w_query_cross, w_kv_cross, w_out_cross)
    )
    normed_ffn = spread_tokens(layer_norm(state_two, ln_gains[2]).astype(jnp.bfloat16))
    state_three = state_two + sum_tokens(ffn_partial(normed_ffn, expert_ids, w_up, w_down))
    return (
        state_three,
        (state_zero, state_one, state_two, normed_self, normed_cross, normed_ffn, memory_all),
    )


def per_device(
    layer_input,
    memory,
    seg_lengths,
    expert_ids,
    ln_gains,
    w_qkv,
    w_out_self,
    w_query_cross,
    w_kv_cross,
    w_out_cross,
    w_up,
    w_down,
    cotangent,
):
    attn_weights = (w_qkv, w_out_self, w_query_cross, w_kv_cross, w_out_cross)
    use_qkv, use_out_self, use_query, use_kv, use_out_cross = attn_weights
    state_three, kept = run_forward(
        layer_input, memory, seg_lengths, expert_ids, ln_gains, attn_weights, w_up, w_down
    )
    fresh = lax.optimization_barrier((layer_input, memory, state_three))
    unused, kept = run_forward(
        fresh[0], fresh[1], seg_lengths, expert_ids, ln_gains, attn_weights, w_up, w_down
    )
    state_zero, state_one, state_two, normed_self, normed_cross, normed_ffn, memory_all = kept
    grad_state = cotangent.astype(jnp.float32)
    grad_normed, grad_up, grad_down = ffn_backward(
        normed_ffn, expert_ids, w_up, w_down, gather_grads(grad_state)
    )
    grad_state, gain_ffn = norm_backward(state_two, ln_gains[2], sum_grads(grad_normed), grad_state)
    grad_normed, memory_part, grad_w_query, grad_w_kv, grad_w_out_cross = cross_backward(
        normed_cross, memory_all, use_query, use_kv, use_out_cross, gather_grads(grad_state)
    )
    grad_normed, grad_memory = (
        lax.psum_scatter(
            grad_normed.astype(jnp.bfloat16), "tp", scatter_dimension=1, tiled=True
        ).astype(jnp.float32),
        lax.psum_scatter(
            memory_part.astype(jnp.bfloat16), "tp", scatter_dimension=1, tiled=True
        ).astype(jnp.float32),
    )
    grad_state, gain_cross = norm_backward(state_one, ln_gains[1], grad_normed, grad_state)
    grad_normed, grad_w_qkv, grad_w_out_self = self_backward(
        normed_self, seg_lengths, use_qkv, use_out_self, gather_grads(grad_state)
    )
    grad_state, gain_self = norm_backward(
        state_zero, ln_gains[0], sum_grads(grad_normed), grad_state
    )
    summed = (
        lax.psum_scatter(
            grad_w_qkv.astype(jnp.bfloat16), "dp", scatter_dimension=1, tiled=True
        ).astype(jnp.float32),
        lax.psum_scatter(
            grad_w_out_self.astype(jnp.bfloat16), "dp", scatter_dimension=1, tiled=True
        ).astype(jnp.float32),
        lax.psum_scatter(
            grad_w_query.astype(jnp.bfloat16), "dp", scatter_dimension=0, tiled=True
        ).astype(jnp.float32),
        lax.psum_scatter(
            grad_w_kv.astype(jnp.bfloat16), "dp", scatter_dimension=1, tiled=True
        ).astype(jnp.float32),
        lax.psum_scatter(
            grad_w_out_cross.astype(jnp.bfloat16), "dp", scatter_dimension=1, tiled=True
        ).astype(jnp.float32),
        lax.psum_scatter(
            grad_up.astype(jnp.bfloat16), "dp", scatter_dimension=1, tiled=True
        ).astype(jnp.float32),
        lax.psum_scatter(
            grad_down.astype(jnp.bfloat16), "dp", scatter_dimension=2, tiled=True
        ).astype(jnp.float32),
    )
    grad_w_qkv, grad_w_out_self, grad_w_query, grad_w_kv, grad_w_out_cross, grad_up, grad_down = (
        summed
    )
    gain_total = lax.psum(jnp.stack([gain_self, gain_cross, gain_ffn]), ("dp", "tp"))
    share_width = gain_total.shape[1] // lax.axis_size("dp")
    gain_share = lax.dynamic_slice_in_dim(
        gain_total, lax.axis_index("dp") * share_width, share_width, 1
    )
    return (
        state_three.astype(jnp.bfloat16),
        grad_state,
        grad_memory,
        gain_share,
        grad_w_qkv,
        grad_w_out_self,
        grad_w_query,
        grad_w_kv,
        grad_w_out_cross,
        grad_up,
        grad_down,
    )


def solution(mesh):
    in_specs = (
        P("dp", "tp", None),
        P("dp", "tp", None),
        P("dp", None),
        P("dp", None),
        P(),
        P(None, None, "tp"),
        P("tp", None),
        P(None, "tp"),
        P(None, None, "tp"),
        P("tp", None),
        P(None, None, "tp"),
        P(None, "tp", None),
        P("dp", "tp", None),
    )
    out_specs = (
        P("dp", "tp", None),
        P("dp", "tp", None),
        P("dp", "tp", None),
        P(None, "dp"),
        P(None, "dp", "tp"),
        P("tp", "dp"),
        P("dp", "tp"),
        P(None, "dp", "tp"),
        P("tp", "dp"),
        P(None, "dp", "tp"),
        P(None, "tp", "dp"),
    )
    return jax.shard_map(
        per_device, mesh=mesh, in_specs=in_specs, out_specs=out_specs, check_vma=False
    )
```

profile of v0, /device:TPU:0, one launch (start us, length us, event | category | flops | bytes accessed | tf_op | source)
XLA Modules:
  0.0 1352.5 jit_solution(12351397615348398571)
XLA Ops:
  14.4 22.6 %all-gather.12.cloned.1.call-done = bf16[1,1024,512]{2,1,0:T(8,128)(2,1)} async-done(((bf16[1,512,512]{2,1,0:T(8,128)(2,1)}), bf16[1,1024,512]{2,1,0:T(8,128)(2,1)}) %all-gather.12.cloned.1.call-update) | async-done | bytes 1048592 | tf_op jit(solution)/shard_map/all_gather | solution.py:73
  59.3 31.2 %reduce-scatter.15.cloned.1.call-done = f32[1,512,512]{2,1,0:T(8,128)} async-done(((f32[1,1024,512]{2,1,0:T(8,128)}), f32[1,512,512]{2,1,0:T(8,128)}) %reduce-scatter.15.cloned.1.call-update) | async-done | bytes 1048592 | tf_op jit(solution)/shard_map/reduce_scatter | solution.py:77
  96.0 17.5 %all-gather.14.cloned.1.call-done = bf16[1,1024,512]{2,1,0:T(8,128)(2,1)} async-done(((bf16[1,512,512]{2,1,0:T(8,128)(2,1)}), bf16[1,1024,512]{2,1,0:T(8,128)(2,1)}) %all-gather.14.cloned.1.call-update) | async-done | bytes 1048592 | tf_op jit(solution)/shard_map/all_gather | solution.py:273
  115.5 21.3 %all-gather.16.cloned.1.call-done = bf16[1,1024,512]{2,1,0:T(8,128)(2,1)} async-done(((bf16[1,512,512]{2,1,0:T(8,128)(2,1)}), bf16[1,1024,512]{2,1,0:T(8,128)(2,1)}) %all-gather.16.cloned.1.call-update) | async-done | bytes 1048592 | tf_op jit(solution)/shard_map/all_gather | solution.py:73
  151.9 16.2 %fusion.94 = bf16[4,64,1024]{2,1,0:T(8,128)(2,1)} fusion(bf16[1024,4,64]{0,2,1:T(8,128)(2,1)S(1)} %bitcast.288, f32[4,1024]{1,0:T(4,128)S(1)} %fusion.222, f32[4,1024,1024]{1,2,0:T(8,128)} %fusion.225), kind=kOutput, calls=%fused_computation.150 | convolution fusion | flops 558109696 | bytes 17842176 | tf_op jit(solution)/shard_map/while/body/eval_jaxpr/hqk,khd->qhd/dot_general | solution.py:159
  171.1 31.9 %reduce-scatter.17.cloned.1.call-done = f32[1,512,512]{2,1,0:T(8,128)} async-done(((f32[1,1024,512]{2,1,0:T(8,128)}), f32[1,512,512]{2,1,0:T(8,128)}) %reduce-scatter.17.cloned.1.call-update) | async-done | bytes 1048592 | tf_op jit(solution)/shard_map/reduce_scatter | solution.py:77
  206.9 20.4 %all-gather.18.cloned.1.call-done = bf16[1,1024,512]{2,1,0:T(8,128)(2,1)} async-done(((bf16[1,512,512]{2,1,0:T(8,128)(2,1)}), bf16[1,1024,512]{2,1,0:T(8,128)(2,1)}) %all-gather.18.cloned.1.call-update) | async-done | bytes 1048592 | tf_op jit(solution)/shard_map/all_gather | solution.py:73
  227.3 13.0 fusion.64
  240.4 31.9 %reduce-scatter.19.cloned.1.call-done = f32[1,512,512]{2,1,0:T(8,128)} async-done(((f32[1,1024,512]{2,1,0:T(8,128)}), f32[1,512,512]{2,1,0:T(8,128)}) %reduce-scatter.19.cloned.1.call-update) | async-done | bytes 1048592 | tf_op jit(solution)/shard_map/reduce_scatter | solution.py:77
  276.8 21.2 %all-gather.20.cloned.1.call-done = bf16[1,1024,512]{2,1,0:T(8,128)(2,1)} async-done(((bf16[1,512,512]{2,1,0:T(8,128)(2,1)}), bf16[1,1024,512]{2,1,0:T(8,128)(2,1)}) %all-gather.20.cloned.1.call-update) | async-done | bytes 1048592 | tf_op jit(solution)/shard_map/all_gather | solution.py:73
  301.3 9.9 fusion.223
  322.0 31.3 %reduce-scatter.21.cloned.1.call-done = f32[1,512,512]{2,1,0:T(8,128)} async-done(((f32[1,1024,512]{2,1,0:T(8,128)}), f32[1,512,512]{2,1,0:T(8,128)}) %reduce-scatter.21.cloned.1.call-update) | async-done | bytes 1048592 | tf_op jit(solution)/shard_map/reduce_scatter | solution.py:77
  356.1 20.0 %all-gather.22.cloned.1.call-done = bf16[1,1024,512]{2,1,0:T(8,128)(2,1)} async-done(((bf16[1,512,512]{2,1,0:T(8,128)(2,1)}), bf16[1,1024,512]{2,1,0:T(8,128)(2,1)}) %all-gather.22.cloned.1.call-update) | async-done | bytes 1048592 | tf_op jit(solution)/shard_map/all_gather | solution.py:273
  379.0 20.6 %all-gather.24.cloned.1.call-done = bf16[1,1024,512]{2,1,0:T(8,128)(2,1)} async-done(((bf16[1,512,512]{2,1,0:T(8,128)(2,1)}), bf16[1,1024,512]{2,1,0:T(8,128)(2,1)}) %all-gather.24.cloned.1.call-update) | async-done | bytes 1048592 | tf_op jit(solution)/shard_map/all_gather | solution.py:73
  420.3 31.7 %reduce-scatter.23.cloned.1.call-done = f32[1,512,512]{2,1,0:T(8,128)} async-done(((f32[1,1024,512]{2,1,0:T(8,128)}), f32[1,512,512]{2,1,0:T(8,128)}) %reduce-scatter.23.cloned.1.call-update) | async-done | bytes 1048592 | tf_op jit(solution)/shard_map/reduce_scatter | solution.py:77
  455.4 20.8 %all-gather.26.cloned.1.call-done = bf16[1,1024,512]{2,1,0:T(8,128)(2,1)} async-done(((bf16[1,512,512]{2,1,0:T(8,128)(2,1)}), bf16[1,1024,512]{2,1,0:T(8,128)(2,1)}) %all-gather.26.cloned.1.call-update) | async-done | bytes 1048592 | tf_op jit(solution)/shard_map/all_gather | solution.py:73
  476.2 12.4 fusion.25
  488.6 10.4 all-gather.28.cloned.1.call-done
  510.5 31.9 %reduce-scatter.25.cloned.1.call-done = f32[1,512,512]{2,1,0:T(8,128)} async-done(((f32[1,1024,512]{2,1,0:T(8,128)}), f32[1,512,512]{2,1,0:T(8,128)}) %reduce-scatter.25.cloned.1.call-update) | async-done | bytes 1048592 | tf_op jit(solution)/shard_map/reduce_scatter | solution.py:85
  548.2 21.0 %all-gather.30.cloned.1.call-done = bf16[1,1024,512]{2,1,0:T(8,128)(2,1)} async-done(((bf16[1,512,512]{2,1,0:T(8,128)(2,1)}), bf16[1,1024,512]{2,1,0:T(8,128)(2,1)}) %all-gather.30.cloned.1.call-update) | async-done | bytes 1048592 | tf_op jit(solution)/shard_map/all_gather | solution.py:81
  571.0 11.1 multiply_reduce_fusion.1
  582.1 11.8 multiply_convert_fusion.3
  599.5 20.4 %reduce-scatter.27.cloned.1.call-done = bf16[1,512,512]{2,1,0:T(8,128)(2,1)} async-done(((bf16[1,1024,512]{2,1,0:T(8,128)(2,1)}), bf16[1,512,512]{2,1,0:T(8,128)(2,1)}) %reduce-scatter.27.cloned.1.call-update) | async-done | bytes 524304 | tf_op jit(solution)/shard_map/reduce_scatter | solution.py:322
  654.4 14.9 %multiply_reduce_fusion = (f32[4,1024]{1,0:T(4,128)S(1)}, f32[4,1024,1024]{1,2,0:T(8,128)}) fusion(f32[4,1024,1024]{1,2,0:T(8,128)} %get-tuple-element.225, f32[4,1024]{1,0:T(4,128)S(1)} %get-tuple-element.224, bf16[1024,4,64]{0,2,1:T(8,128)(2,1)S(1)} %bitcast.280, bf16[1024,4,64]{0,2,1:T(8,128)(2,1)S(1)} %bitcast.285), kind=kOutput, calls=%fused_computation.7 | convolution fusion | flops 549449728 | bytes 34635776 | tf_op jit(solution)/shard_map/while/body/eval_jaxpr/qhd,khd->hqk/dot_general | solution.py:55
  730.9 33.7 %reduce-scatter.35.cloned.1.call-done = bf16[32,256]{1,0:T(8,128)(2,1)} async-done(((bf16[512,256]{1,0:T(8,128)(2,1)}), bf16[32,256]{1,0:T(8,128)(2,1)}) %reduce-scatter.35.cloned.1.call-update) | async-done | bytes 16400 | tf_op jit(solution)/shard_map/reduce_scatter | solution.py:343
  765.9 21.0 %reduce-scatter.31.cloned.1.call-done = bf16[1,512,512]{2,1,0:T(8,128)(2,1)} async-done(((bf16[1,1024,512]{2,1,0:T(8,128)(2,1)}), bf16[1,512,512]{2,1,0:T(8,128)(2,1)}) %reduce-scatter.31.cloned.1.call-update) | async-done | bytes 524304 | tf_op jit(solution)/shard_map/reduce_scatter | solution.py:325
  789.0 56.7 %reduce-scatter.33.cloned.1.call-done = bf16[256,32]{0,1:T(8,128)(2,1)} async-done(((bf16[256,512]{0,1:T(8,128)(2,1)}), bf16[256,32]{0,1:T(8,128)(2,1)}) %reduce-scatter.33.cloned.1.call-update) | async-done | bytes 16400 | tf_op jit(solution)/shard_map/reduce_scatter | solution.py:340
  847.0 97.1 %all-reduce.5.cloned.1.call-done = (bf16[3,512,256]{2,0,1:T(4,128)(2,1)}, bf16[2,512,256]{2,0,1:T(2,128)(2,1)}) async-done(((bf16[3,512,256]{2,0,1:T(4,128)(2,1)}, bf16[2,512,256]{2,0,1:T(2,128)(2,1)}), (bf16[3,512,256]{2,0,1:T(4,128)(2,1)}, bf16[2,512,256]{2,0,1:T(2,128)(2,1)})) %all-reduce.5.cloned.1.call-update) | async-done | bytes 1310736
  947.1 30.5 %reduce-scatter.29.cloned.1.call-done = f32[1,512,512]{2,1,0:T(8,128)} async-done(((f32[1,1024,512]{2,1,0:T(8,128)}), f32[1,512,512]{2,1,0:T(8,128)}) %reduce-scatter.29.cloned.1.call-update) | async-done | bytes 1048592 | tf_op jit(solution)/shard_map/reduce_scatter | solution.py:85
  980.9 39.4 %psum.7 = f32[3,512]{1,0:T(4,128)S(1)} all-reduce(f32[3,512]{1,0:T(4,128)S(1)} %pad_maximum_fusion.6), channel_id=1, replica_groups=mesh['dp'=16,'tp'=2] {'dp','tp'}, use_global_device_ids=true, to_apply=%region_42.43 | all-reduce | flops 1536 | bytes 12288 | tf_op jit(solution)/shard_map/psum | solution.py:362
  1023.6 137.2 %reduce-scatter.39.cloned.1.call-done = bf16[16,32,1024]{2,1,0:T(8,128)(2,1)} async-done(((bf16[16,512,1024]{2,1,0:T(8,128)(2,1)}), bf16[16,32,1024]{2,1,0:T(8,128)(2,1)}) %reduce-scatter.39.cloned.1.call-update) | async-done | bytes 1048592 | tf_op jit(solution)/shard_map/reduce_scatter | solution.py:352
  1163.6 179.3 %reduce-scatter.41.cloned.1.call-done = bf16[16,1024,32]{1,2,0:T(8,128)(2,1)} async-done(((bf16[16,1024,512]{1,2,0:T(8,128)(2,1)}), bf16[16,1024,32]{1,2,0:T(8,128)(2,1)}) %reduce-scatter.41.cloned.1.call-update) | async-done | bytes 1048592 | tf_op jit(solution)/shard_map/reduce_scatter | solution.py:355
  (296 shorter events, 245.5 us)
Async XLA Ops:
  7.2 29.8 %all-gather.12.cloned.1.call-start = ((), (), s32[]{:S(2)}) async-start(), calls=%async_computation.14 | async-start | bytes 1572864 | tf_op jit(solution)/shard_map/all_gather | solution.py:73
  10.7 264.9 %copy-start.49 = (f32[1,512]{1,0:T(1,128)}, f32[1,512]{1,0:T(1,128)S(1)}, u32[]{:S(2)}) copy-start(f32[1,512]{1,0:T(1,128)S(1)} %get-tuple-element.220) | copy-start | bytes 6148
  12.8 77.7 %reduce-scatter.15.cloned.1.call-start = ((), (), s32[]{:S(2)}) async-start(), calls=%async_computation.15 | async-start | bytes 3145728 | tf_op jit(solution)/shard_map/reduce_scatter | solution.py:77
  58.5 54.9 %all-gather.14.cloned.1.call-start = ((), (), s32[]{:S(2)}) async-start(), calls=%async_computation.16 | async-start | bytes 1572864 | tf_op jit(solution)/shard_map/all_gather | solution.py:273
  59.3 77.6 %all-gather.16.cloned.1.call-start = ((), (), s32[]{:S(2)}) async-start(), calls=%async_computation.17 | async-start | bytes 1572864 | tf_op jit(solution)/shard_map/all_gather | solution.py:73
  95.7 107.3 %reduce-scatter.17.cloned.1.call-start = ((), (), s32[]{:S(2)}) async-start(), calls=%async_computation.18 | async-start | bytes 3145728 | tf_op jit(solution)/shard_map/reduce_scatter | solution.py:77
  171.0 56.2 %all-gather.18.cloned.1.call-start = ((), (), s32[]{:S(2)}) async-start(), calls=%async_computation.19 | async-start | bytes 1572864 | tf_op jit(solution)/shard_map/all_gather | solution.py:73
  205.8 66.5 %reduce-scatter.19.cloned.1.call-start = ((), (), s32[]{:S(2)}) async-start(), calls=%async_computation.20 | async-start | bytes 3145728 | tf_op jit(solution)/shard_map/reduce_scatter | solution.py:77
  240.3 57.8 %all-gather.20.cloned.1.call-start = ((), (), s32[]{:S(2)}) async-start(), calls=%async_computation.21 | async-start | bytes 1572864 | tf_op jit(solution)/shard_map/all_gather | solution.py:73
  276.6 76.7 %reduce-scatter.21.cloned.1.call-start = ((), (), s32[]{:S(2)}) async-start(), calls=%async_computation.22 | async-start | bytes 3145728 | tf_op jit(solution)/shard_map/reduce_scatter | solution.py:77
  321.4 54.7 %all-gather.22.cloned.1.call-start = ((), (), s32[]{:S(2)}) async-start(), calls=%async_computation.23 | async-start | bytes 1572864 | tf_op jit(solution)/shard_map/all_gather | solution.py:273
  322.0 77.6 %all-gather.24.cloned.1.call-start = ((), (), s32[]{:S(2)}) async-start(), calls=%async_computation.24 | async-start | bytes 1572864 | tf_op jit(solution)/shard_map/all_gather | solution.py:73
  356.1 95.9 %reduce-scatter.23.cloned.1.call-start = ((), (), s32[]{:S(2)}) async-start(), calls=%async_computation.25 | async-start | bytes 3145728 | tf_op jit(solution)/shard_map/reduce_scatter | solution.py:77
  420.0 56.2 %all-gather.26.cloned.1.call-start = ((), (), s32[]{:S(2)}) async-start(), calls=%async_computation.26 | async-start | bytes 1572864 | tf_op jit(solution)/shard_map/all_gather | solution.py:73
  454.7 44.3 %all-gather.28.cloned.1.call-start = ((), (), s32[]{:S(2)}) async-start(), calls=%async_computation.27 | async-start | bytes 1572864 | tf_op jit(solution)/shard_map/all_gather | solution.py:81
  455.3 87.2 %reduce-scatter.25.cloned.1.call-start = ((), (), s32[]{:S(2)}) async-start(), calls=%async_computation.28 | async-start | bytes 3145728 | tf_op jit(solution)/shard_map/reduce_scatter | solution.py:85
  510.5 58.8 %all-gather.30.cloned.1.call-start = ((), (), s32[]{:S(2)}) async-start(), calls=%async_computation.29 | async-start | bytes 1572864 | tf_op jit(solution)/shard_map/all_gather | solution.py:81
  547.8 72.2 %reduce-scatter.27.cloned.1.call-start = ((), (), s32[]{:S(2)}) async-start(), calls=%async_computation.30 | async-start | bytes 1572864 | tf_op jit(solution)/shard_map/reduce_scatter | solution.py:322
  599.5 53.1 %all-gather.32.cloned.1.call-start = ((), (), s32[]{:S(2)}) async-start(), calls=%async_computation.31 | async-start | bytes 1572864 | tf_op jit(solution)/shard_map/all_gather | solution.py:81
  625.7 103.8 %reduce-scatter.37.cloned.1.call-start = ((), (), s32[]{:S(2)}) async-start(), calls=%async_computation.36 | async-start | bytes 278528 | tf_op jit(solution)/shard_map/reduce_scatter | solution.py:349
  636.6 127.9 %reduce-scatter.35.cloned.1.call-start = ((), (), s32[]{:S(2)}) async-start(), calls=%async_computation.35 | async-start | bytes 278528 | tf_op jit(solution)/shard_map/reduce_scatter | solution.py:343
  646.3 140.6 %reduce-scatter.31.cloned.1.call-start = ((), (), s32[]{:S(2)}) async-start(), calls=%async_computation.33 | async-start | bytes 1572864 | tf_op jit(solution)/shard_map/reduce_scatter | solution.py:325
  652.4 193.3 %reduce-scatter.33.cloned.1.call-start = ((), (), s32[]{:S(2)}) async-start(), calls=%async_computation.34 | async-start | bytes 278528 | tf_op jit(solution)/shard_map/reduce_scatter | solution.py:340
  692.9 251.3 %all-reduce.5.cloned.1.call-start = ((), (), s32[]{:S(2)}) async-start(), calls=%async_computation.39 | async-start | bytes 3145728
  702.5 275.1 %reduce-scatter.29.cloned.1.call-start = ((), (), s32[]{:S(2)}) async-start(), calls=%async_computation.32 | async-start | bytes 3145728 | tf_op jit(solution)/shard_map/reduce_scatter | solution.py:85
  706.2 454.6 %reduce-scatter.39.cloned.1.call-start = ((), (), s32[]{:S(2)}) async-start(), calls=%async_computation.37 | async-start | bytes 17825792 | tf_op jit(solution)/shard_map/reduce_scatter | solution.py:352
  715.2 627.7 %reduce-scatter.41.cloned.1.call-start = ((), (), s32[]{:S(2)}) async-start(), calls=%async_computation.38 | async-start | bytes 17825792 | tf_op jit(solution)/shard_map/reduce_scatter | solution.py:355
  727.6 250.0 %copy-start.48 = (f32[512]{0:T(512)S(1)}, f32[512]{0:T(512)}, u32[]{:S(2)}) copy-start(f32[512]{0:T(512)} %copy-done.47) | copy-start | bytes 6148
  727.6 250.0 %copy-start.50 = (f32[1,512]{1,0:T(1,128)S(1)}, f32[1,512]{1,0:T(1,128)}, u32[]{:S(2)}) copy-start(f32[1,512]{1,0:T(1,128)} %copy-done.49) | copy-start | bytes 6148
  727.6 251.5 %copy-start.54 = (f32[512]{0:T(512)S(1)}, f32[512]{0:T(512)}, u32[]{:S(2)}) copy-start(f32[512]{0:T(512)} %copy-done.53) | copy-start | bytes 6148
  727.6 251.5 %copy-start.52 = (f32[512]{0:T(512)S(1)}, f32[512]{0:T(512)}, u32[]{:S(2)}) copy-start(f32[512]{0:T(512)} %copy-done.51) | copy-start | bytes 6148
  727.7 293.4 %copy-start.11 = (f32[1,512,512]{2,1,0:T(8,128)S(1)}, f32[1,512,512]{2,1,0:T(8,128)}, u32[]{:S(2)}) copy-start(f32[1,512,512]{2,1,0:T(8,128)} %get-tuple-element.200) | copy-start | bytes 3145732
  (56 other events, 1008.8 us)
Sparse Core Ops, SparseCore 0:
  12.9 24.0 all-gather.11
  58.6 31.8 reduce-scatter.14
  92.1 21.2 all-gather.13
  115.5 21.2 all-gather.15
  171.2 31.8 reduce-scatter.16
  205.9 21.2 all-gather.17
  240.4 31.8 reduce-scatter.18
  276.7 21.2 all-gather.19
  321.5 31.8 reduce-scatter.20
  354.7 21.3 all-gather.21
  378.2 21.2 all-gather.23
  420.2 31.8 reduce-scatter.22
  454.9 21.3 all-gather.25
  477.7 21.2 all-gather.27
  510.6 31.8 reduce-scatter.24
  547.9 21.2 all-gather.29
  599.6 20.3 reduce-scatter.26
  625.8 21.2 all-gather.31
  651.0 55.2 reduce-scatter.36
  710.1 54.3 reduce-scatter.34
  767.4 19.3 reduce-scatter.30
  790.3 55.2 reduce-scatter.32
  849.3 94.8 all-reduce.4
  946.8 30.7 reduce-scatter.28
  982.2 178.5 reduce-scatter.38
  1165.4 177.5 reduce-scatter.40
where the time goes:
time: 1360 us; the launch traced here: 1350 us
  waiting for transfers between devices  964 us (71%)
  matrix products  223 us (16%)
  other arithmetic  84.1 us (6%)
  blocking collectives  39.4 us (3%)
  local copies, waits for them, and re-layouts  22.4 us (2%)
  between operations  16.5 us (1%)
    reduce_scatter x1, waiting for transfers between devices, per_device(): lax.psum_scatter(grad_down.astype(jnp.bfloat16), 'dp', scatter_dimension=...  179 us
    reduce_scatter x5, waiting for transfers between devices, sum_tokens(): return lax.psum_scatter(partial_out, 'tp', scatter_dimension=1, tiled=True)  158 us
    reduce_scatter x1, waiting for transfers between devices, per_device(): lax.psum_scatter(grad_up.astype(jnp.bfloat16), 'dp', scatter_dimension=1,...  137 us
    all_gather x6, waiting for transfers between devices, spread_tokens(): return lax.all_gather(normed, 'tp', axis=1, tiled=True)  127 us
    unnamed x27, waiting for transfers between devices  99.2 us
    reduce_scatter x2, waiting for transfers between devices, sum_grads(): return lax.psum_scatter(grad_normed, 'tp', scatter_dimension=1, tiled=True)  62.4 us
    reduce_scatter x1, waiting for transfers between devices, per_device(): lax.psum_scatter(grad_w_out_self.astype(jnp.bfloat16), 'dp', scatter_dime...  56.7 us
    psum x1, blocking collectives, per_device(): lax.psum(jnp.stack([gain_self, gain_cross, gain_ffn]), ('dp', 'tp'))  39.4 us
  transfers between devices with their start and end apart: 26, of which 24 were waited for; matrix products, arithmetic and copies ran while one was open for 11% of the time, Pallas kernels for 0%

commit v1 on v0

--- a/solution.py
+++ b/solution.py
@@ -1,8 +1,11 @@
+import math
 from functools import partial
 
 import jax
 import jax.numpy as jnp
 from jax import lax
+from jax.experimental import pallas as pl
+from jax.experimental.pallas import tpu as pltpu
 from jax.sharding import PartitionSpec as P
 
 HEAD_DIM = 64
@@ -379,6 +382,690 @@
     )
 
 
+F32, BF16 = jnp.float32, jnp.bfloat16
+MESH = pl.DeviceIdType.MESH
+LOG2E = math.log2(math.e)
+QSCALE = LOG2E * HEAD_DIM ** -0.5
+NN = (((1,), (0,)), ((), ()))
+NT = (((1,), (1,)), ((), ()))
+TN = (((0,), (0,)), ((), ()))
+
+LEN, WIDTH, COLS, HIDDEN, BLOCK, HALF = 1024, 512, 256, 1024, 256, 512
+BLOCKS = LEN // BLOCK
+
+
+def dot(left, right, dims=NN):
+    return lax.dot_general(left, right, dims, preferred_element_type=F32)
+
+
+def head_mask(block, side):
+    lanes = lax.broadcasted_iota(jnp.int32, block.shape, 1)
+    keep = (lanes >= HEAD_DIM) if side else (lanes < HEAD_DIM)
+    return jnp.where(keep, block, jnp.zeros_like(block))
+
+
+def window_bias(key_at, query_at, keys, queries, starts):
+    key_place = key_at + lax.broadcasted_iota(jnp.int32, (keys, queries), 0)
+    query_place = query_at + lax.broadcasted_iota(jnp.int32, (keys, queries), 1)
+    return jnp.where((key_place >= starts) & (key_place <= query_place), 0.0, -1e30)
+
+
+def attend_block(qs, k, vt, ht, lse, q_at, q_len, k_at, k_len, bias):
+    for h in range(4):
+        lanes = slice((h // 2) * 128, (h // 2) * 128 + 128)
+        rows = slice(h * 64, h * 64 + 64)
+        keys = head_mask(k[pl.ds(k_at, k_len), lanes], h % 2)
+        s = dot(keys, qs[pl.ds(q_at, q_len), lanes], NT)
+        if bias is not None:
+            s = s + bias
+        top = jnp.max(s, axis=0, keepdims=True)
+        p = jnp.exp2(s - top)
+        total = jnp.sum(p, axis=0, keepdims=True)
+        out = dot(vt[rows, pl.ds(k_at, k_len)], p.astype(BF16)) * (1.0 / total)
+        ht[rows, pl.ds(q_at, q_len)] = out.astype(BF16)
+        lse[h:h + 1, pl.ds(q_at, q_len)] = top + jnp.log2(total)
+
+
+def attend_back_block(qs, k, v, kt, gh, lse, inner, dqt, dk, dv, k_at, k_len, q_at, q_len, bias):
+    for pair in range(2):
+        lanes = slice(pair * 128, pair * 128 + 128)
+        sum_k, sum_v = None, None
+        qp = qs[pl.ds(q_at, q_len), lanes]
+        gp = gh[pl.ds(q_at, q_len), lanes]
+        for side in range(2):
+            h = pair * 2 + side
+            rows = slice(h * 64, h * 64 + 64)
+            keys = head_mask(k[pl.ds(k_at, k_len), lanes], side)
+            vals = head_mask(v[pl.ds(k_at, k_len), lanes], side)
+            s = dot(keys, qp, NT)
+            if bias is not None:
+                s = s + bias
+            p = jnp.exp2(s - lse[h:h + 1, pl.ds(q_at, q_len)])
+            dp = dot(vals, gp, NT)
+            ds = (p * (dp - inner[h:h + 1, pl.ds(q_at, q_len)])).astype(BF16)
+            part_v = dot(p.astype(BF16), head_mask(gp, side))
+            part_k = dot(ds, head_mask(qp, side))
+            sum_v = part_v if sum_v is None else sum_v + part_v
+            sum_k = part_k if sum_k is None else sum_k + part_k
+            dqt[rows, pl.ds(q_at, q_len)] += dot(kt[rows, pl.ds(k_at, k_len)], ds)
+        dv[pl.ds(k_at, k_len), lanes] = sum_v.astype(BF16)
+        dk[pl.ds(k_at, k_len), lanes] = (sum_k * math.log(2.0)).astype(BF16)
+
+
+def gelu_parts(pre):
+    gauss = jnp.exp2(pre * pre * (-0.5 * LOG2E))
+    t = 1.0 / (1.0 + (0.3275911 / math.sqrt(2.0)) * jnp.abs(pre))
+    poly = t * (0.254829592 * 0.5 + t * (-0.284496736 * 0.5 + t * (
+        1.421413741 * 0.5 + t * (-1.453152027 * 0.5 + t * (1.061405429 * 0.5)))))
+    tail = poly * gauss
+    phi = jnp.where(pre >= 0, 1.0 - tail, tail)
+    return phi, phi + pre * (gauss * (1.0 / math.sqrt(2.0 * math.pi)))
+
+
+def normalise(x):
+    c = x - jnp.mean(x, axis=-1, keepdims=True)
+    r = lax.rsqrt(jnp.mean(c * c, axis=-1, keepdims=True) + epsilon)
+    return c * r, r
+
+
+def norm_back(state, gain, grad):
+    xhat, r = normalise(state)
+    y = grad * gain
+    m1 = jnp.mean(y, axis=-1, keepdims=True)
+    m2 = jnp.mean(y * xhat, axis=-1, keepdims=True)
+    return r * (y - m1 - xhat * m2), jnp.sum(grad * xhat, axis=0, keepdims=True)
+
+
+def block_rows(i):
+    return pl.ds(pl.multiple_of(i * BLOCK, BLOCK), BLOCK)
+
+
+def each(count, body):
+    def step(i, carry):
+        body(i)
+        return carry
+
+    lax.fori_loop(0, count, step, 0)
+
+
+def layer_kernel(
+    n_dp,
+    lens, expert, gains, x_in, mem_in, cot_in, wqkv_in, wos_in, wq_in, wkv_in, woc_in, up_in, down_in,
+    lo_out, gi_out, gm_out, eu_out, ed_out, a1_out, a2_out, g_out,
+    x, mem, cot, wqkv, wos, wq, wkv, woc, up, down, starts,
+    s1, s2, gs, n0, n1, n2, q0, k0, v0, q1, k1, v1, kt0, vt0, kt1, vt1, ht0, ht1, lse0, lse1, inner,
+    gb, gh, dqt, dq, dk, dv, hid, gpre, nt, eu, ed, a1, a2,
+    snd, rcv, sndh, rcvh, leaving, half_out, gain_sum, g_send,
+    y_send, y_recv, c_send, c_recv, x_send, x_recv, h_send, h_recv, sc_send, sc_recv, g_ssem, g_rsem, o_send, o_recv,
+):
+    d, t = lax.axis_index("dp"), lax.axis_index("tp")
+    c = lax.rem(d, 2)
+    k2 = d - c
+    row = k2 + t
+    lin = d * 2 + t
+    n_all = n_dp * 2
+    diag = (k2 + 1 - c, 1 - t)
+    sib = (k2 + 1 - c, t)
+    swaps = c != t
+    stays = c == t
+
+    def remote(src, dst, ssem, rsem, to):
+        return pltpu.make_async_remote_copy(
+            src_ref=src, dst_ref=dst, send_sem=ssem, recv_sem=rsem, device_id=to, device_id_type=MESH)
+
+    own = pl.ds(pl.multiple_of(c * HALF, HALF), HALF)
+    other = pl.ds(pl.multiple_of((1 - c) * HALF, HALF), HALF)
+    theirs = pl.ds(pl.multiple_of(t * HALF, HALF), HALF)
+
+    brought = [
+        (x_in, lambda p: x.at[p]), (wqkv_in, wqkv), (wos_in, wos), (mem_in, lambda p: mem.at[p]), (wq_in, wq),
+        (wkv_in, wkv), (woc_in, woc), (up_in, up), (down_in, down), (cot_in, lambda p: cot.at[p]),
+    ]
+    X, WQKV, WOS, MEM, WQ, WKV, WOC, UP, DOWN, COT = range(10)
+
+    def bring(n, place):
+        src, dst = brought[n]
+        dst = dst(place) if callable(dst) else dst
+        return (lambda: remote(src, dst, y_send.at[n], y_recv.at[n], diag),
+                lambda: pltpu.make_async_copy(src, dst, y_recv.at[n]))
+
+    def start_bring(n):
+        far, near = bring(n, theirs)
+
+        @pl.when(swaps)
+        def _():
+            far().start()
+
+    def start_near(n):
+        far, near = bring(n, own)
+
+        @pl.when(stays)
+        def _():
+            near().start()
+
+    def wait_bring(n):
+        far, near = bring(n, own)
+
+        @pl.when(swaps)
+        def _():
+            far().wait_recv()
+
+        @pl.when(stays)
+        def _():
+            near().wait()
+
+    def share(n, buf):
+        return remote(buf.at[own], buf.at[own], c_send.at[n], c_recv.at[n], sib)
+
+    def share_starts():
+        return remote(starts, starts, c_send.at[3], c_recv.at[3], sib)
+
+    for n in (X, WQKV, MEM, COT, WOS, WQ, WKV, WOC, UP, DOWN):
+        start_near(n)
+    barrier = pltpu.get_barrier_semaphore()
+
+    def greet(i):
+        to = lax.rem(lin + 1 + i, n_all)
+        pl.semaphore_signal(barrier, inc=1, device_id=(lax.div(to, 2), lax.rem(to, 2)), device_id_type=MESH)
+
+    each(n_all - 1, greet)
+
+    @pl.when(stays)
+    def _():
+        places = lax.broadcasted_iota(jnp.int32, (8, LEN), 1)
+        start, level = jnp.int32(0), jnp.zeros((8, LEN), jnp.int32)
+        for s in range(lens.shape[1]):
+            level = jnp.where(places >= start, start, level)
+            start = start + lens[0, s]
+        starts[...] = level
+
+    pl.semaphore_wait(barrier, n_all - 1)
+    for n in range(10):
+        start_bring(n)
+
+    @pl.when(stays)
+    def _():
+        share_starts().start()
+
+    def wait_near(n):
+        near = bring(n, own)[1]
+
+        @pl.when(stays)
+        def _():
+            near().wait()
+
+    def wait_swapped(n):
+        far = bring(n, own)[0]
+
+        @pl.when(swaps)
+        def _():
+            far().wait_recv()
+
+    wait_bring(X)
+    share(0, x).start()
+
+    @pl.when(stays)
+    def _():
+        wait_near(MEM)
+        share(1, mem).start()
+        wait_near(COT)
+        share(2, cot).start()
+
+    def self_project(i):
+        r = block_rows(i)
+        xhat, _ = normalise(x[r, :].astype(F32))
+        nn = (xhat * gains[0:1, :]).astype(BF16)
+        n0[r, :] = nn
+        q0[r, :] = (dot(nn, wqkv[0]) * QSCALE).astype(BF16)
+        k0[r, :] = dot(nn, wqkv[1]).astype(BF16)
+        v0[r, :] = dot(nn, wqkv[2]).astype(BF16)
+
+    wait_bring(WQKV)
+    each(2, lambda i: self_project(c * 2 + i))
+    share(0, x).wait_recv()
+    each(2, lambda i: self_project((1 - c) * 2 + i))
+    kt0[...] = k0[...].T
+    vt0[...] = v0[...].T
+
+    @pl.when(swaps)
+    def _():
+        share_starts().wait_recv()
+
+    wait_bring(WOS)
+
+    def exchange(e, i):
+        r = block_rows(i)
+        return remote(snd.at[e, r], rcv.at[e, r], x_send.at[e, i], x_recv.at[e, i], sib)
+
+    def self_out(i):
+        r = block_rows(i)
+        snd[0, r, :] = dot(ht0[:, r], wos[...], TN).astype(BF16)
+        exchange(0, i).start()
+
+    attend_block(q0, k0, vt0, ht0, lse0, 0, 256, 0, 256, window_bias(0, 0, 256, 256, starts[0:1, 0:256]))
+    self_out(0)
+
+    def self_block(j):
+        i = j + 1
+        q_at = pl.multiple_of(i * 256, 256)
+        k_at = pl.multiple_of(j * 256, 256)
+        attend_block(q0, k0, vt0, ht0, lse0, q_at, 256, k_at, 512,
+                     window_bias(k_at, q_at, 512, 256, starts[0:1, pl.ds(q_at, 256)]))
+        self_out(i)
+
+    each(3, self_block)
+
+    wait_swapped(MEM)
+
+    @pl.when(swaps)
+    def _():
+        share(1, mem).start()
+
+    wait_bring(WKV)
+
+    def memory_project(i):
+        r = block_rows(i)
+        k1[r, :] = dot(mem[r, :], wkv[0]).astype(BF16)
+        v1[r, :] = dot(mem[r, :], wkv[1]).astype(BF16)
+
+    each(2, lambda i: memory_project(c * 2 + i))
+    share(1, mem).wait_recv()
+    each(2, lambda i: memory_project((1 - c) * 2 + i))
+    kt1[...] = k1[...].T
+    vt1[...] = v1[...].T
+    wait_bring(WQ)
+    wait_bring(WOC)
+
+    def cross_block(i):
+        r = block_rows(i)
+        exchange(0, i).wait_recv()
+        state = x[r, :].astype(F32) + (snd[0, r, :].astype(F32) + rcv[0, r, :].astype(F32))
+        s1[r, :] = state
+        xhat, _ = normalise(state)
+        nn = (xhat * gains[1:2, :]).astype(BF16)
+        n1[r, :] = nn
+        q1[r, :] = (dot(nn, wq[...]) * QSCALE).astype(BF16)
+        attend_block(q1, k1, vt1, ht1, lse1, pl.multiple_of(i * 256, 256), 256, 0, LEN, None)
+        snd[1, r, :] = dot(ht1[:, r], woc[...], TN).astype(BF16)
+        exchange(1, i).start()
+
+    each(BLOCKS, cross_block)
+
+    wait_bring(UP)
+    wait_bring(DOWN)
+    wait_swapped(COT)
+
+    @pl.when(swaps)
+    def _():
+        share(2, cot).start()
+
+    share(2, cot).wait_recv()
+
+    def half_exchange(e, i):
+        r = block_rows(i)
+        return remote(sndh.at[e, r], rcvh.at[e, r], h_send.at[e, i], h_recv.at[e, i], sib)
+
+    def expert_block(i):
+        r = block_rows(i)
+        exchange(1, i).wait_recv()
+        state = s1[r, :] + (snd[1, r, :].astype(F32) + rcv[1, r, :].astype(F32))
+        s2[r, :] = state
+        xhat, _ = normalise(state)
+        nn = (xhat * gains[2:3, :]).astype(BF16)
+        n2[r, :] = nn
+        for f in range(2):
+            cols = slice(f * 512, f * 512 + 512)
+            pre = dot(nn, up[:, cols])
+            phi, slope = gelu_parts(pre)
+            hid[r, cols] = (pre * phi).astype(BF16)
+            gpre[r, cols] = (dot(cot[r, :], down[cols, :], NT) * slope).astype(BF16)
+        snd[2, r, :] = dot(gpre[r, :], up[...], NT).astype(BF16)
+        exchange(2, i).start()
+        part = dot(hid[r, :], down[...])
+        mine = lax.div(i, 2) == c
+        low = lax.rem(i, 2)
+        rl = block_rows(low)
+
+        @pl.when(mine)
+        def _():
+            half_out[rl, :] = s2[r, :] + part
+
+        @pl.when(jnp.logical_not(mine))
+        def _():
+            sndh[0, rl, :] = part.astype(BF16)
+            half_exchange(0, low).start()
+
+    each(BLOCKS, expert_block)
+
+    def scatter(n, buf, out, action):
+        def one(s):
+            to = lax.rem(d + s, n_dp)
+            src = buf.at[pl.ds(pl.multiple_of(to * 32, 32), 32)]
+            action(remote(src, out.at[row], sc_send.at[n, s], sc_recv.at[n, row], (to, c)))
+
+        src = buf.at[pl.ds(pl.multiple_of(d * 32, 32), 32)]
+
+        @pl.when(stays)
+        def _():
+            if action is begin:
+                pltpu.make_async_copy(src, out.at[row], sc_recv.at[n, row]).start()
+
+        @pl.when(swaps)
+        def _():
+            action(remote(src, out.at[row], sc_send.at[n, 0], sc_recv.at[n, row], (d, c)))
+
+        each(n_dp - 1, lambda s: one(s + 1))
+
+    def begin(copy):
+        copy.start()
+
+    def finish_send(copy):
+        copy.wait_send()
+
+    def collect(n, buf, out):
+        def one(i):
+            @pl.when(stays & (i == row))
+            def _():
+                pltpu.make_async_copy(buf.at[pl.ds(0, 32)], out.at[i], sc_recv.at[n, i]).wait()
+
+            @pl.when(jnp.logical_not(stays & (i == row)))
+            def _():
+                remote(buf.at[pl.ds(0, 32)], out.at[i], sc_send.at[n, 0], sc_recv.at[n, i], diag).wait_recv()
+
+        each(n_dp, one)
+
+    def quarter(i):
+        return pl.ds(pl.multiple_of(i * 256, 256), 256)
+
+    nt[...] = n2[...].T
+
+    def up_grads(i):
+        eu[:, quarter(i)] = dot(nt[...], gpre[:, quarter(i)]).astype(BF16)
+
+    each(HIDDEN // 256, up_grads)
+    scatter(0, eu, eu_out, begin)
+    nt[...] = cot[...].T
+
+    def down_grads(i):
+        ed[:, quarter(i)] = dot(nt[...], hid[:, quarter(i)]).astype(BF16)
+
+    each(HIDDEN // 256, down_grads)
+    scatter(1, ed, ed_out, begin)
+
+    gain_sum[...] = jnp.zeros_like(gain_sum)
+
+    def branch_block(n, i, e, state, base, ht, w_out):
+        r = block_rows(i)
+        exchange(e, i).wait_recv()
+        grad = snd[e, r, :].astype(F32) + rcv[e, r, :].astype(F32)
+        step, share_gain = norm_back(state[r, :], gains[n:n + 1, :], grad)
+        total = base[r, :].astype(F32) + step
+        gs[r, :] = total
+        low = total.astype(BF16)
+        gb[r, :] = low
+        gain_sum[n:n + 1, :] += jnp.where(lax.div(i, 2) == c, share_gain, 0.0)
+        gh[r, :] = dot(low, w_out[...], NT).astype(BF16)
+        ght = dot(w_out[...], low, NT).astype(BF16).astype(F32)
+        prod = ght * ht[:, r].astype(F32)
+        for h in range(4):
+            inner[h:h + 1, r] = jnp.sum(prod[h * 64:h * 64 + 64], axis=0, keepdims=True)
+
+    each(BLOCKS, lambda i: branch_block(2, i, 2, s2, cot, ht1, woc))
+    dqt[...] = jnp.zeros_like(dqt)
+
+    def cross_back(i):
+        at = pl.multiple_of(i * 256, 256)
+        attend_back_block(q1, k1, v1, kt1, gh, lse1, inner, dqt, dk, dv, at, 256, 0, LEN, None)
+
+    each(BLOCKS, cross_back)
+    dq[...] = (dqt[...] * HEAD_DIM ** -0.5).astype(BF16).T
+
+    def cross_grads(i):
+        r = block_rows(i)
+        snd[3, r, :] = dot(dq[r, :], wq[...], NT).astype(BF16)
+        exchange(3, i).start()
+
+    each(BLOCKS, cross_grads)
+
+    def memory_grads(i):
+        r = block_rows(i)
+        part = dot(dk[r, :], wkv[0], NT) + dot(dv[r, :], wkv[1], NT)
+        mine = lax.div(i, 2) == c
+        low = lax.rem(i, 2)
+        rl = block_rows(low)
+
+        @pl.when(mine)
+        def _():
+            half_out[pl.ds(pl.multiple_of(HALF + low * BLOCK, BLOCK), BLOCK), :] = part
+
+        @pl.when(jnp.logical_not(mine))
+        def _():
+            sndh[1, rl, :] = part.astype(BF16)
+            half_exchange(1, low).start()
+
+    each(BLOCKS, memory_grads)
+    a1[:, 0:256] = dot(ht1[...], gb[...]).T.astype(BF16)
+    nt[...] = n1[...].T
+    a1[:, 256:512] = dot(nt[...], dq[...]).astype(BF16)
+    nt[...] = mem[...].T
+    a1[:, 512:768] = dot(nt[...], dk[...]).astype(BF16)
+    a1[:, 768:1024] = dot(nt[...], dv[...]).astype(BF16)
+    scatter(2, a1, a1_out, begin)
+
+    def leave(n, out):
+        buf = leaving.at[n]
+        return (lambda: remote(buf, out, o_send.at[n], o_recv.at[n], diag),
+                lambda: pltpu.make_async_copy(buf, out, o_recv.at[n]))
+
+    def start_leave(n, out):
+        far, near = leave(n, out)
+
+        @pl.when(swaps)
+        def _():
+            far().start()
+
+        @pl.when(stays)
+        def _():
+            near().start()
+
+    def wait_leave(n, out):
+        far, near = leave(n, out)
+
+        @pl.when(swaps)
+        def _():
+            far().wait()
+
+        @pl.when(stays)
+        def _():
+            near().wait()
+
+    for n in range(2):
+        for low in range(2):
+            half_exchange(n, low).wait_recv()
+            r = pl.ds(low * BLOCK, BLOCK)
+            whole = half_out[pl.ds(n * HALF + low * BLOCK, BLOCK), :] + rcvh[n, r, :].astype(F32)
+            leaving[n, r, :] = whole.astype(BF16)
+        start_leave(n, (lo_out, gm_out)[n])
+
+    each(BLOCKS, lambda i: branch_block(1, i, 3, s1, gs, ht0, wos))
+    dqt[...] = jnp.zeros_like(dqt)
+
+    def self_back(i):
+        at = pl.multiple_of(i * 256, 256)
+        attend_back_block(q0, k0, v0, kt0, gh, lse0, inner, dqt, dk, dv, at, 256, at, 512,
+                          window_bias(at, at, 256, 512, starts[0:1, pl.ds(at, 512)]))
+
+    each(BLOCKS - 1, self_back)
+    attend_back_block(q0, k0, v0, kt0, gh, lse0, inner, dqt, dk, dv, 768, 256, 768, 256,
+                      window_bias(768, 768, 256, 256, starts[0:1, 768:1024]))
+    dq[...] = (dqt[...] * HEAD_DIM ** -0.5).astype(BF16).T
+
+    nt[...] = n0[...].T
+    a2[:, 0:256] = dot(ht0[...], gb[...]).T.astype(BF16)
+    a2[:, 256:512] = dot(nt[...], dq[...]).astype(BF16)
+    a2[:, 512:768] = dot(nt[...], dk[...]).astype(BF16)
+    a2[:, 768:1024] = dot(nt[...], dv[...]).astype(BF16)
+    scatter(3, a2, a2_out, begin)
+
+    def input_grads(i):
+        r = block_rows(i)
+        return dot(dq[r, :], wqkv[0], NT) + dot(dk[r, :], wqkv[1], NT) + dot(dv[r, :], wqkv[2], NT)
+
+    def input_send(low):
+        rl = block_rows(low)
+        sndh[2, rl, :] = input_grads((1 - c) * 2 + low).astype(BF16)
+        half_exchange(2, low).start()
+
+    each(2, input_send)
+
+    def input_keep(low):
+        half_out[block_rows(low), :] = input_grads(c * 2 + low)
+
+    each(2, input_keep)
+
+    def input_done(low):
+        half_exchange(2, low).wait_recv()
+        rl = block_rows(low)
+        r = block_rows(c * 2 + low)
+        grad = half_out[rl, :] + rcvh[2, rl, :].astype(F32)
+        step, share_gain = norm_back(x[r, :].astype(F32), gains[0:1, :], grad)
+        gain_sum[0:1, :] += share_gain
+        leaving[2, rl, :] = (gs[r, :] + step).astype(BF16)
+
+    each(2, input_done)
+    start_leave(2, gi_out)
+
+    number = jnp.full((1, 128), expert[0, 0].astype(F32))
+    for j in range(n_dp):
+        turned = gain_sum[...] if j == 0 else pltpu.roll(gain_sum[...], (WIDTH - 32 * j) % WIDTH, 1)
+        g_send[j] = turned[:, :128]
+        g_send[j, 3:4, :] = number
+
+    def gain_copy(s):
+        to = lax.rem(lin + s, n_all)
+        to_dp = lax.div(to, 2)
+        return remote(g_send.at[to_dp], g_out.at[lin], g_ssem.at[s], g_rsem.at[lin], (to_dp, lax.rem(to, 2)))
+
+    each(n_all - 1, lambda s: gain_copy(s + 1).start())
+    keep_gain = pltpu.make_async_copy(g_send.at[d], g_out.at[lin], g_rsem.at[lin])
+    keep_gain.start()
+
+    wait_leave(0, lo_out)
+    wait_leave(1, gm_out)
+    wait_leave(2, gi_out)
+    for n, (buf, out) in enumerate(((eu, eu_out), (ed, ed_out), (a1, a1_out), (a2, a2_out))):
+        collect(n, buf, out)
+        scatter(n, buf, out, finish_send)
+    keep_gain.wait()
+
+    def gain_wait(s):
+        gain_copy(s + 1).wait_send()
+        who = lax.rem(lin + s + 1, n_all)
+        remote(g_send.at[0], g_out.at[who], g_ssem.at[0], g_rsem.at[who], diag).wait_recv()
+
+    each(n_all - 1, gain_wait)
+
+    @pl.when(swaps)
+    def _():
+        for n in range(10):
+            bring(n, theirs)[0]().wait_send()
+
+    for n, buf in enumerate((x, mem, cot)):
+        share(n, buf).wait_send()
+
+    @pl.when(stays)
+    def _():
+        share_starts().wait_send()
+
+    for e in range(4):
+        each(BLOCKS, lambda i: exchange(e, i).wait_send())
+    for e in range(3):
+        each(2, lambda i: half_exchange(e, i).wait_send())
+
+
+def paired_layer(n_dp, lens, expert, gains, *arrays):
+    bf = lambda *shape: pltpu.VMEM(shape, BF16)
+    fl = lambda *shape: pltpu.VMEM(shape, F32)
+    dma = lambda *shape: pltpu.SemaphoreType.DMA(shape)
+    tokens = bf(LEN, WIDTH)
+    heads = bf(LEN, COLS)
+    turned = bf(COLS, LEN)
+    grads = bf(WIDTH, HIDDEN)
+    shares = jax.ShapeDtypeStruct((n_dp, 32, HIDDEN), BF16)
+    half = jax.ShapeDtypeStruct((HALF, WIDTH), BF16)
+    any_place = pl.BlockSpec(memory_space=pl.ANY)
+    return pl.pallas_call(
+        partial(layer_kernel, n_dp),
+        out_shape=(half, half, half, shares, shares, shares, shares,
+                   jax.ShapeDtypeStruct((2 * n_dp, 8, 128), F32)),
+        in_specs=[pl.BlockSpec(memory_space=pltpu.SMEM)] * 2 + [pl.BlockSpec(memory_space=pltpu.VMEM)] + [any_place] * 10,
+        out_specs=(any_place,) * 8,
+        scratch_shapes=[
+            tokens, tokens, tokens, bf(3, WIDTH, COLS), bf(COLS, WIDTH), bf(WIDTH, COLS), bf(2, WIDTH, COLS),
+            bf(COLS, WIDTH), bf(WIDTH, HIDDEN), bf(HIDDEN, WIDTH), pltpu.VMEM((8, LEN), jnp.int32),
+            fl(LEN, WIDTH), fl(LEN, WIDTH), fl(LEN, WIDTH), tokens, tokens, tokens,
+            heads, heads, heads, heads, heads, heads, turned, turned, turned, turned, turned, turned,
+            fl(8, LEN), fl(8, LEN), fl(8, LEN),
+            tokens, heads, fl(COLS, LEN), heads, heads, heads, bf(LEN, HIDDEN), bf(LEN, HIDDEN), bf(WIDTH, LEN),
+            grads, grads, grads, grads,
+            bf(4, LEN, WIDTH), bf(4, LEN, WIDTH), bf(3, HALF, WIDTH), bf(3, HALF, WIDTH), bf(3, HALF, WIDTH),
+            fl(LEN, WIDTH), fl(8, WIDTH), fl(n_dp, 8, 128),
+            dma(10), dma(10), dma(4), dma(4), dma(4, 4), dma(4, 4), dma(3, 2), dma(3, 2),
+            dma(4, n_dp), dma(4, n_dp), dma(2 * n_dp), dma(2 * n_dp), dma(3), dma(3),
+        ],
+        compiler_params=pltpu.CompilerParams(
+            collective_id=0, has_side_effects=True, vmem_limit_bytes=VMEM_BYTES),
+        cost_estimate=pl.CostEstimate(flops=20 * 10**9, bytes_accessed=20 * 2**20, transcendentals=0),
+    )(lens, expert, gains, *arrays)
+
+
+VMEM_BYTES = 63 * 2**20
+
+
+def per_device_paired(
+    layer_input, memory, seg_lengths, expert_ids, ln_gains, w_qkv, w_out_self, w_query_cross, w_kv_cross,
+    w_out_cross, w_up, w_down, cotangent,
+):
+    n_dp = lax.axis_size("dp")
+    experts = w_up.shape[0]
+    outs = paired_layer(
+        n_dp, seg_lengths, expert_ids, ln_gains,
+        layer_input[0], memory[0], cotangent[0], w_qkv, w_out_self, w_query_cross, w_kv_cross, w_out_cross,
+        expert_rows(w_up, expert_ids[0, 0]), expert_rows(w_down, expert_ids[0, 0]),
+    )
+    layer_output, grad_input, grad_memory, up_rows, down_rows, cross_rows, self_rows, gain_rows = outs
+    served = gain_rows[0::2, 3, 0].astype(jnp.int32)
+    order = jnp.argmax(
+        (served[None, :] == jnp.arange(experts, dtype=jnp.int32)[:, None]).astype(jnp.int32), axis=1)
+    grad_up = jnp.take(up_rows, order, axis=0).astype(F32)
+    grad_down = jnp.swapaxes(jnp.take(down_rows, order, axis=0).astype(F32), 1, 2)
+    cross = jnp.sum(cross_rows.astype(F32), axis=0)
+    own = jnp.sum(self_rows.astype(F32), axis=0)
+    gain_share = jnp.sum(gain_rows, axis=0)[:3, :32]
+    return (
+        layer_output[None],
+        grad_input.astype(F32)[None],
+        grad_memory.astype(F32)[None],
+        gain_share,
+        jnp.stack([own[:, 256:512], own[:, 512:768], own[:, 768:1024]]),
+        own[:, 0:256].T,
+        cross[:, 256:512],
+        jnp.stack([cross[:, 512:768], cross[:, 768:1024]]),
+        cross[:, 0:256].T,
+        grad_up,
+        grad_down,
+    )
+
+
+def fits_pairs(mesh, layer_input, seg_lengths, w_up):
+    return (
+        mesh.shape["tp"] == 2
+        and mesh.shape["dp"] == 16
+        and layer_input.shape == (mesh.shape["dp"], LEN, WIDTH)
+        and w_up.shape == (mesh.shape["dp"], WIDTH, 2 * HIDDEN)
+    )
+
+
 def solution(mesh):
     in_specs = (
         P("dp", "tp", None),
@@ -408,6 +1095,13 @@
         P(None, "dp", "tp"),
         P(None, "tp", "dp"),
     )
-    return jax.shard_map(
-        per_device, mesh=mesh, in_specs=in_specs, out_specs=out_specs, check_vma=False
-    )
+
+    def run(*args):
+        layer_input, seg_lengths, w_up = args[0], args[2], args[10]
+        paired = fits_pairs(mesh, layer_input, seg_lengths, w_up)
+        return jax.shard_map(
+            per_device_paired if paired else per_device,
+            mesh=mesh, in_specs=in_specs, out_specs=out_specs, check_vma=False,
+        )(*args)
+
+    return run

time: 1360 us -> 202 us (0.15)
  waiting for transfers between devices: 964 us -> 0 us
  matrix products: 223 us -> 0 us
  Pallas kernels: 0 us -> 181 us
  other arithmetic: 84.1 us -> 10.1 us
  blocking collectives: 39.4 us -> 0 us
  between operations: 16.5 us -> 1.36 us
    reduce_scatter x14 -> x0, waiting for transfers between devices: 669 us -> none  [the longest x1 179 us: per_device(): lax.psum_scatter(grad_down.astype(jnp.bfloat16), 'dp', scatter_dimension=...]
    all_gather x11 -> x0, waiting for transfers between devices: 196 us -> none  [the longest x6 127 us: spread_tokens(): return lax.all_gather(normed, 'tp', axis=1, tiled=True)]
    dot_general x39 -> x0, matrix products: 190 us -> none  [the longest x2 26 us: attend_both(): jnp.einsum('qhd,khd->hqk', grad_heads, value_rows, preferred_element_type...]
    pallas_call x0 -> x1, Pallas kernels: none -> 181 us  [paired_layer(): pl.pallas_call(partial(layer_kernel, n_dp), out_shape=(half, half, half,...]
    unnamed x27 -> x0, waiting for transfers between devices: 99.2 us -> none
    convert_element_type x20 -> x1, other arithmetic: 57.9 us -> 1.31 us  [per_device_paired(): served = gain_rows[0::2, 3, 0].astype(jnp.int32)]
    psum x1 -> x0, blocking collectives: 39.4 us -> none  [per_device(): lax.psum(jnp.stack([gain_self, gain_cross, gain_ffn]), ('dp', 'tp'))]
    sub x4 -> x0, matrix products: 33.7 us -> none  [softmax_rows(): weights = jnp.exp(scores - row_max)]
  transfers between devices with their start and end apart: 26 -> 0, of which waited for: 24 -> 0; matrix products, arithmetic and copies ran while one was open for 11% -> 0% of each run, Pallas kernels for 0% -> 0%
where the time goes in v1:
time: 202 us
  Pallas kernels  181 us (90%)
  other arithmetic  10.1 us (5%)
  local copies, waits for them, and re-layouts  9.63 us (5%)
    pallas_call x1, Pallas kernels, paired_layer(): pl.pallas_call(partial(layer_kernel, n_dp), out_shape=(half, half, half,...  181 us
    squeeze x2, local copies, waits for them, and re-layouts, expert_rows(): return lax.dynamic_index_in_dim(weights, expert, 0, keepdims=False)  4.53 us

profile of v1, /device:TPU:0, one launch (start us, length us, event | category | flops | bytes accessed | tf_op | source)
XLA Modules:
  0.0 202.1 jit_solution(5529656836507206600)
XLA Ops:
  1.3 2.3 %dynamic-slice_bitcast_fusion.1.up_in = bf16[512,1024]{1,0:T(8,128)(2,1)} fusion(bf16[16,512,1024]{2,1,0:T(8,128)(2,1)} %param.25, s32[]{:T(128)S(6)} %select_n.17), kind=kLoop, calls=%fused_computation.7 | loop fusion | bytes 2097156 | tf_op jit(solution)/shard_map/jit(dynamic_index_in_dim)/squeeze | solution.py:225
  3.6 2.3 %dynamic-slice_bitcast_fusion.down_in = bf16[1024,512]{1,0:T(8,128)(2,1)} fusion(bf16[16,1024,512]{2,1,0:T(8,128)(2,1)} %param.26, s32[]{:T(128)S(6)} %select_n.17), kind=kLoop, calls=%fused_computation.6 | loop fusion | bytes 2097156 | tf_op jit(solution)/shard_map/jit(dynamic_index_in_dim)/squeeze | solution.py:225
  5.8 181.0 %shard_map.212 = (bf16[512,512]{1,0:T(8,128)(2,1)}, bf16[512,512]{1,0:T(8,128)(2,1)}, bf16[512,512]{1,0:T(8,128)(2,1)}, bf16[16,32,1024]{2,1,0:T(8,128)(2,1)}, b...) custom-call(s32[1,16]{1,0:T(1,128)} %lens.1, ...), custom_call_target="tpu_custom_call" | custom-call | flops 20000000000 | bytes 20971520 | tf_op jit(solution)/shard_map/pallas_call | solution.py:997
  186.9 0.0 copy-start
  186.9 1.3 convert_reduce_fusion.2
  188.2 0.9 reduce_sum.27
  189.1 0.6 slice.30
  189.7 0.6 iota_reduce_fusion
  190.4 1.8 gather_fusion.1
  192.2 0.0 copy-done
  192.2 0.6 gather_fusion
  192.9 1.9 convert_reduce_fusion
  194.8 0.6 slice_bitcast_fusion
  195.4 0.6 pad_maximum_fusion.1
  196.1 0.6 slice_bitcast_fusion.3
  196.7 0.6 pad_maximum_fusion
  197.3 0.0 copy-start.2
  197.3 0.0 copy-start.3
  197.3 2.4 %convert_bitcast_fusion = (f32[16,1024,32]{1,2,0:T(8,128)}, f32[16,32,1024]{2,1,0:T(8,128)}) fusion(bf16[16,32,1024]{2,1,0:T(8,128)(2,1)S(1)} %gather_fusion.1, pred[16]{0:T(512)(128)(4,1)S(1)} %compare_and_fusion, bf16[16,32,1024]{2,1,0:T(8,128)(2,1)S(1)} %gather_fusion), kind=kLoop, calls=%fused_computation.2 | loop fusion | flops 2097152 | bytes 6291472 | tf_op jit(solution)/shard_map/transpose | solution.py:1041
  199.7 0.0 copy-start.1
  199.7 0.0 copy-done.2
  199.7 0.0 copy-done.3
  199.7 1.6 bitcast_convert_fusion
  201.3 0.0 copy-done.1
  201.3 0.8 copy.26
  (3 shorter events, 0.0 us)
Async XLA Ops:
  186.9 5.4 %copy-start = (bf16[16,32,1024]{2,1,0:T(8,128)(2,1)S(1)}, bf16[16,32,1024]{2,1,0:T(8,128)(2,1)}, u32[]{:S(2)}) copy-start(bf16[16,32,1024]{2,1,0:T(8,128)(2,1)} %get-tuple-element.27) | copy-start | bytes 3145732
  197.3 2.4 %copy-start.2 = (bf16[512,512]{1,0:T(8,128)(2,1)S(1)}, bf16[512,512]{1,0:T(8,128)(2,1)}, u32[]{:S(2)}) copy-start(bf16[512,512]{1,0:T(8,128)(2,1)} %get-tuple-element.22) | copy-start | bytes 1572868
  197.3 2.4 %copy-start.3 = (bf16[512,512]{1,0:T(8,128)(2,1)S(1)}, bf16[512,512]{1,0:T(8,128)(2,1)}, u32[]{:S(2)}) copy-start(bf16[512,512]{1,0:T(8,128)(2,1)} %get-tuple-element.23) | copy-start | bytes 1572868
  199.7 1.6 copy-start.1

commit v2 on v1

--- a/solution.py
+++ b/solution.py
@@ -392,6 +392,8 @@
 
 LEN, WIDTH, COLS, HIDDEN, BLOCK, HALF = 1024, 512, 256, 1024, 256, 512
 BLOCKS = LEN // BLOCK
+TILE = 256
+TILES = HIDDEN // TILE
 
 
 def dot(left, right, dims=NN):
@@ -491,12 +493,13 @@
 def layer_kernel(
     n_dp,
     lens, expert, gains, x_in, mem_in, cot_in, wqkv_in, wos_in, wq_in, wkv_in, woc_in, up_in, down_in,
-    lo_out, gi_out, gm_out, eu_out, ed_out, a1_out, a2_out, g_out,
+    lo_out, gi_out, gm_out, e_out, a1_out, a2_out, g_out,
     x, mem, cot, wqkv, wos, wq, wkv, woc, up, down, starts,
     s1, s2, gs, n0, n1, n2, q0, k0, v0, q1, k1, v1, kt0, vt0, kt1, vt1, ht0, ht1, lse0, lse1, inner,
-    gb, gh, dqt, dq, dk, dv, hid, gpre, nt, eu, ed, a1, a2,
+    gb, gh, dqt, dq, dk, dv, hid, gpre, nt, cot_t, eb, a1, a2, r1, r2,
     snd, rcv, sndh, rcvh, leaving, half_out, gain_sum, g_send,
-    y_send, y_recv, c_send, c_recv, x_send, x_recv, h_send, h_recv, sc_send, sc_recv, g_ssem, g_rsem, o_send, o_recv,
+    y_send, y_recv, w_send, w_recv, c_send, c_recv, x_send, x_recv, h_send, h_recv,
+    e_send, e_recv, p_send, p_recv, a_send, a_recv, g_ssem, g_rsem, o_send, o_recv,
 ):
     d, t = lax.axis_index("dp"), lax.axis_index("tp")
     c = lax.rem(d, 2)
@@ -517,15 +520,20 @@
     other = pl.ds(pl.multiple_of((1 - c) * HALF, HALF), HALF)
     theirs = pl.ds(pl.multiple_of(t * HALF, HALF), HALF)
 
-    brought = [
-        (x_in, lambda p: x.at[p]), (wqkv_in, wqkv), (wos_in, wos), (mem_in, lambda p: mem.at[p]), (wq_in, wq),
-        (wkv_in, wkv), (woc_in, woc), (up_in, up), (down_in, down), (cot_in, lambda p: cot.at[p]),
-    ]
-    X, WQKV, WOS, MEM, WQ, WKV, WOC, UP, DOWN, COT = range(10)
+    X, MEM, COT, UP, DOWN = 0, 1, 2, 3, 3 + TILES
+    n_brought = 3 + 2 * TILES
+
+    def tile(f):
+        return pl.ds(pl.multiple_of(f * TILE, TILE), TILE)
 
     def bring(n, place):
-        src, dst = brought[n]
-        dst = dst(place) if callable(dst) else dst
+        if n < UP:
+            src, dst = ((x_in, x), (mem_in, mem), (cot_in, cot))[n]
+            dst = dst.at[place]
+        elif n < DOWN:
+            src, dst = up_in.at[:, tile(n - UP)], up.at[:, tile(n - UP)]
+        else:
+            src, dst = down_in.at[tile(n - DOWN)], down.at[tile(n - DOWN)]
         return (lambda: remote(src, dst, y_send.at[n], y_recv.at[n], diag),
                 lambda: pltpu.make_async_copy(src, dst, y_recv.at[n]))
 
@@ -560,8 +568,66 @@
     def share_starts():
         return remote(starts, starts, c_send.at[3], c_recv.at[3], sib)
 
-    for n in (X, WQKV, MEM, COT, WOS, WQ, WKV, WOC, UP, DOWN):
-        start_near(n)
+    n_pairs = n_dp // 2
+    pair = lax.div(d, 2)
+    halves = [(wqkv_in, wqkv), (wos_in, wos), (wq_in, wq), (wkv_in, wkv), (woc_in, woc)]
+    WQKV, WOS, WQ, WKV, WOC = range(5)
+
+    def piece(ref, p):
+        if len(ref.shape) == 3:
+            rows = ref.shape[1] // n_pairs
+            return ref.at[:, pl.ds(pl.multiple_of(p * rows, rows), rows)]
+        rows = ref.shape[0] // n_pairs
+        return ref.at[pl.ds(pl.multiple_of(p * rows, rows), rows)]
+
+    def first_piece(n):
+        src, dst = halves[n]
+        return remote(piece(src, pair), piece(dst, pair), w_send.at[n, 0], w_recv.at[n, pair], diag)
+
+    def hand_piece(n, s):
+        dst = halves[n][1]
+        to = lax.rem(pair + s, n_pairs)
+        return remote(piece(dst, pair), piece(dst, pair), w_send.at[n, s], w_recv.at[n, pair], (2 * to + c, t))
+
+    def near_weight(n):
+        src, dst = halves[n]
+        return pltpu.make_async_copy(src, dst, w_recv.at[n, 0])
+
+    def hand_round(n):
+        first_piece(n).wait_recv()
+        each(n_pairs - 1, lambda s: hand_piece(n, s + 1).start())
+
+    def wait_weight(n):
+        @pl.when(swaps)
+        def _():
+            def one(s):
+                dst = halves[n][1]
+                p = lax.rem(pair + s + 1, n_pairs)
+                remote(piece(dst, p), piece(dst, p), w_send.at[n, 0], w_recv.at[n, p], diag).wait_recv()
+
+            each(n_pairs - 1, one)
+
+        @pl.when(stays)
+        def _():
+            near_weight(n).wait()
+
+    start_near(X)
+
+    @pl.when(stays)
+    def _():
+        near_weight(WQKV).start()
+
+    start_near(MEM)
+    start_near(COT)
+
+    @pl.when(stays)
+    def _():
+        for n in (WOS, WKV, WQ, WOC):
+            near_weight(n).start()
+
+    for f in range(TILES):
+        start_near(UP + f)
+        start_near(DOWN + f)
     barrier = pltpu.get_barrier_semaphore()
 
     def greet(i):
@@ -580,8 +646,27 @@
         starts[...] = level
 
     pl.semaphore_wait(barrier, n_all - 1)
-    for n in range(10):
-        start_bring(n)
+
+    @pl.when(swaps)
+    def _():
+        first_piece(WQKV).start()
+
+    start_bring(X)
+
+    @pl.when(swaps)
+    def _():
+        for n in (WOS, WKV, WQ, WOC):
+            first_piece(n).start()
+
+    start_bring(MEM)
+    start_bring(COT)
+    for f in range(TILES):
+        start_bring(UP + f)
+        start_bring(DOWN + f)
+
+    @pl.when(swaps)
+    def _():
+        hand_round(WQKV)
 
     @pl.when(stays)
     def _():
@@ -620,7 +705,12 @@
         k0[r, :] = dot(nn, wqkv[1]).astype(BF16)
         v0[r, :] = dot(nn, wqkv[2]).astype(BF16)
 
-    wait_bring(WQKV)
+    @pl.when(swaps)
+    def _():
+        for n in (WOS, WKV, WQ, WOC):
+            hand_round(n)
+
+    wait_weight(WQKV)
     each(2, lambda i: self_project(c * 2 + i))
     share(0, x).wait_recv()
     each(2, lambda i: self_project((1 - c) * 2 + i))
@@ -631,7 +721,7 @@
     def _():
         share_starts().wait_recv()
 
-    wait_bring(WOS)
+    wait_weight(WOS)
 
     def exchange(e, i):
         r = block_rows(i)
@@ -661,7 +751,7 @@
     def _():
         share(1, mem).start()
 
-    wait_bring(WKV)
+    wait_weight(WKV)
 
     def memory_project(i):
         r = block_rows(i)
@@ -673,8 +763,8 @@
     each(2, lambda i: memory_project((1 - c) * 2 + i))
     kt1[...] = k1[...].T
     vt1[...] = v1[...].T
-    wait_bring(WQ)
-    wait_bring(WOC)
+    wait_weight(WQ)
+    wait_weight(WOC)
 
     def cross_block(i):
         r = block_rows(i)
@@ -691,36 +781,95 @@
 
     each(BLOCKS, cross_block)
 
-    wait_bring(UP)
-    wait_bring(DOWN)
     wait_swapped(COT)
 
     @pl.when(swaps)
     def _():
         share(2, cot).start()
 
-    share(2, cot).wait_recv()
-
     def half_exchange(e, i):
         r = block_rows(i)
         return remote(sndh.at[e, r], rcvh.at[e, r], h_send.at[e, i], h_recv.at[e, i], sib)
 
-    def expert_block(i):
+    def expert_norm(i):
         r = block_rows(i)
         exchange(1, i).wait_recv()
         state = s1[r, :] + (snd[1, r, :].astype(F32) + rcv[1, r, :].astype(F32))
         s2[r, :] = state
         xhat, _ = normalise(state)
-        nn = (xhat * gains[2:3, :]).astype(BF16)
-        n2[r, :] = nn
-        for f in range(2):
-            cols = slice(f * 512, f * 512 + 512)
-            pre = dot(nn, up[:, cols])
-            phi, slope = gelu_parts(pre)
+        n2[r, :] = (xhat * gains[2:3, :]).astype(BF16)
+
+    each(BLOCKS, expert_norm)
+    nt[...] = n2[...].T
+    share(2, cot).wait_recv()
+    cot_t[...] = cot[...].T
+
+    def begin(copy):
+        copy.start()
+
+    def finish_send(copy):
+        copy.wait_send()
+
+    def share_rows(ref, to):
+        return ref.at[pl.ds(pl.multiple_of(to * 32, 32), 32)]
+
+    def scatter(f, action):
+        src, dst = eb.at[f], e_out.at[row, f]
+
+        @pl.when(stays)
+        def _():
+            if action is begin:
+                pltpu.make_async_copy(share_rows(src, d), dst, e_recv.at[f, row]).start()
+
+        @pl.when(swaps)
+        def _():
+            action(remote(share_rows(src, d), dst, e_send.at[f, 0], e_recv.at[f, row], (d, c)))
+
+        def one(s):
+            to = lax.rem(d + s + 1, n_dp)
+            action(remote(share_rows(src, to), dst, e_send.at[f, s + 1], e_recv.at[f, row], (to, c)))
+
+        each(n_dp - 1, one)
+
+    def collect(f):
+        def one(i):
+            src, dst = eb.at[f, pl.ds(0, 32)], e_out.at[i, f]
+
+            @pl.when(stays & (i == row))
+            def _():
+                pltpu.make_async_copy(src, dst, e_recv.at[f, i]).wait()
+
+            @pl.when(jnp.logical_not(stays & (i == row)))
+            def _():
+                remote(src, dst, e_send.at[f, 0], e_recv.at[f, i], diag).wait_recv()
+
+        each(n_dp, one)
+
+    for f in range(TILES):
+        wait_bring(UP + f)
+        wait_bring(DOWN + f)
+        cols = tile(f)
+
+        def expert_block(i):
+            r = block_rows(i)
+            phi, slope = gelu_parts(pre := dot(n2[r, :], up[:, cols]))
             hid[r, cols] = (pre * phi).astype(BF16)
             gpre[r, cols] = (dot(cot[r, :], down[cols, :], NT) * slope).astype(BF16)
+
+        each(BLOCKS, expert_block)
+        eb[f, :, 0:TILE] = dot(nt[...], gpre[:, cols]).astype(BF16)
+        eb[f, :, TILE:2 * TILE] = dot(cot_t[...], hid[:, cols]).astype(BF16)
+        scatter(f, begin)
+
+    def expert_back(i):
+        r = block_rows(i)
         snd[2, r, :] = dot(gpre[r, :], up[...], NT).astype(BF16)
         exchange(2, i).start()
+
+    each(BLOCKS, expert_back)
+
+    def expert_out(i):
+        r = block_rows(i)
         part = dot(hid[r, :], down[...])
         mine = lax.div(i, 2) == c
         low = lax.rem(i, 2)
@@ -735,62 +884,7 @@
             sndh[0, rl, :] = part.astype(BF16)
             half_exchange(0, low).start()
 
-    each(BLOCKS, expert_block)
-
-    def scatter(n, buf, out, action):
-        def one(s):
-            to = lax.rem(d + s, n_dp)
-            src = buf.at[pl.ds(pl.multiple_of(to * 32, 32), 32)]
-            action(remote(src, out.at[row], sc_send.at[n, s], sc_recv.at[n, row], (to, c)))
-
-        src = buf.at[pl.ds(pl.multiple_of(d * 32, 32), 32)]
-
-        @pl.when(stays)
-        def _():
-            if action is begin:
-                pltpu.make_async_copy(src, out.at[row], sc_recv.at[n, row]).start()
-
-        @pl.when(swaps)
-        def _():
-            action(remote(src, out.at[row], sc_send.at[n, 0], sc_recv.at[n, row], (d, c)))
-
-        each(n_dp - 1, lambda s: one(s + 1))
-
-    def begin(copy):
-        copy.start()
-
-    def finish_send(copy):
-        copy.wait_send()
-
-    def collect(n, buf, out):
-        def one(i):
-            @pl.when(stays & (i == row))
-            def _():
-                pltpu.make_async_copy(buf.at[pl.ds(0, 32)], out.at[i], sc_recv.at[n, i]).wait()
-
-            @pl.when(jnp.logical_not(stays & (i == row)))
-            def _():
-                remote(buf.at[pl.ds(0, 32)], out.at[i], sc_send.at[n, 0], sc_recv.at[n, i], diag).wait_recv()
-
-        each(n_dp, one)
-
-    def quarter(i):
-        return pl.ds(pl.multiple_of(i * 256, 256), 256)
-
-    nt[...] = n2[...].T
-
-    def up_grads(i):
-        eu[:, quarter(i)] = dot(nt[...], gpre[:, quarter(i)]).astype(BF16)
-
-    each(HIDDEN // 256, up_grads)
-    scatter(0, eu, eu_out, begin)
-    nt[...] = cot[...].T
-
-    def down_grads(i):
-        ed[:, quarter(i)] = dot(nt[...], hid[:, quarter(i)]).astype(BF16)
-
-    each(HIDDEN // 256, down_grads)
-    scatter(1, ed, ed_out, begin)
+    each(BLOCKS, expert_out)
 
     gain_sum[...] = jnp.zeros_like(gain_sum)
 
@@ -850,7 +944,64 @@
     nt[...] = mem[...].T
     a1[:, 512:768] = dot(nt[...], dk[...]).astype(BF16)
     a1[:, 768:1024] = dot(nt[...], dv[...]).astype(BF16)
-    scatter(2, a1, a1_out, begin)
+
+    def over(n):
+        buf, place = ((a1, r1), (a2.at[0], r2.at[0]), (a2.at[1], r2.at[1]), (a2.at[2], r2.at[2]))[n]
+        return remote(buf, place, p_send.at[n], p_recv.at[n], (d, c))
+
+    def hand_over(n):
+        @pl.when(swaps)
+        def _():
+            over(n).start()
+
+    def hand_out(n):
+        if n == 0:
+            return a1, a1_out.at[pair]
+        return a2.at[n - 1], a2_out.at[pair, n - 1]
+
+    def owners(n, action):
+        src, dst = hand_out(n)
+
+        def one(s):
+            to = lax.rem(d + s + 1, n_dp)
+            action(remote(share_rows(src, to), dst, a_send.at[n, s + 1], a_recv.at[n, pair], (to, t)))
+
+        each(n_dp - 1, one)
+
+    def add_over(n):
+        @pl.when(stays)
+        def _():
+            over(n).wait_recv()
+            if n == 0:
+                a1[...] = (a1[...].astype(F32) + r1[...].astype(F32)).astype(BF16)
+            else:
+                a2[n - 1] = (a2[n - 1].astype(F32) + r2[n - 1].astype(F32)).astype(BF16)
+            src, dst = hand_out(n)
+            pltpu.make_async_copy(share_rows(src, d), dst, a_recv.at[n, pair]).start()
+            owners(n, begin)
+
+    def collect_over(n):
+        def one(i):
+            src = hand_out(n)[0].at[pl.ds(0, 32)]
+            dst = a1_out.at[i] if n == 0 else a2_out.at[i, n - 1]
+
+            @pl.when(stays & (i == pair))
+            def _():
+                pltpu.make_async_copy(src, dst, a_recv.at[n, i]).wait()
+
+            @pl.when(jnp.logical_not(stays & (i == pair)))
+            def _():
+                remote(src, dst, a_send.at[n, 0], a_recv.at[n, i], diag).wait_recv()
+
+        each(n_pairs, one)
+
+        @pl.when(stays)
+        def _():
+            owners(n, finish_send)
+
+        @pl.when(swaps)
+        def _():
+            over(n).wait_send()
 
     def leave(n, out):
         buf = leaving.at[n]
@@ -888,6 +1039,8 @@
         start_leave(n, (lo_out, gm_out)[n])
 
     each(BLOCKS, lambda i: branch_block(1, i, 3, s1, gs, ht0, wos))
+    a1[:, 1024:1280] = dot(ht0[...], gb[...]).T.astype(BF16)
+    hand_over(0)
     dqt[...] = jnp.zeros_like(dqt)
 
     def self_back(i):
@@ -900,13 +1053,6 @@
                       window_bias(768, 768, 256, 256, starts[0:1, 768:1024]))
     dq[...] = (dqt[...] * HEAD_DIM ** -0.5).astype(BF16).T
 
-    nt[...] = n0[...].T
-    a2[:, 0:256] = dot(ht0[...], gb[...]).T.astype(BF16)
-    a2[:, 256:512] = dot(nt[...], dq[...]).astype(BF16)
-    a2[:, 512:768] = dot(nt[...], dk[...]).astype(BF16)
-    a2[:, 768:1024] = dot(nt[...], dv[...]).astype(BF16)
-    scatter(3, a2, a2_out, begin)
-
     def input_grads(i):
         r = block_rows(i)
         return dot(dq[r, :], wqkv[0], NT) + dot(dk[r, :], wqkv[1], NT) + dot(dv[r, :], wqkv[2], NT)
@@ -917,6 +1063,11 @@
         half_exchange(2, low).start()
 
     each(2, input_send)
+    add_over(0)
+    nt[...] = n0[...].T
+    for n, grad in enumerate((dq, dk, dv)):
+        a2[n] = dot(nt[...], grad[...]).astype(BF16)
+        hand_over(n + 1)
 
     def input_keep(low):
         half_out[block_rows(low), :] = input_grads(c * 2 + low)
@@ -934,6 +1085,8 @@
 
     each(2, input_done)
     start_leave(2, gi_out)
+    for n in range(1, 4):
+        add_over(n)
 
     number = jnp.full((1, 128), expert[0, 0].astype(F32))
     for j in range(n_dp):
@@ -953,9 +1106,11 @@
     wait_leave(0, lo_out)
     wait_leave(1, gm_out)
     wait_leave(2, gi_out)
-    for n, (buf, out) in enumerate(((eu, eu_out), (ed, ed_out), (a1, a1_out), (a2, a2_out))):
-        collect(n, buf, out)
-        scatter(n, buf, out, finish_send)
+    for f in range(TILES):
+        collect(f)
+        scatter(f, finish_send)
+    for n in range(4):
+        collect_over(n)
     keep_gain.wait()
 
     def gain_wait(s):
@@ -967,8 +1122,11 @@
 
     @pl.when(swaps)
     def _():
-        for n in range(10):
+        for n in range(n_brought):
             bring(n, theirs)[0]().wait_send()
+        for n in range(5):
+            first_piece(n).wait_send()
+            each(n_pairs - 1, lambda s: hand_piece(n, s + 1).wait_send())
 
     for n, buf in enumerate((x, mem, cot)):
         share(n, buf).wait_send()
@@ -981,6 +1139,13 @@
         each(BLOCKS, lambda i: exchange(e, i).wait_send())
     for e in range(3):
         each(2, lambda i: half_exchange(e, i).wait_send())
+
+
+VMEM_BYTES = 63 * 2**20
+ANY_PLACE = pl.BlockSpec(memory_space=pl.ANY)
+IN_HBM = pl.BlockSpec(memory_space=pltpu.HBM)
+IN_SMEM = pl.BlockSpec(memory_space=pltpu.SMEM)
+IN_VMEM = pl.BlockSpec(memory_space=pltpu.VMEM)
 
 
 def paired_layer(n_dp, lens, expert, gains, *arrays):
@@ -990,16 +1155,17 @@
     tokens = bf(LEN, WIDTH)
     heads = bf(LEN, COLS)
     turned = bf(COLS, LEN)
-    grads = bf(WIDTH, HIDDEN)
-    shares = jax.ShapeDtypeStruct((n_dp, 32, HIDDEN), BF16)
     half = jax.ShapeDtypeStruct((HALF, WIDTH), BF16)
-    any_place = pl.BlockSpec(memory_space=pl.ANY)
+    n_pairs = n_dp // 2
     return pl.pallas_call(
         partial(layer_kernel, n_dp),
-        out_shape=(half, half, half, shares, shares, shares, shares,
+        out_shape=(half, half, half,
+                   jax.ShapeDtypeStruct((n_dp, TILES, 32, 2 * TILE), BF16),
+                   jax.ShapeDtypeStruct((n_pairs, 32, 5 * COLS), BF16),
+                   jax.ShapeDtypeStruct((n_pairs, 3, 32, COLS), BF16),
                    jax.ShapeDtypeStruct((2 * n_dp, 8, 128), F32)),
-        in_specs=[pl.BlockSpec(memory_space=pltpu.SMEM)] * 2 + [pl.BlockSpec(memory_space=pltpu.VMEM)] + [any_place] * 10,
-        out_specs=(any_place,) * 8,
+        in_specs=[IN_SMEM] * 2 + [IN_VMEM] + [ANY_PLACE] * 10,
+        out_specs=(ANY_PLACE,) * 7,
         scratch_shapes=[
             tokens, tokens, tokens, bf(3, WIDTH, COLS), bf(COLS, WIDTH), bf(WIDTH, COLS), bf(2, WIDTH, COLS),
             bf(COLS, WIDTH), bf(WIDTH, HIDDEN), bf(HIDDEN, WIDTH), pltpu.VMEM((8, LEN), jnp.int32),
@@ -1007,11 +1173,14 @@
             heads, heads, heads, heads, heads, heads, turned, turned, turned, turned, turned, turned,
             fl(8, LEN), fl(8, LEN), fl(8, LEN),
             tokens, heads, fl(COLS, LEN), heads, heads, heads, bf(LEN, HIDDEN), bf(LEN, HIDDEN), bf(WIDTH, LEN),
-            grads, grads, grads, grads,
+            bf(WIDTH, LEN), bf(TILES, WIDTH, 2 * TILE), bf(WIDTH, 5 * COLS), bf(3, WIDTH, COLS),
+            bf(WIDTH, 5 * COLS), bf(3, WIDTH, COLS),
             bf(4, LEN, WIDTH), bf(4, LEN, WIDTH), bf(3, HALF, WIDTH), bf(3, HALF, WIDTH), bf(3, HALF, WIDTH),
             fl(LEN, WIDTH), fl(8, WIDTH), fl(n_dp, 8, 128),
-            dma(10), dma(10), dma(4), dma(4), dma(4, 4), dma(4, 4), dma(3, 2), dma(3, 2),
-            dma(4, n_dp), dma(4, n_dp), dma(2 * n_dp), dma(2 * n_dp), dma(3), dma(3),
+            dma(3 + 2 * TILES), dma(3 + 2 * TILES), dma(5, n_pairs), dma(5, n_pairs), dma(4), dma(4),
+            dma(4, 4), dma(4, 4), dma(3, 2), dma(3, 2),
+            dma(TILES, n_dp), dma(TILES, n_dp), dma(4), dma(4), dma(4, n_dp), dma(4, n_pairs),
+            dma(2 * n_dp), dma(2 * n_dp), dma(3), dma(3),
         ],
         compiler_params=pltpu.CompilerParams(
             collective_id=0, has_side_effects=True, vmem_limit_bytes=VMEM_BYTES),
@@ -1019,7 +1188,102 @@
     )(lens, expert, gains, *arrays)
 
 
-VMEM_BYTES = 63 * 2**20
+def choose_kernel(expert, up_in, down_in, up_out, down_out, sems):
+    e = expert[0, 0]
+    parts = 4
+    copies = []
+    for p in range(parts):
+        for n, (src, dst) in enumerate(((up_in, up_out), (down_in, down_out))):
+            rows = dst.shape[0] // parts
+            at = pl.ds(p * rows, rows)
+            copies.append(pltpu.make_async_copy(src.at[e, at], dst.at[at], sems.at[n, p]))
+    for copy in copies:
+        copy.start()
+    for copy in copies:
+        copy.wait()
+
+
+def choose_expert(expert, w_up, w_down):
+    return pl.pallas_call(
+        choose_kernel,
+        out_shape=(jax.ShapeDtypeStruct(w_up.shape[1:], BF16), jax.ShapeDtypeStruct(w_down.shape[1:], BF16)),
+        in_specs=[IN_SMEM, ANY_PLACE, ANY_PLACE],
+        out_specs=(IN_VMEM, IN_VMEM),
+        scratch_shapes=[pltpu.SemaphoreType.DMA((2, 4))],
+        compiler_params=pltpu.CompilerParams(vmem_limit_bytes=VMEM_BYTES),
+    )(expert, w_up, w_down)
+
+
+def place_kernel(
+    gains_any, e_any, a1_any, a2_any, gi_any, gm_any, lo_any,
+    lo_out, gi_out, gm_out, gain_out, qkv_out, os_out, q_out, kv_out, oc_out, up_out, down_out,
+    ids, gains_in, e_in, a1_in, a2_in, gi_in, gm_in, lo_in, gi_v, gm_v, ups, downs, in_sems, e_sems, up_sems, down_sems, out_sems,
+):
+    rows = e_in.shape[0]
+    number = pltpu.make_async_copy(gains_any, ids, in_sems.at[0])
+    number.start()
+    blocks = [pltpu.make_async_copy(e_any.at[r], e_in.at[r], e_sems.at[r]) for r in range(rows)]
+    for copy in blocks:
+        copy.start()
+    pairs = ((lo_any, lo_in), (gi_any, gi_in), (gm_any, gm_in), (gains_any, gains_in), (a1_any, a1_in), (a2_any, a2_in))
+    reads = [pltpu.make_async_copy(src, dst, in_sems.at[1 + n]) for n, (src, dst) in enumerate(pairs)]
+    for copy in reads:
+        copy.start()
+    number.wait()
+    writes = []
+
+    def write(src, dst, sem):
+        writes.append(pltpu.make_async_copy(src, dst, sem))
+        writes[-1].start()
+
+    for r in range(rows):
+        blocks[r].wait()
+        for f in range(TILES):
+            ups[r, :, f * TILE:(f + 1) * TILE] = e_in[r, f, :, 0:TILE].astype(F32)
+            downs[r, :, f * TILE:(f + 1) * TILE] = e_in[r, f, :, TILE:2 * TILE].astype(F32)
+        e = ids[2 * r, 3, 0].astype(jnp.int32)
+        write(ups.at[r], up_out.at[e], up_sems.at[r])
+        write(downs.at[r], down_out.at[e], down_sems.at[r])
+    reads[0].wait()
+    write(lo_in, lo_out, out_sems.at[2])
+    reads[1].wait()
+    gi_v[...] = gi_in[...].astype(F32)
+    write(gi_v, gi_out, out_sems.at[0])
+    reads[2].wait()
+    gm_v[...] = gm_in[...].astype(F32)
+    write(gm_v, gm_out, out_sems.at[1])
+    for copy in reads[3:]:
+        copy.wait()
+    gain_out[...] = jnp.sum(gains_in[...], axis=0)[:3, :32]
+    first = jnp.sum(a1_in[...].astype(F32), axis=0)
+    oc_out[...] = first[:, 0:COLS]
+    q_out[...] = first[:, COLS:2 * COLS]
+    kv_out[0] = first[:, 2 * COLS:3 * COLS]
+    kv_out[1] = first[:, 3 * COLS:4 * COLS]
+    os_out[...] = first[:, 4 * COLS:5 * COLS]
+    qkv_out[...] = jnp.sum(a2_in[...].astype(F32), axis=0)
+    for copy in writes:
+        copy.wait()
+
+
+def place_grads(experts, *arrays):
+    shape = lambda *dims: jax.ShapeDtypeStruct(dims, F32)
+    like = lambda array: pltpu.VMEM(array.shape, array.dtype)
+    dma = lambda *dims: pltpu.SemaphoreType.DMA(dims)
+    rows = arrays[1].shape[0]
+    staged = pltpu.VMEM((rows, 32, HIDDEN), F32)
+    half = pltpu.VMEM((HALF, WIDTH), F32)
+    return pl.pallas_call(
+        place_kernel,
+        out_shape=(jax.ShapeDtypeStruct((HALF, WIDTH), BF16), shape(HALF, WIDTH), shape(HALF, WIDTH), shape(3, 32), shape(3, 32, COLS), shape(32, COLS),
+                   shape(32, COLS), shape(2, 32, COLS), shape(32, COLS),
+                   shape(experts, 32, HIDDEN), shape(experts, 32, HIDDEN)),
+        in_specs=[IN_HBM] * 7,
+        out_specs=(IN_HBM,) * 3 + (IN_VMEM,) * 6 + (IN_HBM,) * 2,
+        scratch_shapes=[pltpu.SMEM(arrays[0].shape, F32)] + [like(array) for array in arrays] + [
+            half, half, staged, staged, dma(7), dma(rows), dma(rows), dma(rows), dma(3)],
+        compiler_params=pltpu.CompilerParams(vmem_limit_bytes=VMEM_BYTES),
+    )(*arrays)
 
 
 def per_device_paired(
@@ -1027,33 +1291,16 @@
     w_out_cross, w_up, w_down, cotangent,
 ):
     n_dp = lax.axis_size("dp")
-    experts = w_up.shape[0]
-    outs = paired_layer(
+    up, down = choose_expert(expert_ids, w_up, w_down)
+    layer_output, grad_input, grad_memory, e_rows, a1_rows, a2_rows, gain_rows = paired_layer(
         n_dp, seg_lengths, expert_ids, ln_gains,
-        layer_input[0], memory[0], cotangent[0], w_qkv, w_out_self, w_query_cross, w_kv_cross, w_out_cross,
-        expert_rows(w_up, expert_ids[0, 0]), expert_rows(w_down, expert_ids[0, 0]),
-    )
-    layer_output, grad_input, grad_memory, up_rows, down_rows, cross_rows, self_rows, gain_rows = outs
-    served = gain_rows[0::2, 3, 0].astype(jnp.int32)
-    order = jnp.argmax(
-        (served[None, :] == jnp.arange(experts, dtype=jnp.int32)[:, None]).astype(jnp.int32), axis=1)
-    grad_up = jnp.take(up_rows, order, axis=0).astype(F32)
-    grad_down = jnp.swapaxes(jnp.take(down_rows, order, axis=0).astype(F32), 1, 2)
-    cross = jnp.sum(cross_rows.astype(F32), axis=0)
-    own = jnp.sum(self_rows.astype(F32), axis=0)
-    gain_share = jnp.sum(gain_rows, axis=0)[:3, :32]
+        layer_input[0], memory[0], cotangent[0], w_qkv, w_out_self, w_query_cross, w_kv_cross, w_out_cross, up, down,
+    )
+    layer_output, grad_input, grad_memory, gain_share, qkv, out_self, query, key_value, out_cross, grad_up, grad_down = place_grads(
+        w_up.shape[0], gain_rows, e_rows, a1_rows, a2_rows, grad_input, grad_memory, layer_output)
     return (
-        layer_output[None],
-        grad_input.astype(F32)[None],
-        grad_memory.astype(F32)[None],
-        gain_share,
-        jnp.stack([own[:, 256:512], own[:, 512:768], own[:, 768:1024]]),
-        own[:, 0:256].T,
-        cross[:, 256:512],
-        jnp.stack([cross[:, 512:768], cross[:, 768:1024]]),
-        cross[:, 0:256].T,
-        grad_up,
-        grad_down,
+        layer_output[None], grad_input[None], grad_memory[None], gain_share, qkv, out_self.T, query, key_value,
+        out_cross.T, grad_up, jnp.swapaxes(grad_down, 1, 2),
     )
 
 

time: 202 us -> 164 us (0.81)
  Pallas kernels: 181 us -> 161 us
  other arithmetic: 10.1 us -> 0 us
  local copies, waits for them, and re-layouts: 9.63 us -> 0 us
    pallas_call x1, Pallas kernels: 181 us -> 152 us  [paired_layer(): pl.pallas_call(partial(layer_kernel, n_dp), out_shape=(half, half, half,...]
    pallas_call x0 -> x2, Pallas kernels: none -> 9.89 us  [the longest x1 7 us: place_grads(): pl.pallas_call(place_kernel, out_shape=(jax.ShapeDtypeStruct((HALF, WIDTH...]
    squeeze x2 -> x0, local copies, waits for them, and re-layouts: 4.53 us -> none  [expert_rows(): return lax.dynamic_index_in_dim(weights, expert, 0, keepdims=False)]
    reduce_sum x2 -> x0, other arithmetic: 2.88 us -> none  [the longest x1 1.93 us: per_device_paired(): cross = jnp.sum(cross_rows.astype(F32), axis=0)]
    gather x2 -> x0, local copies, waits for them, and re-layouts: 2.45 us -> none  [the longest x1 1.84 us: per_device_paired(): jnp.take(down_rows, order, axis=0).astype(F32)]
    transpose x1 -> x0, other arithmetic: 2.35 us -> none  [per_device_paired(): jnp.swapaxes(jnp.take(down_rows, order, axis=0).astype(F32), 1, 2)]
where the time goes in v2:
time: 164 us; the launch traced here: 163 us
  Pallas kernels  161 us (98%)
    pallas_call x1, Pallas kernels, paired_layer(): pl.pallas_call(partial(layer_kernel, n_dp), out_shape=(half, half, half,...  152 us
    pallas_call x1, Pallas kernels, place_grads(): pl.pallas_call(place_kernel, out_shape=(jax.ShapeDtypeStruct((HALF, WIDTH...  7 us

profile of v2, /device:TPU:0, one launch (start us, length us, event | category | flops | bytes accessed | tf_op | source)
XLA Modules:
  0.0 162.9 jit_solution(17594567099376432677)
XLA Ops:
  1.3 2.9 %shard_map.212 = (bf16[512,1024]{1,0:T(8,128)(2,1)}, bf16[1024,512]{1,0:T(8,128)(2,1)}) custom-call(s32[1,1]{1,0:T(1,128)S(6)} %copy.24.expert, bf16[16,512,1024]{2,1,0:T(8,128)(2,1)} %up_in.1, bf16[16,1024,512]{2,1,0:T(8,128)(2,1)} %down_in.1), custom_call_target="tpu_custom_call" | custom-call | tf_op jit(solution)/shard_map/pallas_call | solution.py:1207
  4.2 151.6 %shard_map.213 = (bf16[512,512]{1,0:T(8,128)(2,1)}, bf16[512,512]{1,0:T(8,128)(2,1)}, bf16[512,512]{1,0:T(8,128)(2,1)}, bf16[16,4,32,512]{3,2,1,0:T(8,128)(2,1)}...) custom-call(s32[1,16]{1,0:T(1,128)} %lens.1, s32[1,1]{1,0:T(1,128)S(6)} %copy.24.expert, ...), custom_call_target="tpu_custom_call" | custom-call | flops 20000000000 | bytes 20971520 | tf_op jit(solution)/shard_map/pallas_call | solution.py:1160
  155.7 7.0 %shard_map.214 = (bf16[512,512]{1,0:T(8,128)(2,1)}, f32[512,512]{1,0:T(8,128)}, f32[512,512]{1,0:T(8,128)}, f32[3,32]{1,0:T(4,128)}, f32[3,32,256]{2,1,0:T(8,128...) custom-call(f32[32,8,128]{2,1,0:T(8,128)} %get-tuple-element.33.gain, ...), custom_call_target="tpu_custom_call" | custom-call | tf_op jit(solution)/shard_map/pallas_call | solution.py:1276

commit v3 on v2

--- a/solution.py
+++ b/solution.py
@@ -412,46 +412,77 @@
     return jnp.where((key_place >= starts) & (key_place <= query_place), 0.0, -1e30)
 
 
-def attend_block(qs, k, vt, ht, lse, q_at, q_len, k_at, k_len, bias):
-    for h in range(4):
+def add_up(total, part):
+    return part if total is None else total + part
+
+
+def attend(units, q, k, vt, kept, ht, inverse, q_len, k_len, chunk, before=None, after=None):
+    def scores(unit):
+        h, slot, q_at, k_at, bias = unit
         lanes = slice((h // 2) * 128, (h // 2) * 128 + 128)
+        out, top = [], None
+        queries = q[pl.ds(q_at, q_len), lanes]
+        for j in range(0, k_len, chunk):
+            s = dot(head_mask(k[pl.ds(k_at + j, chunk), lanes], h % 2), queries, NT)
+            if bias is not None:
+                s = s + bias[j:j + chunk]
+            out.append(s)
+            high = jnp.max(s.reshape(chunk // 8, 8, q_len), axis=0)
+            top = high if top is None else jnp.maximum(top, high)
+        return out, jnp.max(top, axis=0, keepdims=True)
+
+    def values(unit, made):
+        h, slot, q_at, k_at, bias = unit
         rows = slice(h * 64, h * 64 + 64)
-        keys = head_mask(k[pl.ds(k_at, k_len), lanes], h % 2)
-        s = dot(keys, qs[pl.ds(q_at, q_len), lanes], NT)
-        if bias is not None:
-            s = s + bias
-        top = jnp.max(s, axis=0, keepdims=True)
-        p = jnp.exp2(s - top)
-        total = jnp.sum(p, axis=0, keepdims=True)
-        out = dot(vt[rows, pl.ds(k_at, k_len)], p.astype(BF16)) * (1.0 / total)
-        ht[rows, pl.ds(q_at, q_len)] = out.astype(BF16)
-        lse[h:h + 1, pl.ds(q_at, q_len)] = top + jnp.log2(total)
-
-
-def attend_back_block(qs, k, v, kt, gh, lse, inner, dqt, dk, dv, k_at, k_len, q_at, q_len, bias):
-    for pair in range(2):
-        lanes = slice(pair * 128, pair * 128 + 128)
-        sum_k, sum_v = None, None
-        qp = qs[pl.ds(q_at, q_len), lanes]
-        gp = gh[pl.ds(q_at, q_len), lanes]
-        for side in range(2):
-            h = pair * 2 + side
-            rows = slice(h * 64, h * 64 + 64)
-            keys = head_mask(k[pl.ds(k_at, k_len), lanes], side)
-            vals = head_mask(v[pl.ds(k_at, k_len), lanes], side)
-            s = dot(keys, qp, NT)
-            if bias is not None:
-                s = s + bias
-            p = jnp.exp2(s - lse[h:h + 1, pl.ds(q_at, q_len)])
-            dp = dot(vals, gp, NT)
-            ds = (p * (dp - inner[h:h + 1, pl.ds(q_at, q_len)])).astype(BF16)
-            part_v = dot(p.astype(BF16), head_mask(gp, side))
-            part_k = dot(ds, head_mask(qp, side))
-            sum_v = part_v if sum_v is None else sum_v + part_v
-            sum_k = part_k if sum_k is None else sum_k + part_k
-            dqt[rows, pl.ds(q_at, q_len)] += dot(kt[rows, pl.ds(k_at, k_len)], ds)
-        dv[pl.ds(k_at, k_len), lanes] = sum_v.astype(BF16)
-        dk[pl.ds(k_at, k_len), lanes] = (sum_k * math.log(2.0)).astype(BF16)
+        out, total = None, None
+        for n, s in enumerate(made[0]):
+            p = jnp.exp2(s - made[1])
+            total = add_up(total, jnp.sum(p.reshape(chunk // 8, 8, q_len), axis=0))
+            low = p.astype(BF16)
+            kept[slot, n * chunk:(n + 1) * chunk, :] = low
+            out = add_up(out, dot(vt[rows, pl.ds(k_at + n * chunk, chunk)], low))
+        inv = 1.0 / jnp.sum(total, axis=0, keepdims=True)
+        ht[rows, pl.ds(q_at, q_len)] = (out * inv).astype(BF16)
+        inverse[h:h + 1, pl.ds(q_at, q_len)] = inv
+
+    made = None
+    for n, unit in enumerate(units):
+        if n == 0:
+            made = scores(unit)
+        following = scores(units[n + 1]) if n + 1 < len(units) else None
+        values(unit, made)
+        made = following
+
+
+def attend_back(units, v, kt, qt, gh, ght, kept, inner, inverse, dqt, dkt, dvt, q_len, k_len, chunk):
+    def first(unit):
+        h, slot, q_at, k_at = unit
+        lanes = slice((h // 2) * 128, (h // 2) * 128 + 128)
+        grads = gh[pl.ds(q_at, q_len), lanes]
+        return [dot(head_mask(v[pl.ds(k_at + j, chunk), lanes], h % 2), grads, NT) for j in range(0, k_len, chunk)]
+
+    def second(unit, made):
+        h, slot, q_at, k_at = unit
+        rows = slice(h * 64, h * 64 + 64)
+        cols = pl.ds(q_at, q_len)
+        shift = inner[h:h + 1, cols]
+        part_q = None
+        for n, dp in enumerate(made):
+            at = pl.ds(k_at + n * chunk, chunk)
+            p = kept[slot, n * chunk:(n + 1) * chunk, :]
+            ds = (p.astype(F32) * (dp - shift)).astype(BF16)
+            dvt[rows, at] += dot(ght[rows, cols], p, NT)
+            dkt[rows, at] += dot(qt[rows, cols], ds, NT)
+            part_q = add_up(part_q, dot(kt[rows, at], ds))
+        dqt[rows, cols] = (part_q * (inverse[h:h + 1, cols] * HEAD_DIM ** -0.5)).astype(BF16)
+
+    made = None
+    for n, unit in enumerate(units):
+        if n == 0:
+            made = first(unit)
+        following = first(units[n + 1]) if n + 1 < len(units) else None
+        second(unit, made)
+        made = following
 
 
 def gelu_parts(pre):
@@ -493,10 +524,10 @@
 def layer_kernel(
     n_dp,
     lens, expert, gains, x_in, mem_in, cot_in, wqkv_in, wos_in, wq_in, wkv_in, woc_in, up_in, down_in,
-    lo_out, gi_out, gm_out, e_out, a1_out, a2_out, g_out,
+    lo_out, gi_out, gm_out, e_out, a0_out, a1_out, a2_out, g_out,
     x, mem, cot, wqkv, wos, wq, wkv, woc, up, down, starts,
-    s1, s2, gs, n0, n1, n2, q0, k0, v0, q1, k1, v1, kt0, vt0, kt1, vt1, ht0, ht1, lse0, lse1, inner,
-    gb, gh, dqt, dq, dk, dv, hid, gpre, nt, cot_t, eb, a1, a2, r1, r2,
+    s1, s2, gs, n0, n1, n2, q0, k0, v0, q1, k1, v1, vt, ht0, ht1, inv0, inv1, inner,
+    kept0, kept1, kept2, gb, dkt, dvt, work, nt, cot_t, eb, a0, a1, a2, ax0, ax1, ax2, ay0, ay1, ay2,
     snd, rcv, sndh, rcvh, leaving, half_out, gain_sum, g_send,
     y_send, y_recv, w_send, w_recv, c_send, c_recv, x_send, x_recv, h_send, h_recv,
     e_send, e_recv, p_send, p_recv, a_send, a_recv, g_ssem, g_rsem, o_send, o_recv,
@@ -714,8 +745,7 @@
     each(2, lambda i: self_project(c * 2 + i))
     share(0, x).wait_recv()
     each(2, lambda i: self_project((1 - c) * 2 + i))
-    kt0[...] = k0[...].T
-    vt0[...] = v0[...].T
+    vt[...] = v0[...].T
 
     @pl.when(swaps)
     def _():
@@ -725,25 +755,27 @@
 
     def exchange(e, i):
         r = block_rows(i)
-        return remote(snd.at[e, r], rcv.at[e, r], x_send.at[e, i], x_recv.at[e, i], sib)
-
-    def self_out(i):
+        return remote(snd.at[e % 2, r], rcv.at[e % 2, r], x_send.at[e, i], x_recv.at[e, i], sib)
+
+    def out_of(e, i, ht, w_out):
         r = block_rows(i)
-        snd[0, r, :] = dot(ht0[:, r], wos[...], TN).astype(BF16)
-        exchange(0, i).start()
-
-    attend_block(q0, k0, vt0, ht0, lse0, 0, 256, 0, 256, window_bias(0, 0, 256, 256, starts[0:1, 0:256]))
-    self_out(0)
+        snd[e % 2, r, :] = dot(ht[:, r], w_out[...], TN).astype(BF16)
+        exchange(e, i).start()
+
+    everything = range(4)
+    first_bias = window_bias(0, 0, 256, 256, starts[0:1, 0:256])
+    attend([(h, h, 0, 0, first_bias) for h in everything], q0, k0, vt, kept0, ht0, inv0, 256, 256, 256)
+    out_of(0, 0, ht0, wos)
 
     def self_block(j):
         i = j + 1
         q_at = pl.multiple_of(i * 256, 256)
         k_at = pl.multiple_of(j * 256, 256)
-        attend_block(q0, k0, vt0, ht0, lse0, q_at, 256, k_at, 512,
-                     window_bias(k_at, q_at, 512, 256, starts[0:1, pl.ds(q_at, 256)]))
-        self_out(i)
-
-    each(3, self_block)
+        bias = window_bias(k_at, q_at, 512, 256, starts[0:1, pl.ds(q_at, 256)])
+        attend([(h, j * 4 + h, q_at, k_at, bias) for h in everything], q0, k0, vt, kept1, ht0, inv0, 256, 512, 256)
+        out_of(0, i, ht0, wos)
+
+    each(BLOCKS - 1, self_block)
 
     wait_swapped(MEM)
 
@@ -761,12 +793,11 @@
     each(2, lambda i: memory_project(c * 2 + i))
     share(1, mem).wait_recv()
     each(2, lambda i: memory_project((1 - c) * 2 + i))
-    kt1[...] = k1[...].T
-    vt1[...] = v1[...].T
+    vt[...] = v1[...].T
     wait_weight(WQ)
     wait_weight(WOC)
 
-    def cross_block(i):
+    def cross_norm(i):
         r = block_rows(i)
         exchange(0, i).wait_recv()
         state = x[r, :].astype(F32) + (snd[0, r, :].astype(F32) + rcv[0, r, :].astype(F32))
@@ -775,11 +806,20 @@
         nn = (xhat * gains[1:2, :]).astype(BF16)
         n1[r, :] = nn
         q1[r, :] = (dot(nn, wq[...]) * QSCALE).astype(BF16)
-        attend_block(q1, k1, vt1, ht1, lse1, pl.multiple_of(i * 256, 256), 256, 0, LEN, None)
-        snd[1, r, :] = dot(ht1[:, r], woc[...], TN).astype(BF16)
-        exchange(1, i).start()
-
-    each(BLOCKS, cross_block)
+
+    each(BLOCKS, cross_norm)
+
+    def cross_pair(j):
+        units = []
+        for i in range(2):
+            for h in everything:
+                at = pl.multiple_of((j * 2 + i) * 256, 256)
+                units.append((h, (j * 2 + i) * 4 + h, at, 0, None))
+        attend(units, q1, k1, vt, kept2, ht1, inv1, 256, LEN, 256)
+        out_of(1, j * 2, ht1, woc)
+        out_of(1, j * 2 + 1, ht1, woc)
+
+    each(BLOCKS // 2, cross_pair)
 
     wait_swapped(COT)
 
@@ -845,25 +885,44 @@
 
         each(n_dp, one)
 
+    hid, gpre = work.at[0:LEN], work.at[LEN:2 * LEN]
+
+    def expert_tile(f):
+        cols = slice(f * TILE, (f + 1) * TILE)
+
+        def first(i):
+            r = slice(i * BLOCK, (i + 1) * BLOCK)
+            return dot(n2[r, :], up[:, cols]), dot(cot[r, :], down[cols, :], NT)
+
+        def second(i, made):
+            r = slice(i * BLOCK, (i + 1) * BLOCK)
+            pre, grad = made
+            phi, slope = gelu_parts(pre)
+            hid[r, cols] = (pre * phi).astype(BF16)
+            gpre[r, cols] = (grad * slope).astype(BF16)
+
+        made = first(0)
+        for i in range(BLOCKS):
+            following = first(i + 1) if i + 1 < BLOCKS else None
+            second(i, made)
+            made = following
+        eb[f, :, 0:TILE] = dot(nt[...], gpre[:, cols]).astype(BF16)
+        eb[f, :, TILE:2 * TILE] = dot(cot_t[...], hid[:, cols]).astype(BF16)
+        scatter(f, begin)
+
     for f in range(TILES):
         wait_bring(UP + f)
         wait_bring(DOWN + f)
-        cols = tile(f)
-
-        def expert_block(i):
-            r = block_rows(i)
-            phi, slope = gelu_parts(pre := dot(n2[r, :], up[:, cols]))
-            hid[r, cols] = (pre * phi).astype(BF16)
-            gpre[r, cols] = (dot(cot[r, :], down[cols, :], NT) * slope).astype(BF16)
-
-        each(BLOCKS, expert_block)
-        eb[f, :, 0:TILE] = dot(nt[...], gpre[:, cols]).astype(BF16)
-        eb[f, :, TILE:2 * TILE] = dot(cot_t[...], hid[:, cols]).astype(BF16)
-        scatter(f, begin)
+        expert_tile(f)
+
+    def done_sending(e):
+        each(BLOCKS, lambda i: exchange(e, i).wait_send())
+
+    done_sending(0)
 
     def expert_back(i):
         r = block_rows(i)
-        snd[2, r, :] = dot(gpre[r, :], up[...], NT).astype(BF16)
+        snd[0, r, :] = dot(gpre[r, :], up[...], NT).astype(BF16)
         exchange(2, i).start()
 
     each(BLOCKS, expert_back)
@@ -872,8 +931,7 @@
         r = block_rows(i)
         part = dot(hid[r, :], down[...])
         mine = lax.div(i, 2) == c
-        low = lax.rem(i, 2)
-        rl = block_rows(low)
+        rl = block_rows(lax.rem(i, 2))
 
         @pl.when(mine)
         def _():
@@ -882,16 +940,23 @@
         @pl.when(jnp.logical_not(mine))
         def _():
             sndh[0, rl, :] = part.astype(BF16)
-            half_exchange(0, low).start()
+            half_exchange(0, lax.rem(i, 2)).start()
 
     each(BLOCKS, expert_out)
 
+    def strip(n):
+        return work.at[n * COLS:(n + 1) * COLS]
+
+    dqt, dkb, dvb, ght = strip(0), strip(1), strip(2), strip(3)
+    kt, qt = cot_t.at[0:COLS], cot_t.at[COLS:2 * COLS]
+    dq, dk = down.at[:, 0:COLS], down.at[:, COLS:2 * COLS]
+    gh, dv = n2.at[:, 0:COLS], n2.at[:, COLS:2 * COLS]
     gain_sum[...] = jnp.zeros_like(gain_sum)
 
-    def branch_block(n, i, e, state, base, ht, w_out):
+    def branch_block(n, i, e, state, base, ht, inv, w_out):
         r = block_rows(i)
         exchange(e, i).wait_recv()
-        grad = snd[e, r, :].astype(F32) + rcv[e, r, :].astype(F32)
+        grad = snd[e % 2, r, :].astype(F32) + rcv[e % 2, r, :].astype(F32)
         step, share_gain = norm_back(state[r, :], gains[n:n + 1, :], grad)
         total = base[r, :].astype(F32) + step
         gs[r, :] = total
@@ -899,175 +964,220 @@
         gb[r, :] = low
         gain_sum[n:n + 1, :] += jnp.where(lax.div(i, 2) == c, share_gain, 0.0)
         gh[r, :] = dot(low, w_out[...], NT).astype(BF16)
-        ght = dot(w_out[...], low, NT).astype(BF16).astype(F32)
-        prod = ght * ht[:, r].astype(F32)
-        for h in range(4):
-            inner[h:h + 1, r] = jnp.sum(prod[h * 64:h * 64 + 64], axis=0, keepdims=True)
-
-    each(BLOCKS, lambda i: branch_block(2, i, 2, s2, cot, ht1, woc))
-    dqt[...] = jnp.zeros_like(dqt)
-
-    def cross_back(i):
-        at = pl.multiple_of(i * 256, 256)
-        attend_back_block(q1, k1, v1, kt1, gh, lse1, inner, dqt, dk, dv, at, 256, 0, LEN, None)
-
-    each(BLOCKS, cross_back)
-    dq[...] = (dqt[...] * HEAD_DIM ** -0.5).astype(BF16).T
+        turned = dot(w_out[...], low, NT).astype(BF16).astype(F32)
+        prod = turned * ht[:, r].astype(F32)
+        for h in everything:
+            rows = slice(h * 64, h * 64 + 64)
+            inner[h:h + 1, r] = jnp.sum(prod[rows], axis=0, keepdims=True)
+            ght[rows, r] = (turned[rows] * inv[h:h + 1, r]).astype(BF16)
+
+    def turn_queries(q, k, inv):
+        kt[...] = k[...].T
+        turned = q[...].T
+        for h in everything:
+            rows = slice(h * 64, h * 64 + 64)
+            qt[rows, :] = (turned[rows].astype(F32) * inv[h:h + 1, :]).astype(BF16)
+        dkt[...] = jnp.zeros_like(dkt)
+        dvt[...] = jnp.zeros_like(dvt)
+
+    zs = n_dp // 4
+    side = lax.rem(pair, 2)
+    z = lax.div(d, 4)
+    across = (d + 2 - 4 * side, t)
+    pieces = ((a0, ax0, ay0, a0_out), (a1, ax1, ay1, a1_out), (a2, ax2, ay2, a2_out))
+
+    def over_x(n):
+        buf, place = pieces[n][:2]
+        return remote(buf.at[:, 1 - side], place, p_send.at[0, n], p_recv.at[0, n], across)
+
+    def over_y(n):
+        buf, place = pieces[n][0], pieces[n][2]
+        return remote(buf.at[:, side], place, p_send.at[1, n], p_recv.at[1, n], (d, c))
+
+    def add_x(n):
+        buf, place = pieces[n][:2]
+        over_x(n).wait_recv()
+        buf[:, side] = (buf[:, side].astype(F32) + place[...].astype(F32)).astype(BF16)
+
+        @pl.when(swaps)
+        def _():
+            over_y(n).start()
+
+    def owners(n, action):
+        buf, out = pieces[n][0], pieces[n][3]
+
+        def one(s):
+            to = lax.rem(z * 2 + c + s + 1, 2 * zs)
+            to_z, to_c = lax.div(to, 2), lax.rem(to, 2)
+            src = buf.at[to_z, side, pl.ds(pl.multiple_of(to_c * 32, 32), 32)]
+            action(remote(src, out.at[z], a_send.at[n, s], a_recv.at[n, z], (to_z * 4 + side * 2 + to_c, t)))
+
+        each(2 * zs - 1, one)
+
+    def own_share(n):
+        src = pieces[n][0].at[z, side, pl.ds(pl.multiple_of(c * 32, 32), 32)]
+        return pltpu.make_async_copy(src, pieces[n][3].at[z], a_recv.at[n, z])
+
+    def add_y(n):
+        @pl.when(stays)
+        def _():
+            buf, place = pieces[n][0], pieces[n][2]
+            over_y(n).wait_recv()
+            buf[:, side] = (buf[:, side].astype(F32) + place[...].astype(F32)).astype(BF16)
+            own_share(n).start()
+            owners(n, begin)
+
+    def collect_piece(n):
+        buf, out = pieces[n][0], pieces[n][3]
+
+        def one(i):
+            @pl.when(stays & (i == z))
+            def _():
+                own_share(n).wait()
+
+            @pl.when(jnp.logical_not(stays & (i == z)))
+            def _():
+                remote(buf.at[0, 0, pl.ds(0, 32)], out.at[i], a_send.at[n, 0], a_recv.at[n, i], diag).wait_recv()
+
+        each(zs, one)
+
+        @pl.when(stays)
+        def _():
+            owners(n, finish_send)
+
+        @pl.when(swaps)
+        def _():
+            over_y(n).wait_send()
+
+        over_x(n).wait_send()
+
+    def by_owner(grad):
+        return grad.astype(BF16).T.reshape(zs, 2, WIDTH // (2 * zs), grad.shape[0])
+
+    each(BLOCKS, lambda i: branch_block(2, i, 2, s2, cot, ht1, inv1, woc))
+    turn_queries(q1, k1, inv1)
+
+    def cross_back(h):
+        units = [(hh, i * 4 + hh, i * 256, 0) for hh in (2 * h, 2 * h + 1) for i in range(BLOCKS)]
+        attend_back(units, v1, kt, qt, gh, ght, kept2, inner, inv1, dqt, dkt, dvt, 256, LEN, 256)
+
+    cross_back(0)
+    cross_back(1)
+
+    def leave(n, out):
+        buf = leaving.at[n]
+        return (lambda: remote(buf, out, o_send.at[n], o_recv.at[n], diag),
+                lambda: pltpu.make_async_copy(buf, out, o_recv.at[n]))
+
+    def start_leave(n, out):
+        far, near = leave(n, out)
+
+        @pl.when(swaps)
+        def _():
+            far().start()
+
+        @pl.when(stays)
+        def _():
+            near().start()
+
+    def wait_leave(n, out):
+        far, near = leave(n, out)
+
+        @pl.when(swaps)
+        def _():
+            far().wait()
+
+        @pl.when(stays)
+        def _():
+            near().wait()
+
+    def half_done(n, out):
+        def one(low):
+            half_exchange(n, low).wait_recv()
+            r = block_rows(low)
+            leaving[n, r, :] = (half_out[r, :] + rcvh[n, r, :].astype(F32)).astype(BF16)
+
+        each(2, one)
+        start_leave(n, out)
+
+    half_done(0, lo_out)
+
+    def settle():
+        dkb[...] = (dkt[...] * math.log(2.0)).astype(BF16)
+        dvb[...] = dvt[...].astype(BF16)
+        dq[...] = dqt[...].T
+        dk[...] = dkb[...].T
+        dv[...] = dvb[...].T
+
+    settle()
+    done_sending(1)
 
     def cross_grads(i):
         r = block_rows(i)
-        snd[3, r, :] = dot(dq[r, :], wq[...], NT).astype(BF16)
+        snd[1, r, :] = dot(dq[r, :], wq[...], NT).astype(BF16)
         exchange(3, i).start()
 
     each(BLOCKS, cross_grads)
+    a0[:, :, :, 0:256] = by_owner(dot(ht1[...], gb[...]))
+    a0[:, :, :, 256:512] = by_owner(dot(dqt[...], n1[...]))
+    a0[:, :, :, 512:768] = by_owner(dot(dkb[...], mem[...]))
+    a0[:, :, :, 768:1024] = by_owner(dot(dvb[...], mem[...]))
+    over_x(0).start()
 
     def memory_grads(i):
         r = block_rows(i)
         part = dot(dk[r, :], wkv[0], NT) + dot(dv[r, :], wkv[1], NT)
         mine = lax.div(i, 2) == c
-        low = lax.rem(i, 2)
-        rl = block_rows(low)
+        rl = block_rows(lax.rem(i, 2))
 
         @pl.when(mine)
         def _():
-            half_out[pl.ds(pl.multiple_of(HALF + low * BLOCK, BLOCK), BLOCK), :] = part
+            half_out[rl, :] = part
 
         @pl.when(jnp.logical_not(mine))
         def _():
             sndh[1, rl, :] = part.astype(BF16)
-            half_exchange(1, low).start()
+            half_exchange(1, lax.rem(i, 2)).start()
 
     each(BLOCKS, memory_grads)
-    a1[:, 0:256] = dot(ht1[...], gb[...]).T.astype(BF16)
-    nt[...] = n1[...].T
-    a1[:, 256:512] = dot(nt[...], dq[...]).astype(BF16)
-    nt[...] = mem[...].T
-    a1[:, 512:768] = dot(nt[...], dk[...]).astype(BF16)
-    a1[:, 768:1024] = dot(nt[...], dv[...]).astype(BF16)
-
-    def over(n):
-        buf, place = ((a1, r1), (a2.at[0], r2.at[0]), (a2.at[1], r2.at[1]), (a2.at[2], r2.at[2]))[n]
-        return remote(buf, place, p_send.at[n], p_recv.at[n], (d, c))
-
-    def hand_over(n):
-        @pl.when(swaps)
-        def _():
-            over(n).start()
-
-    def hand_out(n):
-        if n == 0:
-            return a1, a1_out.at[pair]
-        return a2.at[n - 1], a2_out.at[pair, n - 1]
-
-    def owners(n, action):
-        src, dst = hand_out(n)
-
-        def one(s):
-            to = lax.rem(d + s + 1, n_dp)
-            action(remote(share_rows(src, to), dst, a_send.at[n, s + 1], a_recv.at[n, pair], (to, t)))
-
-        each(n_dp - 1, one)
-
-    def add_over(n):
-        @pl.when(stays)
-        def _():
-            over(n).wait_recv()
-            if n == 0:
-                a1[...] = (a1[...].astype(F32) + r1[...].astype(F32)).astype(BF16)
-            else:
-                a2[n - 1] = (a2[n - 1].astype(F32) + r2[n - 1].astype(F32)).astype(BF16)
-            src, dst = hand_out(n)
-            pltpu.make_async_copy(share_rows(src, d), dst, a_recv.at[n, pair]).start()
-            owners(n, begin)
-
-    def collect_over(n):
-        def one(i):
-            src = hand_out(n)[0].at[pl.ds(0, 32)]
-            dst = a1_out.at[i] if n == 0 else a2_out.at[i, n - 1]
-
-            @pl.when(stays & (i == pair))
-            def _():
-                pltpu.make_async_copy(src, dst, a_recv.at[n, i]).wait()
-
-            @pl.when(jnp.logical_not(stays & (i == pair)))
-            def _():
-                remote(src, dst, a_send.at[n, 0], a_recv.at[n, i], diag).wait_recv()
-
-        each(n_pairs, one)
-
-        @pl.when(stays)
-        def _():
-            owners(n, finish_send)
-
-        @pl.when(swaps)
-        def _():
-            over(n).wait_send()
-
-    def leave(n, out):
-        buf = leaving.at[n]
-        return (lambda: remote(buf, out, o_send.at[n], o_recv.at[n], diag),
-                lambda: pltpu.make_async_copy(buf, out, o_recv.at[n]))
-
-    def start_leave(n, out):
-        far, near = leave(n, out)
-
-        @pl.when(swaps)
-        def _():
-            far().start()
-
-        @pl.when(stays)
-        def _():
-            near().start()
-
-    def wait_leave(n, out):
-        far, near = leave(n, out)
-
-        @pl.when(swaps)
-        def _():
-            far().wait()
-
-        @pl.when(stays)
-        def _():
-            near().wait()
-
-    for n in range(2):
-        for low in range(2):
-            half_exchange(n, low).wait_recv()
-            r = pl.ds(low * BLOCK, BLOCK)
-            whole = half_out[pl.ds(n * HALF + low * BLOCK, BLOCK), :] + rcvh[n, r, :].astype(F32)
-            leaving[n, r, :] = whole.astype(BF16)
-        start_leave(n, (lo_out, gm_out)[n])
-
-    each(BLOCKS, lambda i: branch_block(1, i, 3, s1, gs, ht0, wos))
-    a1[:, 1024:1280] = dot(ht0[...], gb[...]).T.astype(BF16)
-    hand_over(0)
-    dqt[...] = jnp.zeros_like(dqt)
-
-    def self_back(i):
-        at = pl.multiple_of(i * 256, 256)
-        attend_back_block(q0, k0, v0, kt0, gh, lse0, inner, dqt, dk, dv, at, 256, at, 512,
-                          window_bias(at, at, 256, 512, starts[0:1, pl.ds(at, 512)]))
-
-    each(BLOCKS - 1, self_back)
-    attend_back_block(q0, k0, v0, kt0, gh, lse0, inner, dqt, dk, dv, 768, 256, 768, 256,
-                      window_bias(768, 768, 256, 256, starts[0:1, 768:1024]))
-    dq[...] = (dqt[...] * HEAD_DIM ** -0.5).astype(BF16).T
+
+    each(BLOCKS, lambda i: branch_block(1, i, 3, s1, gs, ht0, inv0, wos))
+    half_done(1, gm_out)
+    turn_queries(q0, k0, inv0)
+
+    def self_back(pair_of_heads):
+        heads = (2 * pair_of_heads, 2 * pair_of_heads + 1)
+        attend_back([(h, h, 0, 0) for h in heads], v0, kt, qt, gh, ght, kept0, inner, inv0, dqt, dkt, dvt, 256, 256, 256)
+        units = [(h, j * 4 + h, (j + 1) * 256, j * 256) for h in heads for j in range(BLOCKS - 1)]
+        attend_back(units, v0, kt, qt, gh, ght, kept1, inner, inv0, dqt, dkt, dvt, 256, 512, 256)
+        rows = slice(pair_of_heads * 128, pair_of_heads * 128 + 128)
+        dkb[rows, :] = (dkt[rows, :] * math.log(2.0)).astype(BF16)
+        dvb[rows, :] = dvt[rows, :].astype(BF16)
+        buf = pieces[1 + pair_of_heads][0]
+        for n, grad in enumerate((dqt, dkb, dvb)):
+            buf[:, :, :, n * 128:n * 128 + 128] = by_owner(dot(grad[rows, :], n0[...]))
+
+    a1[:, :, :, 384:640] = by_owner(dot(ht0[...], gb[...]))
+    self_back(0)
+    over_x(1).start()
+    add_x(0)
+    self_back(1)
+    over_x(2).start()
+    dq[...] = dqt[...].T
+    dk[...] = dkb[...].T
+    dv[...] = dvb[...].T
 
     def input_grads(i):
         r = block_rows(i)
         return dot(dq[r, :], wqkv[0], NT) + dot(dk[r, :], wqkv[1], NT) + dot(dv[r, :], wqkv[2], NT)
 
     def input_send(low):
-        rl = block_rows(low)
-        sndh[2, rl, :] = input_grads((1 - c) * 2 + low).astype(BF16)
+        sndh[2, block_rows(low), :] = input_grads((1 - c) * 2 + low).astype(BF16)
         half_exchange(2, low).start()
 
     each(2, input_send)
-    add_over(0)
-    nt[...] = n0[...].T
-    for n, grad in enumerate((dq, dk, dv)):
-        a2[n] = dot(nt[...], grad[...]).astype(BF16)
-        hand_over(n + 1)
+    add_y(0)
+    add_x(1)
 
     def input_keep(low):
         half_out[block_rows(low), :] = input_grads(c * 2 + low)
@@ -1085,8 +1195,8 @@
 
     each(2, input_done)
     start_leave(2, gi_out)
-    for n in range(1, 4):
-        add_over(n)
+    add_x(2)
+    add_y(1)
 
     number = jnp.full((1, 128), expert[0, 0].astype(F32))
     for j in range(n_dp):
@@ -1102,6 +1212,8 @@
     each(n_all - 1, lambda s: gain_copy(s + 1).start())
     keep_gain = pltpu.make_async_copy(g_send.at[d], g_out.at[lin], g_rsem.at[lin])
     keep_gain.start()
+
+    add_y(2)
 
     wait_leave(0, lo_out)
     wait_leave(1, gm_out)
@@ -1109,8 +1221,8 @@
     for f in range(TILES):
         collect(f)
         scatter(f, finish_send)
-    for n in range(4):
-        collect_over(n)
+    for n in range(3):
+        collect_piece(n)
     keep_gain.wait()
 
     def gain_wait(s):
@@ -1135,8 +1247,8 @@
     def _():
         share_starts().wait_send()
 
-    for e in range(4):
-        each(BLOCKS, lambda i: exchange(e, i).wait_send())
+    done_sending(2)
+    done_sending(3)
     for e in range(3):
         each(2, lambda i: half_exchange(e, i).wait_send())
 
@@ -1156,30 +1268,29 @@
     heads = bf(LEN, COLS)
     turned = bf(COLS, LEN)
     half = jax.ShapeDtypeStruct((HALF, WIDTH), BF16)
-    n_pairs = n_dp // 2
+    zs = n_dp // 4
+    sizes = (4 * COLS, 5 * COLS // 2, 3 * COLS // 2)
+    split = [bf(zs, 2, WIDTH // (2 * zs), size) for size in sizes]
+    parts = [bf(zs, WIDTH // (2 * zs), size) for size in sizes]
     return pl.pallas_call(
         partial(layer_kernel, n_dp),
-        out_shape=(half, half, half,
-                   jax.ShapeDtypeStruct((n_dp, TILES, 32, 2 * TILE), BF16),
-                   jax.ShapeDtypeStruct((n_pairs, 32, 5 * COLS), BF16),
-                   jax.ShapeDtypeStruct((n_pairs, 3, 32, COLS), BF16),
+        out_shape=(half, half, half, jax.ShapeDtypeStruct((n_dp, TILES, 32, 2 * TILE), BF16),
+                   *[jax.ShapeDtypeStruct((zs, 32, size), BF16) for size in sizes],
                    jax.ShapeDtypeStruct((2 * n_dp, 8, 128), F32)),
         in_specs=[IN_SMEM] * 2 + [IN_VMEM] + [ANY_PLACE] * 10,
-        out_specs=(ANY_PLACE,) * 7,
+        out_specs=(ANY_PLACE,) * 8,
         scratch_shapes=[
             tokens, tokens, tokens, bf(3, WIDTH, COLS), bf(COLS, WIDTH), bf(WIDTH, COLS), bf(2, WIDTH, COLS),
             bf(COLS, WIDTH), bf(WIDTH, HIDDEN), bf(HIDDEN, WIDTH), pltpu.VMEM((8, LEN), jnp.int32),
             fl(LEN, WIDTH), fl(LEN, WIDTH), fl(LEN, WIDTH), tokens, tokens, tokens,
-            heads, heads, heads, heads, heads, heads, turned, turned, turned, turned, turned, turned,
-            fl(8, LEN), fl(8, LEN), fl(8, LEN),
-            tokens, heads, fl(COLS, LEN), heads, heads, heads, bf(LEN, HIDDEN), bf(LEN, HIDDEN), bf(WIDTH, LEN),
-            bf(WIDTH, LEN), bf(TILES, WIDTH, 2 * TILE), bf(WIDTH, 5 * COLS), bf(3, WIDTH, COLS),
-            bf(WIDTH, 5 * COLS), bf(3, WIDTH, COLS),
-            bf(4, LEN, WIDTH), bf(4, LEN, WIDTH), bf(3, HALF, WIDTH), bf(3, HALF, WIDTH), bf(3, HALF, WIDTH),
-            fl(LEN, WIDTH), fl(8, WIDTH), fl(n_dp, 8, 128),
-            dma(3 + 2 * TILES), dma(3 + 2 * TILES), dma(5, n_pairs), dma(5, n_pairs), dma(4), dma(4),
+            heads, heads, heads, heads, heads, heads, turned, turned, turned, fl(8, LEN), fl(8, LEN), fl(8, LEN),
+            bf(4, 256, 256), bf(12, 512, 256), bf(16, LEN, 256), tokens, fl(COLS, LEN), fl(COLS, LEN),
+            bf(2 * LEN, HIDDEN), bf(WIDTH, LEN), bf(WIDTH, LEN), bf(TILES, WIDTH, 2 * TILE), *split, *parts, *parts,
+            bf(2, LEN, WIDTH), bf(2, LEN, WIDTH), bf(3, HALF, WIDTH), bf(3, HALF, WIDTH), bf(3, HALF, WIDTH),
+            fl(HALF, WIDTH), fl(8, WIDTH), fl(n_dp, 8, 128),
+            dma(3 + 2 * TILES), dma(3 + 2 * TILES), dma(5, n_dp // 2), dma(5, n_dp // 2), dma(4), dma(4),
             dma(4, 4), dma(4, 4), dma(3, 2), dma(3, 2),
-            dma(TILES, n_dp), dma(TILES, n_dp), dma(4), dma(4), dma(4, n_dp), dma(4, n_pairs),
+            dma(TILES, n_dp), dma(TILES, n_dp), dma(2, 3), dma(2, 3), dma(3, 2 * zs), dma(3, zs),
             dma(2 * n_dp), dma(2 * n_dp), dma(3), dma(3),
         ],
         compiler_params=pltpu.CompilerParams(
@@ -1215,9 +1326,9 @@
 
 
 def place_kernel(
-    gains_any, e_any, a1_any, a2_any, gi_any, gm_any, lo_any,
+    gains_any, e_any, a0_any, a1_any, a2_any, gi_any, gm_any, lo_any,
     lo_out, gi_out, gm_out, gain_out, qkv_out, os_out, q_out, kv_out, oc_out, up_out, down_out,
-    ids, gains_in, e_in, a1_in, a2_in, gi_in, gm_in, lo_in, gi_v, gm_v, ups, downs, in_sems, e_sems, up_sems, down_sems, out_sems,
+    ids, gains_in, e_in, a0_in, a1_in, a2_in, gi_in, gm_in, lo_in, gi_v, gm_v, ups, downs, in_sems, e_sems, up_sems, down_sems, out_sems,
 ):
     rows = e_in.shape[0]
     number = pltpu.make_async_copy(gains_any, ids, in_sems.at[0])
@@ -1225,7 +1336,8 @@
     blocks = [pltpu.make_async_copy(e_any.at[r], e_in.at[r], e_sems.at[r]) for r in range(rows)]
     for copy in blocks:
         copy.start()
-    pairs = ((lo_any, lo_in), (gi_any, gi_in), (gm_any, gm_in), (gains_any, gains_in), (a1_any, a1_in), (a2_any, a2_in))
+    pairs = ((lo_any, lo_in), (gi_any, gi_in), (gm_any, gm_in), (gains_any, gains_in), (a0_any, a0_in),
+             (a1_any, a1_in), (a2_any, a2_in))
     reads = [pltpu.make_async_copy(src, dst, in_sems.at[1 + n]) for n, (src, dst) in enumerate(pairs)]
     for copy in reads:
         copy.start()
@@ -1255,13 +1367,17 @@
     for copy in reads[3:]:
         copy.wait()
     gain_out[...] = jnp.sum(gains_in[...], axis=0)[:3, :32]
-    first = jnp.sum(a1_in[...].astype(F32), axis=0)
+    first = jnp.sum(a0_in[...].astype(F32), axis=0)
     oc_out[...] = first[:, 0:COLS]
     q_out[...] = first[:, COLS:2 * COLS]
     kv_out[0] = first[:, 2 * COLS:3 * COLS]
     kv_out[1] = first[:, 3 * COLS:4 * COLS]
-    os_out[...] = first[:, 4 * COLS:5 * COLS]
-    qkv_out[...] = jnp.sum(a2_in[...].astype(F32), axis=0)
+    second = jnp.sum(a1_in[...].astype(F32), axis=0)
+    third = jnp.sum(a2_in[...].astype(F32), axis=0)
+    for n in range(3):
+        qkv_out[n, :, 0:128] = second[:, n * 128:n * 128 + 128]
+        qkv_out[n, :, 128:256] = third[:, n * 128:n * 128 + 128]
+    os_out[...] = second[:, 384:640]
     for copy in writes:
         copy.wait()
 
@@ -1278,10 +1394,10 @@
         out_shape=(jax.ShapeDtypeStruct((HALF, WIDTH), BF16), shape(HALF, WIDTH), shape(HALF, WIDTH), shape(3, 32), shape(3, 32, COLS), shape(32, COLS),
                    shape(32, COLS), shape(2, 32, COLS), shape(32, COLS),
                    shape(experts, 32, HIDDEN), shape(experts, 32, HIDDEN)),
-        in_specs=[IN_HBM] * 7,
+        in_specs=[IN_HBM] * 8,
         out_specs=(IN_HBM,) * 3 + (IN_VMEM,) * 6 + (IN_HBM,) * 2,
         scratch_shapes=[pltpu.SMEM(arrays[0].shape, F32)] + [like(array) for array in arrays] + [
-            half, half, staged, staged, dma(7), dma(rows), dma(rows), dma(rows), dma(3)],
+            half, half, staged, staged, dma(8), dma(rows), dma(rows), dma(rows), dma(3)],
         compiler_params=pltpu.CompilerParams(vmem_limit_bytes=VMEM_BYTES),
     )(*arrays)
 
@@ -1292,12 +1408,12 @@
 ):
     n_dp = lax.axis_size("dp")
     up, down = choose_expert(expert_ids, w_up, w_down)
-    layer_output, grad_input, grad_memory, e_rows, a1_rows, a2_rows, gain_rows = paired_layer(
+    layer_output, grad_input, grad_memory, e_rows, a0_rows, a1_rows, a2_rows, gain_rows = paired_layer(
         n_dp, seg_lengths, expert_ids, ln_gains,
         layer_input[0], memory[0], cotangent[0], w_qkv, w_out_self, w_query_cross, w_kv_cross, w_out_cross, up, down,
     )
     layer_output, grad_input, grad_memory, gain_share, qkv, out_self, query, key_value, out_cross, grad_up, grad_down = place_grads(
-        w_up.shape[0], gain_rows, e_rows, a1_rows, a2_rows, grad_input, grad_memory, layer_output)
+        w_up.shape[0], gain_rows, e_rows, a0_rows, a1_rows, a2_rows, grad_input, grad_memory, layer_output)
     return (
         layer_output[None], grad_input[None], grad_memory[None], gain_share, qkv, out_self.T, query, key_value,
         out_cross.T, grad_up, jnp.swapaxes(grad_down, 1, 2),

time: 164 us -> 136 us (0.83)
  Pallas kernels: 161 us -> 134 us
    pallas_call x1, Pallas kernels: 152 us -> 124 us  [paired_layer(): pl.pallas_call(partial(layer_kernel, n_dp), out_shape=(half, half, half,...]
where the time goes in v3:
time: 136 us
  Pallas kernels  134 us (99%)
  between operations  1.51 us (1%)
    pallas_call x1, Pallas kernels, paired_layer(): pl.pallas_call(partial(layer_kernel, n_dp), out_shape=(half, half, half,...  124 us
    pallas_call x1, Pallas kernels, place_grads(): pl.pallas_call(place_kernel, out_shape=(jax.ShapeDtypeStruct((HALF, WIDTH...  7.01 us
    pallas_call x1, Pallas kernels, choose_expert(): pl.pallas_call(choose_kernel, out_shape=(jax.ShapeDtypeStruct(w_up.shape[...  2.89 us

profile of v3, /device:TPU:0, one launch (start us, length us, event | category | flops | bytes accessed | tf_op | source)
XLA Modules:
  0.0 135.9 jit_solution(6987968186581323867)
XLA Ops:
  1.3 2.9 %shard_map.212 = (bf16[512,1024]{1,0:T(8,128)(2,1)}, bf16[1024,512]{1,0:T(8,128)(2,1)}) custom-call(s32[1,1]{1,0:T(1,128)S(6)} %copy.24.expert, bf16[16,512,1024]{2,1,0:T(8,128)(2,1)} %up_in.1, bf16[16,1024,512]{2,1,0:T(8,128)(2,1)} %down_in.1), custom_call_target="tpu_custom_call" | custom-call | tf_op jit(solution)/shard_map/pallas_call | solution.py:1318
  4.2 124.5 %shard_map.213 = (bf16[512,512]{1,0:T(8,128)(2,1)}, bf16[512,512]{1,0:T(8,128)(2,1)}, bf16[512,512]{1,0:T(8,128)(2,1)}, bf16[16,4,32,512]{3,2,1,0:T(8,128)(2,1)}...) custom-call(s32[1,16]{1,0:T(1,128)} %lens.1, ...), custom_call_target="tpu_custom_call" | custom-call | flops 20000000000 | bytes 20971520 | tf_op jit(solution)/shard_map/pallas_call | solution.py:1275
  128.7 7.0 %shard_map.214 = (bf16[512,512]{1,0:T(8,128)(2,1)}, f32[512,512]{1,0:T(8,128)}, f32[512,512]{1,0:T(8,128)}, f32[3,32]{1,0:T(4,128)}, f32[3,32,256]{2,1,0:T(8,128...) custom-call(f32[32,8,128]{2,1,0:T(8,128)} %get-tuple-element.34.gain, ...), custom_call_target="tpu_custom_call" | custom-call | tf_op jit(solution)/shard_map/pallas_call | solution.py:1392

commit v4 on v3

--- a/solution.py
+++ b/solution.py
@@ -394,6 +394,7 @@
 BLOCKS = LEN // BLOCK
 TILE = 256
 TILES = HIDDEN // TILE
+PIECES = (COLS, 3 * COLS // 2, 3 * COLS // 2) * 2
 
 
 def dot(left, right, dims=NN):
@@ -524,11 +525,12 @@
 def layer_kernel(
     n_dp,
     lens, expert, gains, x_in, mem_in, cot_in, wqkv_in, wos_in, wq_in, wkv_in, woc_in, up_in, down_in,
-    lo_out, gi_out, gm_out, e_out, a0_out, a1_out, a2_out, g_out,
+    lo_out, gi_out, gm_out, e_out, a0_out, a1_out, a2_out, a3_out, a4_out, a5_out, g_out, ids_out,
     x, mem, cot, wqkv, wos, wq, wkv, woc, up, down, starts,
     s1, s2, gs, n0, n1, n2, q0, k0, v0, q1, k1, v1, vt, ht0, ht1, inv0, inv1, inner,
-    kept0, kept1, kept2, gb, dkt, dvt, work, nt, cot_t, eb, a0, a1, a2, ax0, ax1, ax2, ay0, ay1, ay2,
-    snd, rcv, sndh, rcvh, leaving, half_out, gain_sum, g_send,
+    kept0, kept1, kept2, gb, dkt, dvt, work, nt, cot_t, eb,
+    a0, a1, a2, a3, a4, a5, ax0, ax1, ax2, ax3, ax4, ax5, ay0, ay1, ay2, ay3, ay4, ay5,
+    snd, rcv, sndh, rcvh, leaving, half_out, gain_sum, g_send, g_in,
     y_send, y_recv, w_send, w_recv, c_send, c_recv, x_send, x_recv, h_send, h_recv,
     e_send, e_recv, p_send, p_recv, a_send, a_recv, g_ssem, g_rsem, o_send, o_recv,
 ):
@@ -601,8 +603,13 @@
 
     n_pairs = n_dp // 2
     pair = lax.div(d, 2)
-    halves = [(wqkv_in, wqkv), (wos_in, wos), (wq_in, wq), (wkv_in, wkv), (woc_in, woc)]
-    WQKV, WOS, WQ, WKV, WOC = range(5)
+    halves = [(wqkv_in.at[1:3], wqkv.at[1:3]), (wqkv_in.at[0:1], wqkv.at[0:1]), (wos_in, wos), (wkv_in, wkv),
+              (wq_in, wq), (woc_in, woc)]
+    WKV0, WQ0, WOS, WKV, WQ, WOC = range(6)
+    zs = n_dp // 4
+    side = lax.rem(pair, 2)
+    z = lax.div(d, 4)
+    across = (d + 2 - 4 * side, t)
 
     def piece(ref, p):
         if len(ref.shape) == 3:
@@ -615,10 +622,19 @@
         src, dst = halves[n]
         return remote(piece(src, pair), piece(dst, pair), w_send.at[n, 0], w_recv.at[n, pair], diag)
 
-    def hand_piece(n, s):
+    def hand_along(n, s):
         dst = halves[n][1]
-        to = lax.rem(pair + s, n_pairs)
-        return remote(piece(dst, pair), piece(dst, pair), w_send.at[n, s], w_recv.at[n, pair], (2 * to + c, t))
+        to = lax.rem(z + s, zs)
+        return remote(piece(dst, pair), piece(dst, pair), w_send.at[n, s], w_recv.at[n, pair], (d + 4 * (to - z), t))
+
+    def hand_across(n, s):
+        dst = halves[n][1]
+        p = lax.rem(z + s, zs) * 2 + side
+        return remote(piece(dst, p), piece(dst, p), w_send.at[n, zs + s], w_recv.at[n, p], across)
+
+    def wait_piece(n, p):
+        dst = halves[n][1]
+        remote(piece(dst, p), piece(dst, p), w_send.at[n, 0], w_recv.at[n, p], diag).wait_recv()
 
     def near_weight(n):
         src, dst = halves[n]
@@ -626,17 +642,22 @@
 
     def hand_round(n):
         first_piece(n).wait_recv()
-        each(n_pairs - 1, lambda s: hand_piece(n, s + 1).start())
+        each(zs - 1, lambda s: hand_along(n, s + 1).start())
+        hand_across(n, 0).start()
+
+    def hand_on(n):
+        def one(s):
+            wait_piece(n, lax.rem(z + s + 1, zs) * 2 + side)
+            hand_across(n, s + 1).start()
+
+        @pl.when(swaps)
+        def _():
+            each(zs - 1, one)
 
     def wait_weight(n):
         @pl.when(swaps)
         def _():
-            def one(s):
-                dst = halves[n][1]
-                p = lax.rem(pair + s + 1, n_pairs)
-                remote(piece(dst, p), piece(dst, p), w_send.at[n, 0], w_recv.at[n, p], diag).wait_recv()
-
-            each(n_pairs - 1, one)
+            each(zs, lambda s: wait_piece(n, lax.rem(z + s, zs) * 2 + 1 - side))
 
         @pl.when(stays)
         def _():
@@ -646,7 +667,8 @@
 
     @pl.when(stays)
     def _():
-        near_weight(WQKV).start()
+        near_weight(WKV0).start()
+        near_weight(WQ0).start()
 
     start_near(MEM)
     start_near(COT)
@@ -680,7 +702,8 @@
 
     @pl.when(swaps)
     def _():
-        first_piece(WQKV).start()
+        first_piece(WKV0).start()
+        first_piece(WQ0).start()
 
     start_bring(X)
 
@@ -690,19 +713,26 @@
             first_piece(n).start()
 
     start_bring(MEM)
+
+    start_bring(UP)
+    start_bring(DOWN)
     start_bring(COT)
-    for f in range(TILES):
+    for f in range(1, TILES):
         start_bring(UP + f)
         start_bring(DOWN + f)
-
-    @pl.when(swaps)
-    def _():
-        hand_round(WQKV)
 
     @pl.when(stays)
     def _():
         share_starts().start()
 
+    @pl.when(swaps)
+    def _():
+        hand_round(WKV0)
+        hand_round(WQ0)
+
+    hand_on(WKV0)
+    hand_on(WQ0)
+
     def wait_near(n):
         near = bring(n, own)[1]
 
@@ -719,6 +749,12 @@
 
     wait_bring(X)
     share(0, x).start()
+
+    @pl.when(swaps)
+    def _():
+        for n in (WOS, WKV, WQ, WOC):
+            hand_round(n)
+
 
     @pl.when(stays)
     def _():
@@ -736,12 +772,8 @@
         k0[r, :] = dot(nn, wqkv[1]).astype(BF16)
         v0[r, :] = dot(nn, wqkv[2]).astype(BF16)
 
-    @pl.when(swaps)
-    def _():
-        for n in (WOS, WKV, WQ, WOC):
-            hand_round(n)
-
-    wait_weight(WQKV)
+    wait_weight(WKV0)
+    wait_weight(WQ0)
     each(2, lambda i: self_project(c * 2 + i))
     share(0, x).wait_recv()
     each(2, lambda i: self_project((1 - c) * 2 + i))
@@ -751,8 +783,6 @@
     def _():
         share_starts().wait_recv()
 
-    wait_weight(WOS)
-
     def exchange(e, i):
         r = block_rows(i)
         return remote(snd.at[e % 2, r], rcv.at[e % 2, r], x_send.at[e, i], x_recv.at[e, i], sib)
@@ -765,17 +795,19 @@
     everything = range(4)
     first_bias = window_bias(0, 0, 256, 256, starts[0:1, 0:256])
     attend([(h, h, 0, 0, first_bias) for h in everything], q0, k0, vt, kept0, ht0, inv0, 256, 256, 256)
-    out_of(0, 0, ht0, wos)
 
     def self_block(j):
         i = j + 1
-        q_at = pl.multiple_of(i * 256, 256)
-        k_at = pl.multiple_of(j * 256, 256)
-        bias = window_bias(k_at, q_at, 512, 256, starts[0:1, pl.ds(q_at, 256)])
-        attend([(h, j * 4 + h, q_at, k_at, bias) for h in everything], q0, k0, vt, kept1, ht0, inv0, 256, 512, 256)
-        out_of(0, i, ht0, wos)
-
-    each(BLOCKS - 1, self_block)
+        bias = window_bias(j * 256, i * 256, 512, 256, starts[0:1, i * 256:(i + 1) * 256])
+        attend([(h, j * 4 + h, i * 256, j * 256, bias) for h in everything],
+               q0, k0, vt, kept1, ht0, inv0, 256, 512, 256)
+
+    for j, n in enumerate((WOS, WKV, WQ)):
+        hand_on(n)
+        self_block(j)
+    wait_weight(WOS)
+    each(BLOCKS, lambda i: out_of(0, i, ht0, wos))
+    hand_on(WOC)
 
     wait_swapped(MEM)
 
@@ -795,7 +827,6 @@
     each(2, lambda i: memory_project((1 - c) * 2 + i))
     vt[...] = v1[...].T
     wait_weight(WQ)
-    wait_weight(WOC)
 
     def cross_norm(i):
         r = block_rows(i)
@@ -809,6 +840,8 @@
 
     each(BLOCKS, cross_norm)
 
+    wait_weight(WOC)
+
     def cross_pair(j):
         units = []
         for i in range(2):
@@ -839,10 +872,10 @@
         xhat, _ = normalise(state)
         n2[r, :] = (xhat * gains[2:3, :]).astype(BF16)
 
-    each(BLOCKS, expert_norm)
-    nt[...] = n2[...].T
+    each(2, expert_norm)
     share(2, cot).wait_recv()
     cot_t[...] = cot[...].T
+    each(2, lambda i: expert_norm(i + 2))
 
     def begin(copy):
         copy.start()
@@ -855,21 +888,27 @@
 
     def scatter(f, action):
         src, dst = eb.at[f], e_out.at[row, f]
-
-        @pl.when(stays)
-        def _():
-            if action is begin:
-                pltpu.make_async_copy(share_rows(src, d), dst, e_recv.at[f, row]).start()
-
-        @pl.when(swaps)
-        def _():
-            action(remote(share_rows(src, d), dst, e_send.at[f, 0], e_recv.at[f, row], (d, c)))
 
         def one(s):
             to = lax.rem(d + s + 1, n_dp)
             action(remote(share_rows(src, to), dst, e_send.at[f, s + 1], e_recv.at[f, row], (to, c)))
 
         each(n_dp - 1, one)
+
+    def scatter_near(f):
+        @pl.when(stays)
+        def _():
+            pltpu.make_async_copy(share_rows(eb.at[f], d), e_out.at[row, f], e_recv.at[f, row]).start()
+            scatter(f, begin)
+
+    def own_far(f):
+        return remote(share_rows(eb.at[f], d), e_out.at[row, f], e_send.at[f, 0], e_recv.at[f, row], (d, c))
+
+    def scatter_far(f):
+        @pl.when(swaps)
+        def _():
+            own_far(f).start()
+            scatter(f, begin)
 
     def collect(f):
         def one(i):
@@ -906,26 +945,11 @@
             following = first(i + 1) if i + 1 < BLOCKS else None
             second(i, made)
             made = following
-        eb[f, :, 0:TILE] = dot(nt[...], gpre[:, cols]).astype(BF16)
-        eb[f, :, TILE:2 * TILE] = dot(cot_t[...], hid[:, cols]).astype(BF16)
-        scatter(f, begin)
-
-    for f in range(TILES):
-        wait_bring(UP + f)
-        wait_bring(DOWN + f)
-        expert_tile(f)
-
-    def done_sending(e):
-        each(BLOCKS, lambda i: exchange(e, i).wait_send())
-
-    done_sending(0)
 
     def expert_back(i):
         r = block_rows(i)
         snd[0, r, :] = dot(gpre[r, :], up[...], NT).astype(BF16)
         exchange(2, i).start()
-
-    each(BLOCKS, expert_back)
 
     def expert_out(i):
         r = block_rows(i)
@@ -942,6 +966,33 @@
             sndh[0, rl, :] = part.astype(BF16)
             half_exchange(0, lax.rem(i, 2)).start()
 
+    def expert_grads(f):
+        cols = slice(f * TILE, (f + 1) * TILE)
+        eb[f, :, 0:TILE] = dot(nt[...], gpre[:, cols]).astype(BF16)
+        eb[f, :, TILE:2 * TILE] = dot(cot_t[...], hid[:, cols]).astype(BF16)
+
+    def done_sending(e):
+        each(BLOCKS, lambda i: exchange(e, i).wait_send())
+
+    done_sending(0)
+    for f in range(TILES):
+        wait_bring(UP + f)
+        wait_bring(DOWN + f)
+        expert_tile(f)
+        if f == 0:
+            nt[...] = n2[...].T
+        if f + 1 < TILES:
+            expert_grads(f)
+            scatter_near(f)
+        if f + 2 == TILES:
+            scatter_far(0)
+
+    each(BLOCKS, expert_back)
+    scatter_far(1)
+    expert_grads(TILES - 1)
+    scatter_near(TILES - 1)
+    scatter_far(2)
+    scatter_far(3)
     each(BLOCKS, expert_out)
 
     def strip(n):
@@ -958,9 +1009,9 @@
         exchange(e, i).wait_recv()
         grad = snd[e % 2, r, :].astype(F32) + rcv[e % 2, r, :].astype(F32)
         step, share_gain = norm_back(state[r, :], gains[n:n + 1, :], grad)
-        total = base[r, :].astype(F32) + step
-        gs[r, :] = total
-        low = total.astype(BF16)
+        moved = base[r, :].astype(F32) + step
+        gs[r, :] = moved
+        low = moved.astype(BF16)
         gb[r, :] = low
         gain_sum[n:n + 1, :] += jnp.where(lax.div(i, 2) == c, share_gain, 0.0)
         gh[r, :] = dot(low, w_out[...], NT).astype(BF16)
@@ -980,11 +1031,9 @@
         dkt[...] = jnp.zeros_like(dkt)
         dvt[...] = jnp.zeros_like(dvt)
 
-    zs = n_dp // 4
-    side = lax.rem(pair, 2)
-    z = lax.div(d, 4)
-    across = (d + 2 - 4 * side, t)
-    pieces = ((a0, ax0, ay0, a0_out), (a1, ax1, ay1, a1_out), (a2, ax2, ay2, a2_out))
+    pieces = tuple(zip((a0, a1, a2, a3, a4, a5), (ax0, ax1, ax2, ax3, ax4, ax5), (ay0, ay1, ay2, ay3, ay4, ay5),
+                       (a0_out, a1_out, a2_out, a3_out, a4_out, a5_out)))
+    n_pieces = len(pieces)
 
     def over_x(n):
         buf, place = pieces[n][:2]
@@ -1055,15 +1104,6 @@
         return grad.astype(BF16).T.reshape(zs, 2, WIDTH // (2 * zs), grad.shape[0])
 
     each(BLOCKS, lambda i: branch_block(2, i, 2, s2, cot, ht1, inv1, woc))
-    turn_queries(q1, k1, inv1)
-
-    def cross_back(h):
-        units = [(hh, i * 4 + hh, i * 256, 0) for hh in (2 * h, 2 * h + 1) for i in range(BLOCKS)]
-        attend_back(units, v1, kt, qt, gh, ght, kept2, inner, inv1, dqt, dkt, dvt, 256, LEN, 256)
-
-    cross_back(0)
-    cross_back(1)
-
     def leave(n, out):
         buf = leaving.at[n]
         return (lambda: remote(buf, out, o_send.at[n], o_recv.at[n], diag),
@@ -1091,24 +1131,44 @@
         def _():
             near().wait()
 
-    def half_done(n, out):
+    def half_done(n):
         def one(low):
             half_exchange(n, low).wait_recv()
             r = block_rows(low)
             leaving[n, r, :] = (half_out[r, :] + rcvh[n, r, :].astype(F32)).astype(BF16)
 
         each(2, one)
-        start_leave(n, out)
-
-    half_done(0, lo_out)
+
+    half_done(0)
+    start_leave(0, lo_out)
+    a0[...] = by_owner(dot(ht1[...], gb[...]))
+    over_x(0).start()
+    turn_queries(q1, k1, inv1)
+
+    def pair_grads(pair_of_heads, n, source_q, source_kv):
+        rows = slice(pair_of_heads * 128, pair_of_heads * 128 + 128)
+        dkb[rows, :] = (dkt[rows, :] * math.log(2.0)).astype(BF16)
+        dvb[rows, :] = dvt[rows, :].astype(BF16)
+        buf = pieces[n][0]
+        for part, (grad, source) in enumerate(((dqt, source_q), (dkb, source_kv), (dvb, source_kv))):
+            buf[:, :, :, part * 128:part * 128 + 128] = by_owner(dot(grad[rows, :], source[...]))
+        over_x(n).start()
+
+    def cross_back(pair_of_heads):
+        heads = (2 * pair_of_heads, 2 * pair_of_heads + 1)
+        units = [(h, i * 4 + h, i * 256, 0) for h in heads for i in range(BLOCKS)]
+        attend_back(units, v1, kt, qt, gh, ght, kept2, inner, inv1, dqt, dkt, dvt, 256, LEN, 256)
+        pair_grads(pair_of_heads, 1 + pair_of_heads, n1, mem)
+
+    cross_back(0)
+    cross_back(1)
 
     def settle():
-        dkb[...] = (dkt[...] * math.log(2.0)).astype(BF16)
-        dvb[...] = dvt[...].astype(BF16)
         dq[...] = dqt[...].T
         dk[...] = dkb[...].T
         dv[...] = dvb[...].T
 
+    add_x(0)
     settle()
     done_sending(1)
 
@@ -1118,12 +1178,6 @@
         exchange(3, i).start()
 
     each(BLOCKS, cross_grads)
-    a0[:, :, :, 0:256] = by_owner(dot(ht1[...], gb[...]))
-    a0[:, :, :, 256:512] = by_owner(dot(dqt[...], n1[...]))
-    a0[:, :, :, 512:768] = by_owner(dot(dkb[...], mem[...]))
-    a0[:, :, :, 768:1024] = by_owner(dot(dvb[...], mem[...]))
-    over_x(0).start()
-
     def memory_grads(i):
         r = block_rows(i)
         part = dot(dk[r, :], wkv[0], NT) + dot(dv[r, :], wkv[1], NT)
@@ -1140,9 +1194,11 @@
             half_exchange(1, lax.rem(i, 2)).start()
 
     each(BLOCKS, memory_grads)
+    add_x(1)
 
     each(BLOCKS, lambda i: branch_block(1, i, 3, s1, gs, ht0, inv0, wos))
-    half_done(1, gm_out)
+    half_done(1)
+    start_leave(1, gm_out)
     turn_queries(q0, k0, inv0)
 
     def self_back(pair_of_heads):
@@ -1150,22 +1206,14 @@
         attend_back([(h, h, 0, 0) for h in heads], v0, kt, qt, gh, ght, kept0, inner, inv0, dqt, dkt, dvt, 256, 256, 256)
         units = [(h, j * 4 + h, (j + 1) * 256, j * 256) for h in heads for j in range(BLOCKS - 1)]
         attend_back(units, v0, kt, qt, gh, ght, kept1, inner, inv0, dqt, dkt, dvt, 256, 512, 256)
-        rows = slice(pair_of_heads * 128, pair_of_heads * 128 + 128)
-        dkb[rows, :] = (dkt[rows, :] * math.log(2.0)).astype(BF16)
-        dvb[rows, :] = dvt[rows, :].astype(BF16)
-        buf = pieces[1 + pair_of_heads][0]
-        for n, grad in enumerate((dqt, dkb, dvb)):
-            buf[:, :, :, n * 128:n * 128 + 128] = by_owner(dot(grad[rows, :], n0[...]))
-
-    a1[:, :, :, 384:640] = by_owner(dot(ht0[...], gb[...]))
+        pair_grads(pair_of_heads, 4 + pair_of_heads, n0, n0)
+
+    a3[...] = by_owner(dot(ht0[...], gb[...]))
+    over_x(3).start()
     self_back(0)
-    over_x(1).start()
-    add_x(0)
+    add_x(2)
     self_back(1)
-    over_x(2).start()
-    dq[...] = dqt[...].T
-    dk[...] = dkb[...].T
-    dv[...] = dvb[...].T
+    settle()
 
     def input_grads(i):
         r = block_rows(i)
@@ -1176,8 +1224,6 @@
         half_exchange(2, low).start()
 
     each(2, input_send)
-    add_y(0)
-    add_x(1)
 
     def input_keep(low):
         half_out[block_rows(low), :] = input_grads(c * 2 + low)
@@ -1195,8 +1241,8 @@
 
     each(2, input_done)
     start_leave(2, gi_out)
-    add_x(2)
-    add_y(1)
+    add_y(0)
+    add_x(3)
 
     number = jnp.full((1, 128), expert[0, 0].astype(F32))
     for j in range(n_dp):
@@ -1207,13 +1253,19 @@
     def gain_copy(s):
         to = lax.rem(lin + s, n_all)
         to_dp = lax.div(to, 2)
-        return remote(g_send.at[to_dp], g_out.at[lin], g_ssem.at[s], g_rsem.at[lin], (to_dp, lax.rem(to, 2)))
+        return remote(g_send.at[to_dp], g_in.at[lin], g_ssem.at[s], g_rsem.at[lin], (to_dp, lax.rem(to, 2)))
 
     each(n_all - 1, lambda s: gain_copy(s + 1).start())
-    keep_gain = pltpu.make_async_copy(g_send.at[d], g_out.at[lin], g_rsem.at[lin])
+    keep_gain = pltpu.make_async_copy(g_send.at[d], g_in.at[lin], g_rsem.at[lin])
     keep_gain.start()
 
+    add_y(1)
+    add_x(4)
     add_y(2)
+    add_x(5)
+    add_y(3)
+    add_y(4)
+    add_y(5)
 
     wait_leave(0, lo_out)
     wait_leave(1, gm_out)
@@ -1221,24 +1273,33 @@
     for f in range(TILES):
         collect(f)
         scatter(f, finish_send)
-    for n in range(3):
+
+        @pl.when(swaps)
+        def _():
+            own_far(f).wait_send()
+
+    for n in range(n_pieces):
         collect_piece(n)
     keep_gain.wait()
 
     def gain_wait(s):
         gain_copy(s + 1).wait_send()
         who = lax.rem(lin + s + 1, n_all)
-        remote(g_send.at[0], g_out.at[who], g_ssem.at[0], g_rsem.at[who], diag).wait_recv()
+        remote(g_send.at[0], g_in.at[who], g_ssem.at[0], g_rsem.at[who], diag).wait_recv()
 
     each(n_all - 1, gain_wait)
+    g_out[...] = jnp.sum(g_in[...], axis=0)
+    for r in range(n_dp):
+        ids_out[r:r + 1, :] = g_in[2 * r, 3:4, :]
 
     @pl.when(swaps)
     def _():
         for n in range(n_brought):
             bring(n, theirs)[0]().wait_send()
-        for n in range(5):
+        for n in range(6):
             first_piece(n).wait_send()
-            each(n_pairs - 1, lambda s: hand_piece(n, s + 1).wait_send())
+            each(zs - 1, lambda s: hand_along(n, s + 1).wait_send())
+            each(zs, lambda s: hand_across(n, s).wait_send())
 
     for n, buf in enumerate((x, mem, cot)):
         share(n, buf).wait_send()
@@ -1269,28 +1330,28 @@
     turned = bf(COLS, LEN)
     half = jax.ShapeDtypeStruct((HALF, WIDTH), BF16)
     zs = n_dp // 4
-    sizes = (4 * COLS, 5 * COLS // 2, 3 * COLS // 2)
+    sizes = PIECES
     split = [bf(zs, 2, WIDTH // (2 * zs), size) for size in sizes]
-    parts = [bf(zs, WIDTH // (2 * zs), size) for size in sizes]
+    x_parts = [bf(zs, WIDTH // (2 * zs), size) for size in sizes]
     return pl.pallas_call(
         partial(layer_kernel, n_dp),
         out_shape=(half, half, half, jax.ShapeDtypeStruct((n_dp, TILES, 32, 2 * TILE), BF16),
                    *[jax.ShapeDtypeStruct((zs, 32, size), BF16) for size in sizes],
-                   jax.ShapeDtypeStruct((2 * n_dp, 8, 128), F32)),
+                   jax.ShapeDtypeStruct((8, 128), F32), jax.ShapeDtypeStruct((n_dp, 128), F32)),
         in_specs=[IN_SMEM] * 2 + [IN_VMEM] + [ANY_PLACE] * 10,
-        out_specs=(ANY_PLACE,) * 8,
+        out_specs=(ANY_PLACE,) * (4 + len(sizes)) + (IN_VMEM,) * 2,
         scratch_shapes=[
             tokens, tokens, tokens, bf(3, WIDTH, COLS), bf(COLS, WIDTH), bf(WIDTH, COLS), bf(2, WIDTH, COLS),
             bf(COLS, WIDTH), bf(WIDTH, HIDDEN), bf(HIDDEN, WIDTH), pltpu.VMEM((8, LEN), jnp.int32),
             fl(LEN, WIDTH), fl(LEN, WIDTH), fl(LEN, WIDTH), tokens, tokens, tokens,
             heads, heads, heads, heads, heads, heads, turned, turned, turned, fl(8, LEN), fl(8, LEN), fl(8, LEN),
             bf(4, 256, 256), bf(12, 512, 256), bf(16, LEN, 256), tokens, fl(COLS, LEN), fl(COLS, LEN),
-            bf(2 * LEN, HIDDEN), bf(WIDTH, LEN), bf(WIDTH, LEN), bf(TILES, WIDTH, 2 * TILE), *split, *parts, *parts,
+            bf(2 * LEN, HIDDEN), bf(WIDTH, LEN), bf(WIDTH, LEN), bf(TILES, WIDTH, 2 * TILE), *split, *x_parts, *x_parts,
             bf(2, LEN, WIDTH), bf(2, LEN, WIDTH), bf(3, HALF, WIDTH), bf(3, HALF, WIDTH), bf(3, HALF, WIDTH),
-            fl(HALF, WIDTH), fl(8, WIDTH), fl(n_dp, 8, 128),
-            dma(3 + 2 * TILES), dma(3 + 2 * TILES), dma(5, n_dp // 2), dma(5, n_dp // 2), dma(4), dma(4),
+            fl(HALF, WIDTH), fl(8, WIDTH), fl(n_dp, 8, 128), fl(2 * n_dp, 8, 128),
+            dma(3 + 2 * TILES), dma(3 + 2 * TILES), dma(6, n_dp // 2), dma(6, n_dp // 2), dma(4), dma(4),
             dma(4, 4), dma(4, 4), dma(3, 2), dma(3, 2),
-            dma(TILES, n_dp), dma(TILES, n_dp), dma(2, 3), dma(2, 3), dma(3, 2 * zs), dma(3, zs),
+            dma(TILES, n_dp), dma(TILES, n_dp), dma(2, len(sizes)), dma(2, len(sizes)), dma(len(sizes), 2 * zs), dma(len(sizes), zs),
             dma(2 * n_dp), dma(2 * n_dp), dma(3), dma(3),
         ],
         compiler_params=pltpu.CompilerParams(
@@ -1326,18 +1387,18 @@
 
 
 def place_kernel(
-    gains_any, e_any, a0_any, a1_any, a2_any, gi_any, gm_any, lo_any,
+    ids_any, gains_any, e_any, a0_any, a1_any, a2_any, a3_any, a4_any, a5_any, gi_any, gm_any, lo_any,
     lo_out, gi_out, gm_out, gain_out, qkv_out, os_out, q_out, kv_out, oc_out, up_out, down_out,
-    ids, gains_in, e_in, a0_in, a1_in, a2_in, gi_in, gm_in, lo_in, gi_v, gm_v, ups, downs, in_sems, e_sems, up_sems, down_sems, out_sems,
+    ids, ids_in, gains_in, e_in, a0_in, a1_in, a2_in, a3_in, a4_in, a5_in, gi_in, gm_in, lo_in, gi_v, gm_v, ups, downs, in_sems, e_sems, up_sems, down_sems, out_sems,
 ):
     rows = e_in.shape[0]
-    number = pltpu.make_async_copy(gains_any, ids, in_sems.at[0])
+    number = pltpu.make_async_copy(ids_any, ids, in_sems.at[0])
     number.start()
     blocks = [pltpu.make_async_copy(e_any.at[r], e_in.at[r], e_sems.at[r]) for r in range(rows)]
     for copy in blocks:
         copy.start()
     pairs = ((lo_any, lo_in), (gi_any, gi_in), (gm_any, gm_in), (gains_any, gains_in), (a0_any, a0_in),
-             (a1_any, a1_in), (a2_any, a2_in))
+             (a1_any, a1_in), (a2_any, a2_in), (a3_any, a3_in), (a4_any, a4_in), (a5_any, a5_in))
     reads = [pltpu.make_async_copy(src, dst, in_sems.at[1 + n]) for n, (src, dst) in enumerate(pairs)]
     for copy in reads:
         copy.start()
@@ -1353,7 +1414,7 @@
         for f in range(TILES):
             ups[r, :, f * TILE:(f + 1) * TILE] = e_in[r, f, :, 0:TILE].astype(F32)
             downs[r, :, f * TILE:(f + 1) * TILE] = e_in[r, f, :, TILE:2 * TILE].astype(F32)
-        e = ids[2 * r, 3, 0].astype(jnp.int32)
+        e = ids[r, 0].astype(jnp.int32)
         write(ups.at[r], up_out.at[e], up_sems.at[r])
         write(downs.at[r], down_out.at[e], down_sems.at[r])
     reads[0].wait()
@@ -1366,18 +1427,18 @@
     write(gm_v, gm_out, out_sems.at[1])
     for copy in reads[3:]:
         copy.wait()
-    gain_out[...] = jnp.sum(gains_in[...], axis=0)[:3, :32]
-    first = jnp.sum(a0_in[...].astype(F32), axis=0)
-    oc_out[...] = first[:, 0:COLS]
-    q_out[...] = first[:, COLS:2 * COLS]
-    kv_out[0] = first[:, 2 * COLS:3 * COLS]
-    kv_out[1] = first[:, 3 * COLS:4 * COLS]
-    second = jnp.sum(a1_in[...].astype(F32), axis=0)
-    third = jnp.sum(a2_in[...].astype(F32), axis=0)
-    for n in range(3):
-        qkv_out[n, :, 0:128] = second[:, n * 128:n * 128 + 128]
-        qkv_out[n, :, 128:256] = third[:, n * 128:n * 128 + 128]
-    os_out[...] = second[:, 384:640]
+    gain_out[...] = gains_in[0:3, 0:32]
+    oc_out[...] = jnp.sum(a0_in[...].astype(F32), axis=0)
+    os_out[...] = jnp.sum(a3_in[...].astype(F32), axis=0)
+    for pair, (cross, own) in enumerate(((a1_in, a4_in), (a2_in, a5_in))):
+        cols = slice(pair * 128, pair * 128 + 128)
+        cross = jnp.sum(cross[...].astype(F32), axis=0)
+        own = jnp.sum(own[...].astype(F32), axis=0)
+        q_out[:, cols] = cross[:, 0:128]
+        for n in range(2):
+            kv_out[n, :, cols] = cross[:, 128 + n * 128:256 + n * 128]
+        for n in range(3):
+            qkv_out[n, :, cols] = own[:, n * 128:n * 128 + 128]
     for copy in writes:
         copy.wait()
 
@@ -1386,7 +1447,7 @@
     shape = lambda *dims: jax.ShapeDtypeStruct(dims, F32)
     like = lambda array: pltpu.VMEM(array.shape, array.dtype)
     dma = lambda *dims: pltpu.SemaphoreType.DMA(dims)
-    rows = arrays[1].shape[0]
+    rows = arrays[2].shape[0]
     staged = pltpu.VMEM((rows, 32, HIDDEN), F32)
     half = pltpu.VMEM((HALF, WIDTH), F32)
     return pl.pallas_call(
@@ -1394,10 +1455,10 @@
         out_shape=(jax.ShapeDtypeStruct((HALF, WIDTH), BF16), shape(HALF, WIDTH), shape(HALF, WIDTH), shape(3, 32), shape(3, 32, COLS), shape(32, COLS),
                    shape(32, COLS), shape(2, 32, COLS), shape(32, COLS),
                    shape(experts, 32, HIDDEN), shape(experts, 32, HIDDEN)),
-        in_specs=[IN_HBM] * 8,
+        in_specs=[IN_HBM] * 12,
         out_specs=(IN_HBM,) * 3 + (IN_VMEM,) * 6 + (IN_HBM,) * 2,
         scratch_shapes=[pltpu.SMEM(arrays[0].shape, F32)] + [like(array) for array in arrays] + [
-            half, half, staged, staged, dma(8), dma(rows), dma(rows), dma(rows), dma(3)],
+            half, half, staged, staged, dma(11), dma(rows), dma(rows), dma(rows), dma(3)],
         compiler_params=pltpu.CompilerParams(vmem_limit_bytes=VMEM_BYTES),
     )(*arrays)
 
@@ -1408,12 +1469,12 @@
 ):
     n_dp = lax.axis_size("dp")
     up, down = choose_expert(expert_ids, w_up, w_down)
-    layer_output, grad_input, grad_memory, e_rows, a0_rows, a1_rows, a2_rows, gain_rows = paired_layer(
+    layer_output, grad_input, grad_memory, e_rows, *a_rows, gain_rows, numbers = paired_layer(
         n_dp, seg_lengths, expert_ids, ln_gains,
         layer_input[0], memory[0], cotangent[0], w_qkv, w_out_self, w_query_cross, w_kv_cross, w_out_cross, up, down,
     )
     layer_output, grad_input, grad_memory, gain_share, qkv, out_self, query, key_value, out_cross, grad_up, grad_down = place_grads(
-        w_up.shape[0], gain_rows, e_rows, a0_rows, a1_rows, a2_rows, grad_input, grad_memory, layer_output)
+        w_up.shape[0], numbers, gain_rows, e_rows, *a_rows, grad_input, grad_memory, layer_output)
     return (
         layer_output[None], grad_input[None], grad_memory[None], gain_share, qkv, out_self.T, query, key_value,
         out_cross.T, grad_up, jnp.swapaxes(grad_down, 1, 2),

time: 136 us -> 127 us (0.934)
  Pallas kernels: 134 us -> 126 us
    pallas_call x1, Pallas kernels: 124 us -> 117 us  [paired_layer(): pl.pallas_call(partial(layer_kernel, n_dp), out_shape=(half, half, half,...]
where the time goes in v4:
time: 127 us
  Pallas kernels  126 us (99%)
  between operations  1.49 us (1%)
    pallas_call x1, Pallas kernels, paired_layer(): pl.pallas_call(partial(layer_kernel, n_dp), out_shape=(half, half, half,...  117 us
    pallas_call x1, Pallas kernels, place_grads(): pl.pallas_call(place_kernel, out_shape=(jax.ShapeDtypeStruct((HALF, WIDTH...  5.91 us
    pallas_call x1, Pallas kernels, choose_expert(): pl.pallas_call(choose_kernel, out_shape=(jax.ShapeDtypeStruct(w_up.shape[...  2.89 us

profile of v4, /device:TPU:0, one launch (start us, length us, event | category | flops | bytes accessed | tf_op | source)
XLA Modules:
  0.0 127.2 jit_solution(3453043712969610138)
XLA Ops:
  1.3 2.9 %shard_map.212 = (bf16[512,1024]{1,0:T(8,128)(2,1)}, bf16[1024,512]{1,0:T(8,128)(2,1)}) custom-call(s32[1,1]{1,0:T(1,128)S(6)} %copy.24.expert, bf16[16,512,1024]{2,1,0:T(8,128)(2,1)} %up_in.1, bf16[16,1024,512]{2,1,0:T(8,128)(2,1)} %down_in.1), custom_call_target="tpu_custom_call" | custom-call | tf_op jit(solution)/shard_map/pallas_call | solution.py:1379
  4.2 116.9 %shard_map.213 = (bf16[512,512]{1,0:T(8,128)(2,1)}, bf16[512,512]{1,0:T(8,128)(2,1)}, bf16[512,512]{1,0:T(8,128)(2,1)}, bf16[16,4,32,512]{3,2,1,0:T(8,128)(2,1)}...) custom-call(s32[1,16]{1,0:T(1,128)} %lens.1, ...), custom_call_target="tpu_custom_call" | custom-call | flops 20000000000 | bytes 20971520 | tf_op jit(solution)/shard_map/pallas_call | solution.py:1336
  121.1 5.9 %shard_map.214 = (bf16[512,512]{1,0:T(8,128)(2,1)}, f32[512,512]{1,0:T(8,128)}, f32[512,512]{1,0:T(8,128)}, f32[3,32]{1,0:T(4,128)}, f32[3,32,256]{2,1,0:T(8,128...) custom-call(f32[16,128]{1,0:T(8,128)} %get-tuple-element.38.ids_any,, ...), custom_call_target="tpu_custom_call" | custom-call | tf_op jit(solution)/shard_map/pallas_call | solution.py:1453

commit v5 on v4

--- a/solution.py
+++ b/solution.py
@@ -1360,28 +1360,33 @@
     )(lens, expert, gains, *arrays)
 
 
-def choose_kernel(expert, up_in, down_in, up_out, down_out, sems):
+def choose_kernel(expert, up_in, down_in, up_out, down_out, up_v, down_v, in_sems, out_sems):
     e = expert[0, 0]
-    parts = 4
-    copies = []
+    parts = in_sems.shape[1]
+    steps = []
     for p in range(parts):
-        for n, (src, dst) in enumerate(((up_in, up_out), (down_in, down_out))):
-            rows = dst.shape[0] // parts
+        for n, (src, mid, dst) in enumerate(((up_in, up_v, up_out), (down_in, down_v, down_out))):
+            rows = mid.shape[0] // parts
             at = pl.ds(p * rows, rows)
-            copies.append(pltpu.make_async_copy(src.at[e, at], dst.at[at], sems.at[n, p]))
-    for copy in copies:
-        copy.start()
-    for copy in copies:
-        copy.wait()
+            steps.append((pltpu.make_async_copy(src.at[e, at], mid.at[at], in_sems.at[n, p]),
+                          pltpu.make_async_copy(mid.at[at], dst.at[at], out_sems.at[n, p])))
+    for first, _ in steps:
+        first.start()
+    for first, second in steps:
+        first.wait()
+        second.start()
+    for _, second in steps:
+        second.wait()
 
 
 def choose_expert(expert, w_up, w_down):
     return pl.pallas_call(
         choose_kernel,
         out_shape=(jax.ShapeDtypeStruct(w_up.shape[1:], BF16), jax.ShapeDtypeStruct(w_down.shape[1:], BF16)),
-        in_specs=[IN_SMEM, ANY_PLACE, ANY_PLACE],
-        out_specs=(IN_VMEM, IN_VMEM),
-        scratch_shapes=[pltpu.SemaphoreType.DMA((2, 4))],
+        in_specs=[IN_SMEM, IN_HBM, IN_HBM],
+        out_specs=(IN_HBM, IN_HBM),
+        scratch_shapes=[pltpu.VMEM(w_up.shape[1:], BF16), pltpu.VMEM(w_down.shape[1:], BF16),
+                        pltpu.SemaphoreType.DMA((2, 8)), pltpu.SemaphoreType.DMA((2, 8))],
         compiler_params=pltpu.CompilerParams(vmem_limit_bytes=VMEM_BYTES),
     )(expert, w_up, w_down)
 
@@ -1389,26 +1394,50 @@
 def place_kernel(
     ids_any, gains_any, e_any, a0_any, a1_any, a2_any, a3_any, a4_any, a5_any, gi_any, gm_any, lo_any,
     lo_out, gi_out, gm_out, gain_out, qkv_out, os_out, q_out, kv_out, oc_out, up_out, down_out,
-    ids, ids_in, gains_in, e_in, a0_in, a1_in, a2_in, a3_in, a4_in, a5_in, gi_in, gm_in, lo_in, gi_v, gm_v, ups, downs, in_sems, e_sems, up_sems, down_sems, out_sems,
+    ids, ids_in, gains_in, e_in, a0_in, a1_in, a2_in, a3_in, a4_in, a5_in, gi_in, gm_in, lo_in, gi_v, gm_v, gain_v, qkv_v, os_v, q_v, kv_v, oc_v,
+    ups, downs, in_sems, e_sems, up_sems, down_sems, out_sems,
 ):
     rows = e_in.shape[0]
     number = pltpu.make_async_copy(ids_any, ids, in_sems.at[0])
     number.start()
-    blocks = [pltpu.make_async_copy(e_any.at[r], e_in.at[r], e_sems.at[r]) for r in range(rows)]
-    for copy in blocks:
-        copy.start()
-    pairs = ((lo_any, lo_in), (gi_any, gi_in), (gm_any, gm_in), (gains_any, gains_in), (a0_any, a0_in),
+    pairs = ((gi_any, gi_in), (gm_any, gm_in), (lo_any, lo_in), (gains_any, gains_in), (a0_any, a0_in),
              (a1_any, a1_in), (a2_any, a2_in), (a3_any, a3_in), (a4_any, a4_in), (a5_any, a5_in))
     reads = [pltpu.make_async_copy(src, dst, in_sems.at[1 + n]) for n, (src, dst) in enumerate(pairs)]
-    for copy in reads:
+    blocks = [pltpu.make_async_copy(e_any.at[r], e_in.at[r], e_sems.at[r]) for r in range(rows)]
+    for copy in reads + blocks:
         copy.start()
-    number.wait()
     writes = []
 
     def write(src, dst, sem):
         writes.append(pltpu.make_async_copy(src, dst, sem))
         writes[-1].start()
 
+    reads[0].wait()
+    gi_v[...] = gi_in[...].astype(F32)
+    write(gi_v, gi_out, out_sems.at[0])
+    reads[1].wait()
+    gm_v[...] = gm_in[...].astype(F32)
+    write(gm_v, gm_out, out_sems.at[1])
+    reads[2].wait()
+    write(lo_in, lo_out, out_sems.at[2])
+    for copy in reads[3:]:
+        copy.wait()
+    gain_v[...] = gains_in[0:3, 0:32]
+    oc_v[...] = jnp.sum(a0_in[...].astype(F32), axis=0)
+    os_v[...] = jnp.sum(a3_in[...].astype(F32), axis=0)
+    for pair, (cross, own) in enumerate(((a1_in, a4_in), (a2_in, a5_in))):
+        cols = slice(pair * 128, pair * 128 + 128)
+        cross = jnp.sum(cross[...].astype(F32), axis=0)
+        own = jnp.sum(own[...].astype(F32), axis=0)
+        q_v[:, cols] = cross[:, 0:128]
+        for n in range(2):
+            kv_v[n, :, cols] = cross[:, 128 + n * 128:256 + n * 128]
+        for n in range(3):
+            qkv_v[n, :, cols] = own[:, n * 128:n * 128 + 128]
+    small = ((gain_v, gain_out), (qkv_v, qkv_out), (os_v, os_out), (q_v, q_out), (kv_v, kv_out), (oc_v, oc_out))
+    for n, (src, dst) in enumerate(small):
+        write(src, dst, out_sems.at[3 + n])
+    number.wait()
     for r in range(rows):
         blocks[r].wait()
         for f in range(TILES):
@@ -1417,28 +1446,6 @@
         e = ids[r, 0].astype(jnp.int32)
         write(ups.at[r], up_out.at[e], up_sems.at[r])
         write(downs.at[r], down_out.at[e], down_sems.at[r])
-    reads[0].wait()
-    write(lo_in, lo_out, out_sems.at[2])
-    reads[1].wait()
-    gi_v[...] = gi_in[...].astype(F32)
-    write(gi_v, gi_out, out_sems.at[0])
-    reads[2].wait()
-    gm_v[...] = gm_in[...].astype(F32)
-    write(gm_v, gm_out, out_sems.at[1])
-    for copy in reads[3:]:
-        copy.wait()
-    gain_out[...] = gains_in[0:3, 0:32]
-    oc_out[...] = jnp.sum(a0_in[...].astype(F32), axis=0)
-    os_out[...] = jnp.sum(a3_in[...].astype(F32), axis=0)
-    for pair, (cross, own) in enumerate(((a1_in, a4_in), (a2_in, a5_in))):
-        cols = slice(pair * 128, pair * 128 + 128)
-        cross = jnp.sum(cross[...].astype(F32), axis=0)
-        own = jnp.sum(own[...].astype(F32), axis=0)
-        q_out[:, cols] = cross[:, 0:128]
-        for n in range(2):
-            kv_out[n, :, cols] = cross[:, 128 + n * 128:256 + n * 128]
-        for n in range(3):
-            qkv_out[n, :, cols] = own[:, n * 128:n * 128 + 128]
     for copy in writes:
         copy.wait()
 
@@ -1450,15 +1457,16 @@
     rows = arrays[2].shape[0]
     staged = pltpu.VMEM((rows, 32, HIDDEN), F32)
     half = pltpu.VMEM((HALF, WIDTH), F32)
+    small = [pltpu.VMEM(dims, F32) for dims in ((3, 32), (3, 32, COLS), (32, COLS), (32, COLS), (2, 32, COLS), (32, COLS))]
     return pl.pallas_call(
         place_kernel,
         out_shape=(jax.ShapeDtypeStruct((HALF, WIDTH), BF16), shape(HALF, WIDTH), shape(HALF, WIDTH), shape(3, 32), shape(3, 32, COLS), shape(32, COLS),
                    shape(32, COLS), shape(2, 32, COLS), shape(32, COLS),
                    shape(experts, 32, HIDDEN), shape(experts, 32, HIDDEN)),
         in_specs=[IN_HBM] * 12,
-        out_specs=(IN_HBM,) * 3 + (IN_VMEM,) * 6 + (IN_HBM,) * 2,
+        out_specs=(IN_HBM,) * 11,
         scratch_shapes=[pltpu.SMEM(arrays[0].shape, F32)] + [like(array) for array in arrays] + [
-            half, half, staged, staged, dma(11), dma(rows), dma(rows), dma(rows), dma(3)],
+            half, half, *small, staged, staged, dma(11), dma(rows), dma(rows), dma(rows), dma(9)],
         compiler_params=pltpu.CompilerParams(vmem_limit_bytes=VMEM_BYTES),
     )(*arrays)
 

time: 127 us -> 126 us (level)
  Pallas kernels: 126 us -> 124 us
where the time goes in v5:
time: 126 us
  Pallas kernels  124 us (98%)
  between operations  1.49 us (1%)
    pallas_call x1, Pallas kernels, paired_layer(): pl.pallas_call(partial(layer_kernel, n_dp), out_shape=(half, half, half,...  117 us
    pallas_call x1, Pallas kernels, place_grads(): pl.pallas_call(place_kernel, out_shape=(jax.ShapeDtypeStruct((HALF, WIDTH...  4.92 us
    pallas_call x1, Pallas kernels, choose_expert(): pl.pallas_call(choose_kernel, out_shape=(jax.ShapeDtypeStruct(w_up.shape[...  2.57 us

profile of v5, /device:TPU:0, one launch (start us, length us, event | category | flops | bytes accessed | tf_op | source)
XLA Modules:
  0.0 125.9 jit_solution(8561044693379388582)
XLA Ops:
  1.3 2.6 %shard_map.212 = (bf16[512,1024]{1,0:T(8,128)(2,1)}, bf16[1024,512]{1,0:T(8,128)(2,1)}) custom-call(s32[1,1]{1,0:T(1,128)S(6)} %copy.24.expert, bf16[16,512,1024]{2,1,0:T(8,128)(2,1)} %up_in.1, bf16[16,1024,512]{2,1,0:T(8,128)(2,1)} %down_in.1), custom_call_target="tpu_custom_call" | custom-call | tf_op jit(solution)/shard_map/pallas_call | solution.py:1383
  3.9 116.9 %shard_map.213 = (bf16[512,512]{1,0:T(8,128)(2,1)}, bf16[512,512]{1,0:T(8,128)(2,1)}, bf16[512,512]{1,0:T(8,128)(2,1)}, bf16[16,4,32,512]{3,2,1,0:T(8,128)(2,1)}...) custom-call(s32[1,16]{1,0:T(1,128)} %lens.1, ...), custom_call_target="tpu_custom_call" | custom-call | flops 20000000000 | bytes 20971520 | tf_op jit(solution)/shard_map/pallas_call | solution.py:1336
  120.8 4.9 %shard_map.214 = (bf16[512,512]{1,0:T(8,128)(2,1)}, f32[512,512]{1,0:T(8,128)}, f32[512,512]{1,0:T(8,128)}, f32[3,32]{1,0:T(4,128)}, f32[3,32,256]{2,1,0:T(8,128...) custom-call(f32[16,128]{1,0:T(8,128)} %get-tuple-element.38.ids_any,, ...), custom_call_target="tpu_custom_call" | custom-call | tf_op jit(solution)/shard_map/pallas_call | solution.py:1461
